TPU v7x, 128 devices: a whole 4x4x4 slice. The times are simulated.
128 devices in a mesh: group: 4 (over x), col: 32 (over y, z, core).
Axes of the slice: x: 4, y: 4, z: 4, core: 2. Of those that a mesh axis runs over, the one named last changes fastest.
Arguments:
- momentum: bfloat16 [4, 14336, 2048], P(None, ('group', 'col')), may hold values from -6 to 6
- lengths: int32 [4, 128], P(None, ('group', 'col')), may hold values from 1 to 112, 7168 in all within a row
- weight: float32 [4, 14336, 2048], P(None, ('group', 'col')), may hold values from -6 to 6
Outputs:
- update: bfloat16 [4, 14336, 2048], P(None, ('group', 'col'))
- new_weight: float32 [4, 14336, 2048], P(None, ('group', 'col'))
Inputs may be any that keep to these rules, and one draw needn't show every extreme that they name: For every expert the 128 lengths sum to 7168, and some device's shard of each expert holds exactly 112 live rows.
All inputs are finite; a program needn't handle non-finite values.
Results may differ from a plain program's by a relative error of at most 0.005.
Values may be sent and summed in bfloat16 or wider, within the bound.
No kernel may reach another device: no remote copies, remote signals or barrier semaphores. Data moves between devices by JAX's collectives and lax.ppermute only.
A program may use at most 128 MiB of HBM per device.

v0:
```python
import math

import jax
import jax.numpy as jnp
from jax import lax
from jax.sharding import PartitionSpec as P

C = 7168


quintic_first = 3.4445
quintic_second = -4.775
quintic_third = 2.0315
margin_square = 2.25
epsilon_norm = 1e-06
learn_rate = 0.02
decay_rate = 0.1


def on_device(momentum, lengths, weight):
    slot_index = lax.broadcasted_iota(jnp.int32, (momentum.shape[0], momentum.shape[1]), 1)
    live_rows = jnp.where((slot_index < lengths)[:, :, None], momentum, jnp.zeros((), jnp.bfloat16))
    gathered = lax.all_to_all(live_rows, "group", split_axis=0, concat_axis=1, tiled=True)
    expert_rows = gathered[0]
    local_gram = jnp.dot(expert_rows.T, expert_rows, preferred_element_type=jnp.float32)
    gram_total = lax.psum(local_gram.astype(jnp.bfloat16), "col").astype(jnp.float32)
    norm_scale = margin_square / (jnp.sqrt(jnp.sum(gram_total * gram_total)) + epsilon_norm)
    gram_round = gram_total.astype(jnp.bfloat16)
    scaled = (expert_rows.astype(jnp.float32) * jnp.sqrt(norm_scale)).astype(jnp.bfloat16)
    first_term = jnp.dot(scaled, gram_round, preferred_element_type=jnp.float32)
    second_term = jnp.dot(
        first_term.astype(jnp.bfloat16), gram_round, preferred_element_type=jnp.float32
    )
    combined = (
        quintic_first * scaled.astype(jnp.float32)
        + quintic_second * norm_scale * first_term
        + quintic_third * norm_scale * norm_scale * second_term
    )
    results = [(math.sqrt(C) * combined).astype(jnp.bfloat16)]
    stacked = jnp.stack(results)
    returned = lax.all_to_all(stacked, "group", split_axis=1, concat_axis=0, tiled=True)
    new_weight = weight * (1.0 - learn_rate * decay_rate) - learn_rate * returned.astype(
        jnp.float32
    )
    return (returned, new_weight)


def solution(mesh):
    placed = (
        P(None, ("group", "col"), None),
        P(None, ("group", "col")),
        P(None, ("group", "col"), None),
    )
    return jax.shard_map(
        on_device,
        mesh=mesh,
        in_specs=placed,
        out_specs=(P(None, ("group", "col"), None), P(None, ("group", "col"), None)),
        check_vma=False,
    )
```

profile of v0, /device:TPU:0, one launch (start us, length us, event | category | flops | bytes accessed | tf_op | source)
XLA Modules:
  0.0 253.1 jit_solution(3897875810350511134)
XLA Ops:
  7.2 0.0 all-reduce.2.cloned.1.call-start
  7.2 0.7 iota_compare_fusion
  7.9 1.7 broadcast_select_fusion
  9.6 27.7 %all_to_all.21 = bf16[4,112,2048]{2,1,0:T(8,128)(2,1)S(1)} all-to-all(bf16[4,112,2048]{2,1,0:T(8,128)(2,1)S(1)} %broadcast_select_fusion), channel_id=1, replica_groups=mesh['group'=4,'col'=32] {'group'}, dimensions={0} | all-to-all | bytes 3670016 | tf_op jit(solution)/shard_map/all_to_all | solution.py:23
  37.3 6.8 %bitcast_convert_fusion = bf16[2048,2048]{1,0:T(8,128)(2,1)} fusion(bf16[4,112,2048]{2,1,0:T(8,128)(2,1)S(1)} %all_to_all.21), kind=kOutput, calls=%fused_computation | convolution fusion | flops 3762290688 | bytes 10223616 | tf_op jit(solution)/shard_map/dot_general | solution.py:25
  44.1 0.0 all-reduce.2.cloned.1.call-update
  44.1 122.0 %all-reduce.2.cloned.1.call-done = bf16[2048,2048]{1,0:T(8,128)(2,1)} async-done(((bf16[2048,2048]{1,0:T(8,128)(2,1)}), bf16[2048,2048]{1,0:T(8,128)(2,1)}) %all-reduce.2.cloned.1.call-update) | async-done | bytes 8388624 | tf_op jit(solution)/shard_map/psum | solution.py:26
  166.1 8.3 %multiply_reduce_fusion = f32[]{:T(128)} fusion(bf16[2048,2048]{1,0:T(8,128)(2,1)} %all-reduce.2.cloned.1.call-done), kind=kLoop, calls=%fused_computation.1 | loop fusion | flops 12582911 | bytes 8388612 | tf_op jit(solution)/shard_map/reduce_sum | solution.py:27
  175.2 0.0 slice-start
  175.2 0.5 multiply_convert_fusion.1
  175.7 0.0 slice-start.1
  175.7 6.8 %fusion.2 = f32[448,2048]{1,0:T(8,128)S(1)} fusion(bf16[448,2048]{1,0:T(8,128)(2,1)S(1)} %bitcast.22, bf16[2048,2048]{1,0:T(8,128)(2,1)} %all-reduce.2.cloned.1.call-done), kind=kOutput, calls=%fused_computation.10 | convolution fusion | flops 3758096384 | bytes 13893632 | tf_op jit(solution)/shard_map/dot_general | solution.py:30
  182.5 0.0 slice-done
  182.5 0.0 slice-done.1
  182.6 4.4 %fusion = bf16[1,448,2048]{2,1,0:T(8,128)(2,1)S(1)} fusion(bf16[2048,2048]{1,0:T(8,128)(2,1)S(1)} %bitcast.19, f32[448,2048]{1,0:T(8,128)S(1)} %fusion.2, bf16[448,2048]{1,0:T(8,128)(2,1)S(1)} %bitcast.23, f32[]{:T(128)S(6)} %mul.56, f32[]{:T(128)S(6)} %mul_shard_map.6), kind=kOutput, calls=%fused_computation.5 | convolution fusion | flops 3766353920 | bytes 15728648 | tf_op jit(solution)/shard_map/dot_general | solution.py:31
  186.9 4.7 %copy.9 = bf16[1,448,2048]{2,0,1:T(2,128)(2,1)} copy(bf16[1,448,2048]{2,1,0:T(8,128)(2,1)S(1)} %fusion) | data formatting | bytes 3670016 | tf_op jit(solution)/shard_map/stack | solution.py:40
  191.6 0.5 broadcast.14
  192.1 12.9 %reduce = bf16[448,2048]{1,0:T(8,128)(2,1)} reduce(bf16[448,1,2048]{2,1,0:T(2,128)(2,1)} %bitcast.16, bf16[]{:T(256)} %broadcast.14), dimensions={1}, to_apply=%bitcast.15.reduce_sub_computation | reduce | bytes 3670018
  204.9 3.1 %reshape.36 = bf16[4,2,114688]{2,1,0:T(2,128)(2,1)S(1)} reshape(bf16[448,2048]{1,0:T(8,128)(2,1)} %reduce) | data formatting | bytes 3670016
  208.1 27.4 %all_to_all.22 = bf16[4,2,114688]{2,1,0:T(2,128)(2,1)} all-to-all(bf16[4,2,114688]{2,1,0:T(2,128)(2,1)S(1)} %reshape.36), channel_id=1, replica_groups=mesh['group'=4,'col'=32] {'group'}, dimensions={0} | all-to-all | bytes 3670016 | tf_op jit(solution)/shard_map/all_to_all | solution.py:41
  235.5 4.7 %reshape.37 = bf16[448,1,2048]{2,1,0:T(2,128)(2,1)} reshape(bf16[4,2,114688]{2,1,0:T(2,128)(2,1)} %all_to_all.22) | data formatting | bytes 3670016
  240.2 0.0 copy-start.1
  240.2 3.3 %copy.7 = bf16[1,448,2048]{2,1,0:T(8,128)(2,1)S(1)} copy(bf16[1,448,2048]{2,0,1:T(2,128)(2,1)} %bitcast.17) | data formatting | bytes 3670016
  243.5 0.0 copy-start
  243.5 0.0 copy-done.1
  243.5 2.7 %multiply_subtract_fusion = f32[4,112,2048]{2,1,0:T(8,128)} fusion(bf16[4,112,2048]{2,1,0:T(8,128)(2,1)S(1)} %bitcast.20, f32[4,112,2048]{2,1,0:T(8,128)S(1)} %copy-done.1), kind=kLoop, calls=%fused_computation.2 | loop fusion | flops 3670016 | bytes 9175040 | tf_op jit(solution)/shard_map/sub | solution.py:42
  246.2 0.0 copy-done
  (1 shorter events, 0.0 us)
Async XLA Ops:
  7.2 159.0 %all-reduce.2.cloned.1.call-start = ((), (), s32[]{:S(2)}) async-start(), calls=%async_computation.2 | async-start | bytes 16777216 | tf_op jit(solution)/shard_map/psum | solution.py:26
  175.2 7.3 %slice-start = ((s8[8388608]{0:T(1024)(128)(4,1)}), s8[4194304]{0:T(1024)(128)(4,1)S(1)}, s32[]{:S(2)}) async-start(s8[8388608]{0:T(1024)(128)(4,1)} %bitcast.18), calls=%async_computation.3 | async-start | bytes 8388608
  175.7 6.9 %slice-start.1 = ((s8[8388608]{0:T(1024)(128)(4,1)}), s8[4194304]{0:T(1024)(128)(4,1)S(1)}, s32[]{:S(2)}) async-start(s8[8388608]{0:T(1024)(128)(4,1)} %bitcast.18), calls=%async_computation.4 | async-start | bytes 8388608
  240.2 3.3 %copy-start.1 = (f32[4,112,2048]{2,1,0:T(8,128)S(1)}, f32[4,112,2048]{2,1,0:T(8,128)}, u32[]{:S(2)}) copy-start(f32[4,112,2048]{2,1,0:T(8,128)} %param.5) | copy-start | bytes 11010052
  243.5 2.7 %copy-start = (bf16[1,448,2048]{2,1,0:T(8,128)(2,1)}, bf16[1,448,2048]{2,1,0:T(8,128)(2,1)S(1)}, u32[]{:S(2)}) copy-start(bf16[1,448,2048]{2,1,0:T(8,128)(2,1)S(1)} %copy.7) | copy-start | bytes 5505028
Sparse Core Ops, SparseCore 0:
  44.3 121.8 all-reduce.1
where the time goes:
time: 253 us
  waiting for transfers between devices  122 us (48%)
  blocking collectives  55.1 us (22%)
  other arithmetic  26.7 us (11%)
  matrix products  18 us (7%)
  local copies, waits for them, and re-layouts  16.3 us (6%)
  between operations  14.9 us (6%)
    psum x1, waiting for transfers between devices, on_device(): lax.psum(local_gram.astype(jnp.bfloat16), 'col').astype(jnp.float32)  122 us
    all_to_all x1, blocking collectives, on_device(): lax.all_to_all(live_rows, 'group', split_axis=0, concat_axis=1, tiled=True)  27.7 us
    all_to_all x1, blocking collectives, on_device(): lax.all_to_all(stacked, 'group', split_axis=1, concat_axis=0, tiled=True)  27.4 us
    unnamed x2, other arithmetic  12.9 us
    unnamed x12, local copies, waits for them, and re-layouts  11.6 us
    reduce_sum x1, other arithmetic, on_device(): jnp.sum(gram_total * gram_total)  8.3 us
    dot_general x1, matrix products, on_device(): first_term = jnp.dot(scaled, gram_round, preferred_element_type=jnp.float32)  6.83 us
    dot_general x1, matrix products, on_device(): jnp.dot(expert_rows.T, expert_rows, preferred_element_type=jnp.float32)  6.79 us
  transfers between devices with their start and end apart: 1, of which 1 were waited for; matrix products, arithmetic and copies ran while one was open for 0% of the time, Pallas kernels for 0%

commit v1 on v0

v1 whole, which is shorter than its diff:
```python
import functools
import math

import jax
import jax.numpy as jnp
from jax import lax
from jax.experimental import pallas as pl
from jax.experimental.pallas import tpu as pltpu
from jax.sharding import PartitionSpec as P

C = 7168
R = 2048
CAP = 112
AXES = ("group", "col")

quintic_first = 3.4445
quintic_second = -4.775
quintic_third = 2.0315
margin_square = 2.25
epsilon_norm = 1e-06
learn_rate = 0.02
decay_rate = 0.1

BLOCK = 256
SLOTS = 18
HALF = SLOTS * BLOCK
ROUTE = HALF // 2
CHUNK = ROUTE // 4
PIECE = CHUNK // 4
SAME = [(a, b) for a in range(4) for b in range(a, 4)]


def pairs(move):
    def place(x, y, z, c):
        return (x % 4) * 32 + (y % 4) * 8 + (z % 4) * 2 + c

    return [
        (place(x, y, z, c), place(*move(x, y, z, c)))
        for x in range(4) for y in range(4) for z in range(4) for c in range(2)
    ]


def flipped(steps):
    return [(b, a) for a, b in steps]


def to_expert(d):
    def move(x, y, z, c):
        if d == 2:
            return (x + 1, y + 1, z, c) if c == 0 else (x - 1, y - 1, z, c)
        d1 = 1 if d == 1 else -1
        return (x + d1, y, z, c) if c == 0 else (x, y + d1, z, c)

    return pairs(move)


RING_P = {k: pairs(lambda x, y, z, c, k=k: (x + k, y - k, z, c)) for k in (1, 2, 3)}
RING_Q = {k: pairs(lambda x, y, z, c, k=k: (x, y, z + k, c)) for k in (1, 2, 3)}
OTHER_CORE = pairs(lambda x, y, z, c: (x, y, z, 1 - c))


def shift(value, steps):
    return lax.ppermute(value, AXES, steps)


def gram_kernel(place, *refs):
    rows, outs = refs[:8], refs[8:16]
    x_all, x_turned, blocks, in_sems, out_sems = refs[16:]
    core, p, q = place[0], place[1], place[2]
    loads = [
        pltpu.make_async_copy(rows[i], x_all.at[pl.ds(CAP * i, CAP)], in_sems.at[i])
        for i in range(8)
    ]
    for load in loads:
        load.start()
    for load in loads:
        load.wait()

    def columns(at):
        return pl.ds(pl.multiple_of(at * BLOCK, BLOCK), BLOCK)

    for a in range(4):
        x_turned[a * BLOCK:(a + 1) * BLOCK, :] = x_all[:, columns(core * 4 + a)].T
    for slot in range(SLOTS):
        if slot < 10:
            a, b = SAME[slot]
            left = x_turned[a * BLOCK:(a + 1) * BLOCK, :]
            at = core * 4 + b
        else:
            s = slot - 10
            a = jnp.where(core == 0, s // 2, 2 + s // 4)
            left = x_turned[columns(a), :]
            at = jnp.where(core == 0, 4 + s % 2, s % 4)
        blocks[slot * BLOCK:(slot + 1) * BLOCK, :] = jnp.dot(
            left, x_all[:, columns(at)], preferred_element_type=jnp.float32
        ).astype(jnp.bfloat16)
    stores = []
    for route, own in ((0, p), (1, q)):
        for k in range(4):
            start = route * ROUTE + lax.rem(own + k, 4) * CHUNK
            stores.append(pltpu.make_async_copy(
                blocks.at[pl.ds(pl.multiple_of(start, 16), CHUNK)],
                outs[route * 4 + k],
                out_sems.at[route * 4 + k],
            ))
    for store in stores:
        store.start()
    for store in stores:
        store.wait()


def gram(place, rows):
    anywhere = pl.BlockSpec(memory_space=pl.ANY)
    return pl.pallas_call(
        gram_kernel,
        out_shape=[jax.ShapeDtypeStruct((CHUNK, BLOCK), jnp.bfloat16)] * 8,
        in_specs=[pl.BlockSpec(memory_space=pltpu.SMEM)] + [anywhere] * 8,
        out_specs=[anywhere] * 8,
        scratch_shapes=[
            pltpu.VMEM((8 * CAP, R), jnp.bfloat16),
            pltpu.VMEM((4 * BLOCK, 8 * CAP), jnp.bfloat16),
            pltpu.VMEM((HALF, BLOCK), jnp.bfloat16),
            pltpu.SemaphoreType.DMA((8,)),
            pltpu.SemaphoreType.DMA((8,)),
        ],
        compiler_params=pltpu.CompilerParams(vmem_limit_bytes=40 << 20),
        name="gram",
    )(place, *rows)


def stored_at(i, j):
    if i // 4 == j // 4:
        a, b = i % 4, j % 4
        return i // 4, SAME.index((min(a, b), max(a, b))), a > b
    low, high = min(i, j), max(i, j)
    if high < 6:
        return 0, 10 + 2 * low + (high - 4), i > j
    return 1, 10 + 4 * (high - 6) + low, i < j


def update_kernel(place, *refs):
    rows, chunks, outs = refs[:4], refs[4:20], refs[20:24]
    x_all, blocks, first, first_round, in_sems = refs[24:]
    core, p, q = place[0], place[1], place[2]
    loads = [
        pltpu.make_async_copy(rows[i], x_all.at[pl.ds(CAP * i, CAP)], in_sems.at[i])
        for i in range(4)
    ]
    for side in range(2):
        half = core if side == 0 else 1 - core
        for route, own in ((0, p), (1, q)):
            for k in range(4):
                i = side * 8 + route * 4 + k
                start = half * HALF + route * ROUTE + lax.rem(own + 4 - k, 4) * CHUNK
                loads.append(pltpu.make_async_copy(
                    chunks[i],
                    blocks.at[pl.ds(pl.multiple_of(start, 16), CHUNK)],
                    in_sems.at[4 + i],
                ))
    for load in loads:
        load.start()
    for load in loads:
        load.wait()

    def block(half, slot):
        start = half * HALF + slot * BLOCK
        return blocks[start:start + BLOCK, :]

    def times_gram(left, j):
        total = None
        for i in range(8):
            half, slot, turned = stored_at(i, j)
            term = lax.dot_general(
                left[:, i * BLOCK:(i + 1) * BLOCK],
                block(half, slot),
                (((1,), (1 if turned else 0,)), ((), ())),
                preferred_element_type=jnp.float32,
            )
            total = term if total is None else total + term
        return total

    squares = jnp.zeros((BLOCK, BLOCK), jnp.float32)
    for half in range(2):
        for slot in range(SLOTS):
            value = block(half, slot).astype(jnp.float32)
            diagonal = slot < 10 and SAME[slot][0] == SAME[slot][1]
            squares += value * value * (1.0 if diagonal else 2.0)
    total = jnp.sum(squares, axis=(0, 1), keepdims=True)
    norm_scale = margin_square / (jnp.sqrt(total) + epsilon_norm)
    root = jnp.sqrt(norm_scale)

    for j in range(8):
        at = slice(j * BLOCK, (j + 1) * BLOCK)
        value = times_gram(x_all, j)
        first[:, at] = value
        first_round[:, at] = value.astype(jnp.bfloat16)
    for j in range(8):
        at = slice(j * BLOCK, (j + 1) * BLOCK)
        second = times_gram(first_round, j)
        scaled = (x_all[:, at].astype(jnp.float32) * root).astype(jnp.bfloat16)
        combined = (
            quintic_first * scaled.astype(jnp.float32)
            + (quintic_second * norm_scale * root) * first[:, at]
            + (quintic_third * norm_scale * norm_scale * root) * second
        )
        value = (math.sqrt(C) * combined).astype(jnp.bfloat16)
        for d in range(4):
            outs[d][:, at] = value[CAP * d:CAP * (d + 1)]


def update(place, rows, chunks):
    anywhere = pl.BlockSpec(memory_space=pl.ANY)
    return pl.pallas_call(
        update_kernel,
        out_shape=[jax.ShapeDtypeStruct((CAP, R), jnp.bfloat16)] * 4,
        in_specs=[pl.BlockSpec(memory_space=pltpu.SMEM)] + [anywhere] * 20,
        out_specs=[pl.BlockSpec(memory_space=pltpu.VMEM)] * 4,
        scratch_shapes=[
            pltpu.VMEM((4 * CAP, R), jnp.bfloat16),
            pltpu.VMEM((2 * HALF, BLOCK), jnp.bfloat16),
            pltpu.VMEM((4 * CAP, R), jnp.float32),
            pltpu.VMEM((4 * CAP, R), jnp.bfloat16),
            pltpu.SemaphoreType.DMA((20,)),
        ],
        compiler_params=pltpu.CompilerParams(vmem_limit_bytes=48 << 20),
        name="update",
    )(place, *rows, *chunks)


def apply_kernel(home, a0, a1, a2, a3, weight, out, new_weight):
    step = pl.program_id(0)
    for d, ref in enumerate((a0, a1, a2, a3)):
        @pl.when(step == d)
        def _(ref=ref):
            value = ref[...]
            out[0] = value
            new_weight[0] = (
                weight[0] * (1.0 - learn_rate * decay_rate)
                - learn_rate * value.astype(jnp.float32)
            )


def apply(home, returned, weight):
    whole = pl.BlockSpec((CAP, R), lambda d, h: (0, 0))
    one = pl.BlockSpec((1, CAP, R), lambda d, h: (lax.rem(h[0] + d, 4), 0, 0))
    return pl.pallas_call(
        apply_kernel,
        out_shape=[
            jax.ShapeDtypeStruct((4, CAP, R), jnp.bfloat16),
            jax.ShapeDtypeStruct((4, CAP, R), jnp.float32),
        ],
        grid_spec=pltpu.PrefetchScalarGridSpec(
            num_scalar_prefetch=1,
            grid=(4,),
            in_specs=[whole] * 4 + [one],
            out_specs=[one, one],
        ),
        compiler_params=pltpu.CompilerParams(vmem_limit_bytes=32 << 20),
        name="apply",
    )(home, *returned, weight)


def summed(parts, at=None):
    total = None
    for part in parts:
        if at is not None:
            part = lax.dynamic_index_in_dim(part, at, 0, keepdims=False)
        part = part.astype(jnp.float32)
        total = part if total is None else total + part
    return total.astype(jnp.bfloat16)


def on_device(momentum, lengths, weight):
    x, col = lax.axis_index("group"), lax.axis_index("col")
    y, z, core = col // 8, col // 2 % 4, col % 2
    home = (x + y) % 4
    place = jnp.stack([core, x, z]).astype(jnp.int32)
    slot_index = lax.broadcasted_iota(jnp.int32, (CAP, R), 0)

    def live(d):
        e = (home + d) % 4
        rows = lax.dynamic_index_in_dim(momentum, e, 0, keepdims=False)
        limit = lax.dynamic_index_in_dim(lengths, e, 0, keepdims=False)
        return jnp.where(slot_index < limit, rows, jnp.zeros((), jnp.bfloat16))

    routes = {d: to_expert(d) for d in (1, 2, 3)}
    rows = [live(0)] + [shift(live(d), routes[d]) for d in (1, 2, 3)]
    other_rows = [shift(part, OTHER_CORE) for part in rows]

    parts = gram(place, rows + other_rows)
    parts = [part.reshape(4, PIECE, BLOCK) for part in parts]
    ring_of = ((RING_P, RING_Q), (RING_Q, RING_P))
    own_of = ((x, z), (z, x))
    summed_one = []
    for route in range(2):
        mine = parts[route * 4:route * 4 + 4]
        summed_one.append([mine[0]] + [shift(mine[k], ring_of[route][0][k]) for k in (1, 2, 3)])
    pieces = []
    for route in range(2):
        own = own_of[route][1]
        send = [summed(summed_one[route], (own + k) % 4) for k in range(4)]
        arrived = [send[0]] + [shift(send[k], ring_of[route][1][k]) for k in (1, 2, 3)]
        pieces.append(arrived)
    pieces = [summed(arrived) for arrived in pieces]

    chunks = []
    for route in range(2):
        own = own_of[route][1]
        chunk = jnp.zeros((4, PIECE, BLOCK), jnp.bfloat16)
        got = [pieces[route]] + [shift(pieces[route], ring_of[route][1][k]) for k in (1, 2, 3)]
        for k in range(4):
            chunk = lax.dynamic_update_index_in_dim(chunk, got[k], (own + 4 - k) % 4, 0)
        chunks.append(chunk.reshape(CHUNK, BLOCK))
    mine = []
    for route in range(2):
        mine += [chunks[route]]
        mine += [shift(chunks[route], ring_of[route][0][k]) for k in (1, 2, 3)]
    others = [shift(chunk, OTHER_CORE) for chunk in mine]

    updates = update(place, rows, mine + others)
    returned = [updates[0]] + [shift(updates[d], flipped(routes[d])) for d in (1, 2, 3)]
    return tuple(apply(home.reshape(1).astype(jnp.int32), returned, weight))


def solution(mesh):
    placed = (
        P(None, ("group", "col"), None),
        P(None, ("group", "col")),
        P(None, ("group", "col"), None),
    )
    return jax.shard_map(
        on_device,
        mesh=mesh,
        in_specs=placed,
        out_specs=(P(None, ("group", "col"), None), P(None, ("group", "col"), None)),
        check_vma=False,
    )
```

time: 253 us -> 153 us (0.60)
  waiting for transfers between devices: 122 us -> 56 us
  starting transfers between devices: 0.04 us -> 64.6 us
  blocking collectives: 55.1 us -> 0 us
  Pallas kernels: 0 us -> 21.6 us
  other arithmetic: 26.7 us -> 6.53 us
  matrix products: 18 us -> 0 us
  local copies, waits for them, and re-layouts: 16.3 us -> 2.3 us
  between operations: 14.9 us -> 1.01 us
    psum x1 -> x0, waiting for transfers between devices: 122 us -> none  [on_device(): lax.psum(local_gram.astype(jnp.bfloat16), 'col').astype(jnp.float32)]
    ppermute x0 -> x42, starting transfers between devices: none -> 64.6 us  [shift(): return lax.ppermute(value, AXES, steps)]
    ppermute x0 -> x42, waiting for transfers between devices: none -> 56 us  [shift(): return lax.ppermute(value, AXES, steps)]
    all_to_all x2 -> x0, blocking collectives: 55.1 us -> none  [the longest x1 27.7 us: on_device(): lax.all_to_all(live_rows, 'group', split_axis=0, concat_axis=1, tiled=True)]
    pallas_call x0 -> x3, Pallas kernels: none -> 21.6 us  [the longest x1 11.4 us: update(): pl.pallas_call(update_kernel, out_shape=[jax.ShapeDtypeStruct((CAP, R), j...]
    dot_general x3 -> x0, matrix products: 18 us -> none  [the longest x1 6.83 us: on_device(): first_term = jnp.dot(scaled, gram_round, preferred_element_type=jnp.float32)]
    unnamed x2 -> x0, other arithmetic: 12.9 us -> none
    unnamed x12, local copies, waits for them, and re-layouts: 11.6 us -> 0.73 us
  transfers between devices with their start and end apart: 1 -> 42, of which waited for: 1 -> 15; matrix products, arithmetic and copies ran while one was open for 0% -> 2% of each run, Pallas kernels for 0% -> 0%
where the time goes in v1:
time: 153 us; the launch traced here: 152 us
  starting transfers between devices  64.6 us (42%)
  waiting for transfers between devices  56 us (37%)
  Pallas kernels  21.6 us (14%)
  other arithmetic  6.53 us (4%)
  local copies, waits for them, and re-layouts  2.3 us (2%)
    ppermute x42, starting transfers between devices, shift(): return lax.ppermute(value, AXES, steps)  64.6 us
    ppermute x42, waiting for transfers between devices, shift(): return lax.ppermute(value, AXES, steps)  56 us
    pallas_call x1, Pallas kernels, update(): pl.pallas_call(update_kernel, out_shape=[jax.ShapeDtypeStruct((CAP, R), j...  11.4 us
    pallas_call x1, Pallas kernels, gram(): pl.pallas_call(gram_kernel, out_shape=[jax.ShapeDtypeStruct((CHUNK, BLOCK...  7.29 us
  transfers between devices with their start and end apart: 42, of which 15 were waited for; matrix products, arithmetic and copies ran while one was open for 2% of the time, Pallas kernels for 0%

profile of v1, /device:TPU:0, one launch (start us, length us, event | category | flops | bytes accessed | tf_op | source)
XLA Modules:
  0.0 152.0 jit_solution(9334564464108573898)
XLA Ops:
  0.7 1.5 constant_dynamic-slice_fusion
  2.2 1.3 iota_compare_fusion
  3.5 1.3 iota_compare_fusion.2
  4.8 1.6 %bitcast_select_fusion = (bf16[112,2048]{1,0:T(8,128)(2,1)S(1)}, bf16[112,2048]{1,0:T(8,128)(2,1)S(1)}, bf16[112,2048]{1,0:T(8,128)(2,1)S(1)}, bf16[112,2048]{1,0:T(8,128)(2,1)S(1)}) fusion(bf16[4,112,2048]{2,1,0:T(8,128)(2,1)} %param.3, s32[]{:T(128)S(6)} %select_n.198, pred[112]{0:T(512)(128)(4,1)S(1)} %get-tuple-element.44, s32[]{:T(128)S(6)} %select_n.192, ...), kind=kLoop, calls=%fused_computation | loop fusion | flops 917504 | bytes 3670480 | tf_op jit(solution)/shard_map/jit(_where)/select_n | solution.py:284
  6.4 2.9 %collective-permute-start.2 = (bf16[112,2048]{1,0:T(8,128)(2,1)S(1)}, bf16[112,2048]{1,0:T(8,128)(2,1)S(1)}, u32[]{:S(2)}, u32[]{:S(2)}) collective-permute-start(bf16[112,2048]{1,0:T(8,128)(2,1)S(1)} %get-tuple-element.30), channel_id=1, source_target_pairs={{0,96},{1,25},{2,98},{3,27},{4,100},{5,29},{6,102},{7,31},{8,104},... | collective-permute-start | bytes 1376264 | tf_op jit(solution)/shard_map/ppermute | solution.py:63
  9.3 1.8 %collective-permute-start.1 = (bf16[112,2048]{1,0:T(8,128)(2,1)S(1)}, bf16[112,2048]{1,0:T(8,128)(2,1)S(1)}, u32[]{:S(2)}, u32[]{:S(2)}) collective-permute-start(bf16[112,2048]{1,0:T(8,128)(2,1)S(1)} %get-tuple-element.33), channel_id=1, source_target_pairs={{0,40},{1,121},{2,42},{3,123},{4,44},{5,125},{6,46},{7,127},{8,48}... | collective-permute-start | bytes 1376264 | tf_op jit(solution)/shard_map/ppermute | solution.py:63
  11.1 2.9 %collective-permute-start.3 = (bf16[112,2048]{1,0:T(8,128)(2,1)S(1)}, bf16[112,2048]{1,0:T(8,128)(2,1)S(1)}, u32[]{:S(2)}, u32[]{:S(2)}) collective-permute-start(bf16[112,2048]{1,0:T(8,128)(2,1)S(1)} %get-tuple-element.32.refs_0_), channel_id=1, source_target_pairs={{0,1},{1,0},{2,3},{3,2},{4,5},{5,4},{6,7},{7,6},{8,9},{9,8},{10,11... | collective-permute-start | bytes 1376264 | tf_op jit(solution)/shard_map/ppermute | solution.py:63
  14.0 2.2 %collective-permute-done.2.refs_3_ = bf16[112,2048]{1,0:T(8,128)(2,1)S(1)} collective-permute-done((bf16[112,2048]{1,0:T(8,128)(2,1)S(1)}, bf16[112,2048]{1,0:T(8,128)(2,1)S(1)}, u32[]{:S(2)}, u32[]{:S(2)}) %collective-permute-start.2) | collective-permute-done | bytes 458784 | tf_op jit(solution)/shard_map/ppermute | solution.py:63
  16.2 3.3 %collective-permute-start.6 = (bf16[112,2048]{1,0:T(8,128)(2,1)S(1)}, bf16[112,2048]{1,0:T(8,128)(2,1)S(1)}, u32[]{:S(2)}, u32[]{:S(2)}) collective-permute-start(bf16[112,2048]{1,0:T(8,128)(2,1)S(1)} %collective-permute-done.2.refs_3_), channel_id=1, source_target_pairs={{0,1},{1,0},{2,3},{3,2},{4,5},{5,4},{6,7},{7,6},{8,9},{9,8},{10,11... | collective-permute-start | bytes 1376264 | tf_op jit(solution)/shard_map/ppermute | solution.py:63
  19.6 6.8 %collective-permute-done.1.refs_2_ = bf16[112,2048]{1,0:T(8,128)(2,1)S(1)} collective-permute-done((bf16[112,2048]{1,0:T(8,128)(2,1)S(1)}, bf16[112,2048]{1,0:T(8,128)(2,1)S(1)}, u32[]{:S(2)}, u32[]{:S(2)}) %collective-permute-start.1) | collective-permute-done | bytes 458784 | tf_op jit(solution)/shard_map/ppermute | solution.py:63
  26.5 1.9 %collective-permute-done.5.refs_6_ = bf16[112,2048]{1,0:T(8,128)(2,1)} collective-permute-done((bf16[112,2048]{1,0:T(8,128)(2,1)S(1)}, bf16[112,2048]{1,0:T(8,128)(2,1)}, u32[]{:S(2)}, u32[]{:S(2)}) %collective-permute-start.5) | collective-permute-done | bytes 458784 | tf_op jit(solution)/shard_map/ppermute | solution.py:63
  28.3 7.3 %gram.1 = (bf16[576,256]{1,0:T(8,128)(2,1)S(1)}, bf16[576,256]{1,0:T(8,128)(2,1)S(1)}, bf16[576,256]{1,0:T(8,128)(2,1)}, bf16[576,256]{1,0:T(8,128)(2,1)}, bf16[...) custom-call(s32[3]{0:T(128)S(1)} %pad_add_fusion.place, ...), custom_call_target="tpu_custom_call" | custom-call | tf_op jit(solution)/shard_map/gram/pallas_call | solution.py:114
  36.4 2.0 %collective-permute-start.8 = (bf16[4,144,256]{2,1,0:T(8,128)(2,1)}, bf16[4,144,256]{2,1,0:T(8,128)(2,1)S(1)}, u32[]{:S(2)}, u32[]{:S(2)}) collective-permute-start(bf16[4,144,256]{2,1,0:T(8,128)(2,1)} %bitcast.14), channel_id=1, source_target_pairs={{0,80},{1,81},{2,82},{3,83},{4,84},{5,85},{6,86},{7,87},{8,88},{9,... | collective-permute-start | bytes 884744 | tf_op jit(solution)/shard_map/ppermute | solution.py:63
  38.4 2.1 %collective-permute-start.9 = (bf16[4,144,256]{2,1,0:T(8,128)(2,1)}, bf16[4,144,256]{2,1,0:T(8,128)(2,1)S(1)}, u32[]{:S(2)}, u32[]{:S(2)}) collective-permute-start(bf16[4,144,256]{2,1,0:T(8,128)(2,1)} %bitcast.15), channel_id=1, source_target_pairs={{0,104},{1,105},{2,106},{3,107},{4,108},{5,109},{6,110},{7,111},{8... | collective-permute-start | bytes 884744 | tf_op jit(solution)/shard_map/ppermute | solution.py:63
  40.5 1.9 %collective-permute-start.19 = (bf16[4,144,256]{2,1,0:T(8,128)(2,1)}, bf16[4,144,256]{2,1,0:T(8,128)(2,1)S(1)}, u32[]{:S(2)}, u32[]{:S(2)}) collective-permute-start(bf16[4,144,256]{2,1,0:T(8,128)(2,1)} %bitcast.26), channel_id=1, source_target_pairs={{0,2},{1,3},{2,4},{3,5},{4,6},{5,7},{6,0},{7,1},{8,10},{9,11},{10,... | collective-permute-start | bytes 884744 | tf_op jit(solution)/shard_map/ppermute | solution.py:63
  42.5 3.6 %collective-permute-start.20 = (bf16[4,144,256]{2,1,0:T(8,128)(2,1)}, bf16[4,144,256]{2,1,0:T(8,128)(2,1)S(1)}, u32[]{:S(2)}, u32[]{:S(2)}) collective-permute-start(bf16[4,144,256]{2,1,0:T(8,128)(2,1)} %bitcast.27), channel_id=1, source_target_pairs={{0,4},{1,5},{2,6},{3,7},{4,0},{5,1},{6,2},{7,3},{8,12},{9,13},{10,... | collective-permute-start | bytes 884744 | tf_op jit(solution)/shard_map/ppermute | solution.py:63
  46.1 9.1 %collective-permute-done.7 = bf16[4,144,256]{2,1,0:T(8,128)(2,1)S(1)} collective-permute-done((bf16[4,144,256]{2,1,0:T(8,128)(2,1)S(1)}, bf16[4,144,256]{2,1,0:T(8,128)(2,1)S(1)}, u32[]{:S(2)}, u32[]{:S(2)}) %collective-permute-start.7) | collective-permute-done | bytes 294944 | tf_op jit(solution)/shard_map/ppermute | solution.py:63
  55.2 4.0 %collective-permute-start.21 = (bf16[4,144,256]{2,1,0:T(8,128)(2,1)}, bf16[4,144,256]{2,1,0:T(8,128)(2,1)S(1)}, u32[]{:S(2)}, u32[]{:S(2)}) collective-permute-start(bf16[4,144,256]{2,1,0:T(8,128)(2,1)} %bitcast.28), channel_id=1, source_target_pairs={{0,6},{1,7},{2,0},{3,1},{4,2},{5,3},{6,4},{7,5},{8,14},{9,15},{10,... | collective-permute-start | bytes 884744 | tf_op jit(solution)/shard_map/ppermute | solution.py:63
  59.2 1.1 fusion.7
  60.3 1.3 collective-permute-start.10
  61.6 2.2 %collective-permute-start.12 = (bf16[144,256]{1,0:T(8,128)(2,1)S(1)}, bf16[144,256]{1,0:T(8,128)(2,1)S(1)}, u32[]{:S(2)}, u32[]{:S(2)}) collective-permute-start(bf16[144,256]{1,0:T(8,128)(2,1)S(1)} %get-tuple-element.38), channel_id=1, source_target_pairs={{0,6},{1,7},{2,0},{3,1},{4,2},{5,3},{6,4},{7,5},{8,14},{9,15},{10,... | collective-permute-start | bytes 221192 | tf_op jit(solution)/shard_map/ppermute | solution.py:63
  63.8 1.8 %collective-permute-start.11 = (bf16[144,256]{1,0:T(8,128)(2,1)S(1)}, bf16[144,256]{1,0:T(8,128)(2,1)S(1)}, u32[]{:S(2)}, u32[]{:S(2)}) collective-permute-start(bf16[144,256]{1,0:T(8,128)(2,1)S(1)} %get-tuple-element.39), channel_id=1, source_target_pairs={{0,4},{1,5},{2,6},{3,7},{4,0},{5,1},{6,2},{7,3},{8,12},{9,13},{10,... | collective-permute-start | bytes 221192 | tf_op jit(solution)/shard_map/ppermute | solution.py:63
  65.6 1.0 collective-permute-done.21
  66.7 4.1 %collective-permute-start.24 = (bf16[144,256]{1,0:T(8,128)(2,1)S(1)}, bf16[144,256]{1,0:T(8,128)(2,1)S(1)}, u32[]{:S(2)}, u32[]{:S(2)}) collective-permute-start(bf16[144,256]{1,0:T(8,128)(2,1)S(1)} %get-tuple-element.35), channel_id=1, source_target_pairs={{0,104},{1,105},{2,106},{3,107},{4,108},{5,109},{6,110},{7,111},{8... | collective-permute-start | bytes 221192 | tf_op jit(solution)/shard_map/ppermute | solution.py:63
  70.9 3.9 %collective-permute-start.23 = (bf16[144,256]{1,0:T(8,128)(2,1)S(1)}, bf16[144,256]{1,0:T(8,128)(2,1)S(1)}, u32[]{:S(2)}, u32[]{:S(2)}) collective-permute-start(bf16[144,256]{1,0:T(8,128)(2,1)S(1)} %get-tuple-element.36), channel_id=1, source_target_pairs={{0,80},{1,81},{2,82},{3,83},{4,84},{5,85},{6,86},{7,87},{8,88},{9,... | collective-permute-start | bytes 221192 | tf_op jit(solution)/shard_map/ppermute | solution.py:63
  74.8 1.0 bitcast_dynamic-update-slice_fusion.7
  75.8 1.8 %collective-permute-start.14 = (bf16[144,256]{1,0:T(8,128)(2,1)S(1)}, bf16[144,256]{1,0:T(8,128)(2,1)S(1)}, u32[]{:S(2)}, u32[]{:S(2)}) collective-permute-start(bf16[144,256]{1,0:T(8,128)(2,1)S(1)} %get-tuple-element.29), channel_id=1, source_target_pairs={{0,4},{1,5},{2,6},{3,7},{4,0},{5,1},{6,2},{7,3},{8,12},{9,13},{10,... | collective-permute-start | bytes 221192 | tf_op jit(solution)/shard_map/ppermute | solution.py:63
  77.6 3.2 %collective-permute-start.15 = (bf16[144,256]{1,0:T(8,128)(2,1)S(1)}, bf16[144,256]{1,0:T(8,128)(2,1)S(1)}, u32[]{:S(2)}, u32[]{:S(2)}) collective-permute-start(bf16[144,256]{1,0:T(8,128)(2,1)S(1)} %get-tuple-element.29), channel_id=1, source_target_pairs={{0,6},{1,7},{2,0},{3,1},{4,2},{5,3},{6,4},{7,5},{8,14},{9,15},{10,... | collective-permute-start | bytes 221192 | tf_op jit(solution)/shard_map/ppermute | solution.py:63
  80.9 2.3 %collective-permute-start.26 = (bf16[144,256]{1,0:T(8,128)(2,1)S(1)}, bf16[144,256]{1,0:T(8,128)(2,1)S(1)}, u32[]{:S(2)}, u32[]{:S(2)}) collective-permute-start(bf16[144,256]{1,0:T(8,128)(2,1)S(1)} %get-tuple-element.27), channel_id=1, source_target_pairs={{0,80},{1,81},{2,82},{3,83},{4,84},{5,85},{6,86},{7,87},{8,88},{9,... | collective-permute-start | bytes 221192 | tf_op jit(solution)/shard_map/ppermute | solution.py:63
  84.0 3.4 %collective-permute-start.27 = (bf16[144,256]{1,0:T(8,128)(2,1)S(1)}, bf16[144,256]{1,0:T(8,128)(2,1)S(1)}, u32[]{:S(2)}, u32[]{:S(2)}) collective-permute-start(bf16[144,256]{1,0:T(8,128)(2,1)S(1)} %get-tuple-element.27), channel_id=1, source_target_pairs={{0,104},{1,105},{2,106},{3,107},{4,108},{5,109},{6,110},{7,111},{8... | collective-permute-start | bytes 221192 | tf_op jit(solution)/shard_map/ppermute | solution.py:63
  87.6 2.1 %collective-permute-done.25 = bf16[144,256]{1,0:T(8,128)(2,1)S(1)} collective-permute-done((bf16[144,256]{1,0:T(8,128)(2,1)S(1)}, bf16[144,256]{1,0:T(8,128)(2,1)S(1)}, u32[]{:S(2)}, u32[]{:S(2)}) %collective-permute-start.25) | collective-permute-done | bytes 73760 | tf_op jit(solution)/shard_map/ppermute | solution.py:63
  89.7 2.5 %collective-permute-start.17 = (bf16[576,256]{1,0:T(8,128)(2,1)S(1)}, bf16[576,256]{1,0:T(8,128)(2,1)S(1)}, u32[]{:S(2)}, u32[]{:S(2)}) collective-permute-start(bf16[576,256]{1,0:T(8,128)(2,1)S(1)} %bitcast.73), channel_id=1, source_target_pairs={{0,80},{1,81},{2,82},{3,83},{4,84},{5,85},{6,86},{7,87},{8,88},{9,... | collective-permute-start | bytes 884744 | tf_op jit(solution)/shard_map/ppermute | solution.py:63
  92.2 1.3 collective-permute-start.16
  93.6 1.6 %collective-permute-start.30 = (bf16[576,256]{1,0:T(8,128)(2,1)S(1)}, bf16[576,256]{1,0:T(8,128)(2,1)S(1)}, u32[]{:S(2)}, u32[]{:S(2)}) collective-permute-start(bf16[576,256]{1,0:T(8,128)(2,1)S(1)} %bitcast.67), channel_id=1, source_target_pairs={{0,6},{1,7},{2,0},{3,1},{4,2},{5,3},{6,4},{7,5},{8,14},{9,15},{10,... | collective-permute-start | bytes 884744 | tf_op jit(solution)/shard_map/ppermute | solution.py:63
  95.2 9.5 %collective-permute-done.18.refs_7_ = bf16[576,256]{1,0:T(8,128)(2,1)S(1)} collective-permute-done((bf16[576,256]{1,0:T(8,128)(2,1)S(1)}, bf16[576,256]{1,0:T(8,128)(2,1)S(1)}, u32[]{:S(2)}, u32[]{:S(2)}) %collective-permute-start.18) | collective-permute-done | bytes 294944 | tf_op jit(solution)/shard_map/ppermute | solution.py:63
  104.7 1.7 %collective-permute-start.29 = (bf16[576,256]{1,0:T(8,128)(2,1)S(1)}, bf16[576,256]{1,0:T(8,128)(2,1)S(1)}, u32[]{:S(2)}, u32[]{:S(2)}) collective-permute-start(bf16[576,256]{1,0:T(8,128)(2,1)S(1)} %bitcast.68), channel_id=1, source_target_pairs={{0,4},{1,5},{2,6},{3,7},{4,0},{5,1},{6,2},{7,3},{8,12},{9,13},{10,... | collective-permute-start | bytes 884744 | tf_op jit(solution)/shard_map/ppermute | solution.py:63
  106.7 2.6 %collective-permute-done.16.refs_5_ = bf16[576,256]{1,0:T(8,128)(2,1)S(1)} collective-permute-done((bf16[576,256]{1,0:T(8,128)(2,1)S(1)}, bf16[576,256]{1,0:T(8,128)(2,1)S(1)}, u32[]{:S(2)}, u32[]{:S(2)}) %collective-permute-start.16) | collective-permute-done | bytes 294944 | tf_op jit(solution)/shard_map/ppermute | solution.py:63
  109.9 6.3 %collective-permute-done.29.refs_10_ = bf16[576,256]{1,0:T(8,128)(2,1)S(1)} collective-permute-done((bf16[576,256]{1,0:T(8,128)(2,1)S(1)}, bf16[576,256]{1,0:T(8,128)(2,1)S(1)}, u32[]{:S(2)}, u32[]{:S(2)}) %collective-permute-start.29) | collective-permute-done | bytes 294944 | tf_op jit(solution)/shard_map/ppermute | solution.py:63
  116.2 4.0 %collective-permute-done.28.refs_9_ = bf16[576,256]{1,0:T(8,128)(2,1)S(1)} collective-permute-done((bf16[576,256]{1,0:T(8,128)(2,1)S(1)}, bf16[576,256]{1,0:T(8,128)(2,1)S(1)}, u32[]{:S(2)}, u32[]{:S(2)}) %collective-permute-start.28) | collective-permute-done | bytes 294944 | tf_op jit(solution)/shard_map/ppermute | solution.py:63
  120.7 1.1 collective-permute-done.37.refs_18_
  122.2 11.4 %update.1 = (bf16[112,2048]{1,0:T(8,128)(2,1)S(1)}, bf16[112,2048]{1,0:T(8,128)(2,1)S(1)}, bf16[112,2048]{1,0:T(8,128)(2,1)S(1)}, bf16[112,2048]{1,0:T(8,128)(2,1)}) custom-call(s32[3]{0:T(128)S(1)} %pad_add_fusion.place, bf16[112,2048]{1,0:T(8,128)(2,1)} %copy-done, bf16[112,2048]{1,0:T(8,128)(2,1)} %copy-done.3, bf16[112,2048]{1,0:T(8,128)(2,1)} %copy-done.4, ...), custom_call_target="tpu_custom_call" | custom-call | tf_op jit(solution)/shard_map/update/pallas_call | solution.py:213
  133.6 2.5 %collective-permute-start.39 = (bf16[112,2048]{1,0:T(8,128)(2,1)S(1)}, bf16[112,2048]{1,0:T(8,128)(2,1)S(1)}, u32[]{:S(2)}, u32[]{:S(2)}) collective-permute-start(bf16[112,2048]{1,0:T(8,128)(2,1)S(1)} %get-tuple-element.23), channel_id=1, source_target_pairs={{32,0},{9,1},{34,2},{11,3},{36,4},{13,5},{38,6},{15,7},{40,8},{17,... | collective-permute-start | bytes 1376264 | tf_op jit(solution)/shard_map/ppermute | solution.py:63
  136.0 2.0 %collective-permute-start.40 = (bf16[112,2048]{1,0:T(8,128)(2,1)S(1)}, bf16[112,2048]{1,0:T(8,128)(2,1)S(1)}, u32[]{:S(2)}, u32[]{:S(2)}) collective-permute-start(bf16[112,2048]{1,0:T(8,128)(2,1)S(1)} %get-tuple-element.24), channel_id=1, source_target_pairs={{40,0},{121,1},{42,2},{123,3},{44,4},{125,5},{46,6},{127,7},{48,8}... | collective-permute-start | bytes 1376264 | tf_op jit(solution)/shard_map/ppermute | solution.py:63
  138.0 1.9 %collective-permute-start.41 = (bf16[112,2048]{1,0:T(8,128)(2,1)}, bf16[112,2048]{1,0:T(8,128)(2,1)S(1)}, u32[]{:S(2)}, u32[]{:S(2)}) collective-permute-start(bf16[112,2048]{1,0:T(8,128)(2,1)} %get-tuple-element.25), channel_id=1, source_target_pairs={{96,0},{25,1},{98,2},{27,3},{100,4},{29,5},{102,6},{31,7},{104,8},... | collective-permute-start | bytes 1376264 | tf_op jit(solution)/shard_map/ppermute | solution.py:63
  140.0 2.2 %collective-permute-done.39.a1 = bf16[112,2048]{1,0:T(8,128)(2,1)S(1)} collective-permute-done((bf16[112,2048]{1,0:T(8,128)(2,1)S(1)}, bf16[112,2048]{1,0:T(8,128)(2,1)S(1)}, u32[]{:S(2)}, u32[]{:S(2)}) %collective-permute-start.39) | collective-permute-done | bytes 458784 | tf_op jit(solution)/shard_map/ppermute | solution.py:63
  142.1 4.8 %collective-permute-done.40.a2 = bf16[112,2048]{1,0:T(8,128)(2,1)S(1)} collective-permute-done((bf16[112,2048]{1,0:T(8,128)(2,1)S(1)}, bf16[112,2048]{1,0:T(8,128)(2,1)S(1)}, u32[]{:S(2)}, u32[]{:S(2)}) %collective-permute-start.40) | collective-permute-done | bytes 458784 | tf_op jit(solution)/shard_map/ppermute | solution.py:63
  147.0 2.1 %collective-permute-done.41.a3 = bf16[112,2048]{1,0:T(8,128)(2,1)S(1)} collective-permute-done((bf16[112,2048]{1,0:T(8,128)(2,1)}, bf16[112,2048]{1,0:T(8,128)(2,1)S(1)}, u32[]{:S(2)}, u32[]{:S(2)}) %collective-permute-start.41) | collective-permute-done | bytes 458784 | tf_op jit(solution)/shard_map/ppermute | solution.py:63
  149.1 3.0 %apply.1 = (bf16[4,112,2048]{2,1,0:T(8,128)(2,1)}, f32[4,112,2048]{2,1,0:T(8,128)}) custom-call(s32[1]{0:T(128)} %bitcast.home, bf16[112,2048]{1,0:T(8,128)(2,1)S(1)} %get-tuple-element.22.a0, bf16[112,2048]{1,0:T(8,128)(2,1)S(1)} %collective-permute-done.39.a1, bf16[112,2048]{1,0:T(8,128)(2,1)S(1)} %collective-permute-done.40.a2, ...), custom_call_target="tpu_custom_call" | custom-call | tf_op jit(solution)/shard_map/apply/pallas_call | solution.py:246
  (68 shorter events, 4.2 us)
Async XLA Ops:
  6.4 29.2 %copy-start = (bf16[112,2048]{1,0:T(8,128)(2,1)}, bf16[112,2048]{1,0:T(8,128)(2,1)S(1)}, u32[]{:S(2)}) copy-start(bf16[112,2048]{1,0:T(8,128)(2,1)S(1)} %get-tuple-element.32.refs_0_) | copy-start | bytes 1376260
  6.4 9.8 %collective-permute-start.2 = (bf16[112,2048]{1,0:T(8,128)(2,1)S(1)}, bf16[112,2048]{1,0:T(8,128)(2,1)S(1)}, u32[]{:S(2)}, u32[]{:S(2)}) collective-permute-start(bf16[112,2048]{1,0:T(8,128)(2,1)S(1)} %get-tuple-element.30), channel_id=1, source_target_pairs={{0,96},{1,25},{2,98},{3,27},{4,100},{5,29},{6,102},{7,31},{8,104},... | collective-permute-start | bytes 1376264 | tf_op jit(solution)/shard_map/ppermute | solution.py:63
  9.3 10.2 %collective-permute-start = (bf16[112,2048]{1,0:T(8,128)(2,1)S(1)}, bf16[112,2048]{1,0:T(8,128)(2,1)S(1)}, u32[]{:S(2)}, u32[]{:S(2)}) collective-permute-start(bf16[112,2048]{1,0:T(8,128)(2,1)S(1)} %get-tuple-element.31), channel_id=1, source_target_pairs={{0,32},{1,9},{2,34},{3,11},{4,36},{5,13},{6,38},{7,15},{8,40},{9,1... | collective-permute-start | bytes 1376264 | tf_op jit(solution)/shard_map/ppermute | solution.py:63
  9.3 17.1 %collective-permute-start.1 = (bf16[112,2048]{1,0:T(8,128)(2,1)S(1)}, bf16[112,2048]{1,0:T(8,128)(2,1)S(1)}, u32[]{:S(2)}, u32[]{:S(2)}) collective-permute-start(bf16[112,2048]{1,0:T(8,128)(2,1)S(1)} %get-tuple-element.33), channel_id=1, source_target_pairs={{0,40},{1,121},{2,42},{3,123},{4,44},{5,125},{6,46},{7,127},{8,48}... | collective-permute-start | bytes 1376264 | tf_op jit(solution)/shard_map/ppermute | solution.py:63
  11.1 15.4 %collective-permute-start.3 = (bf16[112,2048]{1,0:T(8,128)(2,1)S(1)}, bf16[112,2048]{1,0:T(8,128)(2,1)S(1)}, u32[]{:S(2)}, u32[]{:S(2)}) collective-permute-start(bf16[112,2048]{1,0:T(8,128)(2,1)S(1)} %get-tuple-element.32.refs_0_), channel_id=1, source_target_pairs={{0,1},{1,0},{2,3},{3,2},{4,5},{5,4},{6,7},{7,6},{8,9},{9,8},{10,11... | collective-permute-start | bytes 1376264 | tf_op jit(solution)/shard_map/ppermute | solution.py:63
  16.2 19.5 %copy-start.2 = (bf16[112,2048]{1,0:T(8,128)(2,1)}, bf16[112,2048]{1,0:T(8,128)(2,1)S(1)}, u32[]{:S(2)}) copy-start(bf16[112,2048]{1,0:T(8,128)(2,1)S(1)} %collective-permute-done.2.refs_3_) | copy-start | bytes 1376260
  16.2 10.3 %collective-permute-start.6 = (bf16[112,2048]{1,0:T(8,128)(2,1)S(1)}, bf16[112,2048]{1,0:T(8,128)(2,1)S(1)}, u32[]{:S(2)}, u32[]{:S(2)}) collective-permute-start(bf16[112,2048]{1,0:T(8,128)(2,1)S(1)} %collective-permute-done.2.refs_3_), channel_id=1, source_target_pairs={{0,1},{1,0},{2,3},{3,2},{4,5},{5,4},{6,7},{7,6},{8,9},{9,8},{10,11... | collective-permute-start | bytes 1376264 | tf_op jit(solution)/shard_map/ppermute | solution.py:63
  19.5 16.2 %copy-start.3 = (bf16[112,2048]{1,0:T(8,128)(2,1)}, bf16[112,2048]{1,0:T(8,128)(2,1)S(1)}, u32[]{:S(2)}) copy-start(bf16[112,2048]{1,0:T(8,128)(2,1)S(1)} %collective-permute-done.refs_1_) | copy-start | bytes 1376260
  19.5 7.0 %collective-permute-start.4 = (bf16[112,2048]{1,0:T(8,128)(2,1)S(1)}, bf16[112,2048]{1,0:T(8,128)(2,1)S(1)}, u32[]{:S(2)}, u32[]{:S(2)}) collective-permute-start(bf16[112,2048]{1,0:T(8,128)(2,1)S(1)} %collective-permute-done.refs_1_), channel_id=1, source_target_pairs={{0,1},{1,0},{2,3},{3,2},{4,5},{5,4},{6,7},{7,6},{8,9},{9,8},{10,11... | collective-permute-start | bytes 1376264 | tf_op jit(solution)/shard_map/ppermute | solution.py:63
  26.4 9.3 %copy-start.4 = (bf16[112,2048]{1,0:T(8,128)(2,1)}, bf16[112,2048]{1,0:T(8,128)(2,1)S(1)}, u32[]{:S(2)}) copy-start(bf16[112,2048]{1,0:T(8,128)(2,1)S(1)} %collective-permute-done.1.refs_2_) | copy-start | bytes 1376260
  26.4 1.9 %collective-permute-start.5 = (bf16[112,2048]{1,0:T(8,128)(2,1)S(1)}, bf16[112,2048]{1,0:T(8,128)(2,1)}, u32[]{:S(2)}, u32[]{:S(2)}) collective-permute-start(bf16[112,2048]{1,0:T(8,128)(2,1)S(1)} %collective-permute-done.1.refs_2_), channel_id=1, source_target_pairs={{0,1},{1,0},{2,3},{3,2},{4,5},{5,4},{6,7},{7,6},{8,9},{9,8},{10,11... | collective-permute-start | bytes 1376264 | tf_op jit(solution)/shard_map/ppermute | solution.py:63
  35.7 0.7 copy-start.5
  36.4 18.8 %collective-permute-start.7 = (bf16[4,144,256]{2,1,0:T(8,128)(2,1)S(1)}, bf16[4,144,256]{2,1,0:T(8,128)(2,1)S(1)}, u32[]{:S(2)}, u32[]{:S(2)}) collective-permute-start(bf16[4,144,256]{2,1,0:T(8,128)(2,1)S(1)} %bitcast.80), channel_id=1, source_target_pairs={{0,56},{1,57},{2,58},{3,59},{4,60},{5,61},{6,62},{7,63},{8,32},{9,... | collective-permute-start | bytes 884744 | tf_op jit(solution)/shard_map/ppermute | solution.py:63
  36.4 22.8 %collective-permute-start.8 = (bf16[4,144,256]{2,1,0:T(8,128)(2,1)}, bf16[4,144,256]{2,1,0:T(8,128)(2,1)S(1)}, u32[]{:S(2)}, u32[]{:S(2)}) collective-permute-start(bf16[4,144,256]{2,1,0:T(8,128)(2,1)} %bitcast.14), channel_id=1, source_target_pairs={{0,80},{1,81},{2,82},{3,83},{4,84},{5,85},{6,86},{7,87},{8,88},{9,... | collective-permute-start | bytes 884744 | tf_op jit(solution)/shard_map/ppermute | solution.py:63
  38.4 20.8 %collective-permute-start.9 = (bf16[4,144,256]{2,1,0:T(8,128)(2,1)}, bf16[4,144,256]{2,1,0:T(8,128)(2,1)S(1)}, u32[]{:S(2)}, u32[]{:S(2)}) collective-permute-start(bf16[4,144,256]{2,1,0:T(8,128)(2,1)} %bitcast.15), channel_id=1, source_target_pairs={{0,104},{1,105},{2,106},{3,107},{4,108},{5,109},{6,110},{7,111},{8... | collective-permute-start | bytes 884744 | tf_op jit(solution)/shard_map/ppermute | solution.py:63
  40.5 23.2 %collective-permute-start.19 = (bf16[4,144,256]{2,1,0:T(8,128)(2,1)}, bf16[4,144,256]{2,1,0:T(8,128)(2,1)S(1)}, u32[]{:S(2)}, u32[]{:S(2)}) collective-permute-start(bf16[4,144,256]{2,1,0:T(8,128)(2,1)} %bitcast.26), channel_id=1, source_target_pairs={{0,2},{1,3},{2,4},{3,5},{4,6},{5,7},{6,0},{7,1},{8,10},{9,11},{10,... | collective-permute-start | bytes 884744 | tf_op jit(solution)/shard_map/ppermute | solution.py:63
  42.5 23.1 %collective-permute-start.20 = (bf16[4,144,256]{2,1,0:T(8,128)(2,1)}, bf16[4,144,256]{2,1,0:T(8,128)(2,1)S(1)}, u32[]{:S(2)}, u32[]{:S(2)}) collective-permute-start(bf16[4,144,256]{2,1,0:T(8,128)(2,1)} %bitcast.27), channel_id=1, source_target_pairs={{0,4},{1,5},{2,6},{3,7},{4,0},{5,1},{6,2},{7,3},{8,12},{9,13},{10,... | collective-permute-start | bytes 884744 | tf_op jit(solution)/shard_map/ppermute | solution.py:63
  55.2 11.4 %collective-permute-start.21 = (bf16[4,144,256]{2,1,0:T(8,128)(2,1)}, bf16[4,144,256]{2,1,0:T(8,128)(2,1)S(1)}, u32[]{:S(2)}, u32[]{:S(2)}) collective-permute-start(bf16[4,144,256]{2,1,0:T(8,128)(2,1)} %bitcast.28), channel_id=1, source_target_pairs={{0,6},{1,7},{2,0},{3,1},{4,2},{5,3},{6,4},{7,5},{8,14},{9,15},{10,... | collective-permute-start | bytes 884744 | tf_op jit(solution)/shard_map/ppermute | solution.py:63
  60.3 10.6 %collective-permute-start.10 = (bf16[144,256]{1,0:T(8,128)(2,1)S(1)}, bf16[144,256]{1,0:T(8,128)(2,1)S(1)}, u32[]{:S(2)}, u32[]{:S(2)}) collective-permute-start(bf16[144,256]{1,0:T(8,128)(2,1)S(1)} %get-tuple-element.37), channel_id=1, source_target_pairs={{0,2},{1,3},{2,4},{3,5},{4,6},{5,7},{6,0},{7,1},{8,10},{9,11},{10,... | collective-permute-start | bytes 221192 | tf_op jit(solution)/shard_map/ppermute | solution.py:63
  61.6 13.2 %collective-permute-start.12 = (bf16[144,256]{1,0:T(8,128)(2,1)S(1)}, bf16[144,256]{1,0:T(8,128)(2,1)S(1)}, u32[]{:S(2)}, u32[]{:S(2)}) collective-permute-start(bf16[144,256]{1,0:T(8,128)(2,1)S(1)} %get-tuple-element.38), channel_id=1, source_target_pairs={{0,6},{1,7},{2,0},{3,1},{4,2},{5,3},{6,4},{7,5},{8,14},{9,15},{10,... | collective-permute-start | bytes 221192 | tf_op jit(solution)/shard_map/ppermute | solution.py:63
  63.8 11.0 %collective-permute-start.11 = (bf16[144,256]{1,0:T(8,128)(2,1)S(1)}, bf16[144,256]{1,0:T(8,128)(2,1)S(1)}, u32[]{:S(2)}, u32[]{:S(2)}) collective-permute-start(bf16[144,256]{1,0:T(8,128)(2,1)S(1)} %get-tuple-element.39), channel_id=1, source_target_pairs={{0,4},{1,5},{2,6},{3,7},{4,0},{5,1},{6,2},{7,3},{8,12},{9,13},{10,... | collective-permute-start | bytes 221192 | tf_op jit(solution)/shard_map/ppermute | solution.py:63
  66.7 10.9 %collective-permute-start.22 = (bf16[144,256]{1,0:T(8,128)(2,1)S(1)}, bf16[144,256]{1,0:T(8,128)(2,1)S(1)}, u32[]{:S(2)}, u32[]{:S(2)}) collective-permute-start(bf16[144,256]{1,0:T(8,128)(2,1)S(1)} %get-tuple-element.34), channel_id=1, source_target_pairs={{0,56},{1,57},{2,58},{3,59},{4,60},{5,61},{6,62},{7,63},{8,32},{9,... | collective-permute-start | bytes 221192 | tf_op jit(solution)/shard_map/ppermute | solution.py:63
  66.7 14.1 %collective-permute-start.24 = (bf16[144,256]{1,0:T(8,128)(2,1)S(1)}, bf16[144,256]{1,0:T(8,128)(2,1)S(1)}, u32[]{:S(2)}, u32[]{:S(2)}) collective-permute-start(bf16[144,256]{1,0:T(8,128)(2,1)S(1)} %get-tuple-element.35), channel_id=1, source_target_pairs={{0,104},{1,105},{2,106},{3,107},{4,108},{5,109},{6,110},{7,111},{8... | collective-permute-start | bytes 221192 | tf_op jit(solution)/shard_map/ppermute | solution.py:63
  70.9 9.9 %collective-permute-start.23 = (bf16[144,256]{1,0:T(8,128)(2,1)S(1)}, bf16[144,256]{1,0:T(8,128)(2,1)S(1)}, u32[]{:S(2)}, u32[]{:S(2)}) collective-permute-start(bf16[144,256]{1,0:T(8,128)(2,1)S(1)} %get-tuple-element.36), channel_id=1, source_target_pairs={{0,80},{1,81},{2,82},{3,83},{4,84},{5,85},{6,86},{7,87},{8,88},{9,... | collective-permute-start | bytes 221192 | tf_op jit(solution)/shard_map/ppermute | solution.py:63
  75.8 11.6 %collective-permute-start.14 = (bf16[144,256]{1,0:T(8,128)(2,1)S(1)}, bf16[144,256]{1,0:T(8,128)(2,1)S(1)}, u32[]{:S(2)}, u32[]{:S(2)}) collective-permute-start(bf16[144,256]{1,0:T(8,128)(2,1)S(1)} %get-tuple-element.29), channel_id=1, source_target_pairs={{0,4},{1,5},{2,6},{3,7},{4,0},{5,1},{6,2},{7,3},{8,12},{9,13},{10,... | collective-permute-start | bytes 221192 | tf_op jit(solution)/shard_map/ppermute | solution.py:63
  77.6 6.4 %collective-permute-start.13 = (bf16[144,256]{1,0:T(8,128)(2,1)S(1)}, bf16[144,256]{1,0:T(8,128)(2,1)S(1)}, u32[]{:S(2)}, u32[]{:S(2)}) collective-permute-start(bf16[144,256]{1,0:T(8,128)(2,1)S(1)} %get-tuple-element.29), channel_id=1, source_target_pairs={{0,2},{1,3},{2,4},{3,5},{4,6},{5,7},{6,0},{7,1},{8,10},{9,11},{10,... | collective-permute-start | bytes 221192 | tf_op jit(solution)/shard_map/ppermute | solution.py:63
  77.6 9.8 %collective-permute-start.15 = (bf16[144,256]{1,0:T(8,128)(2,1)S(1)}, bf16[144,256]{1,0:T(8,128)(2,1)S(1)}, u32[]{:S(2)}, u32[]{:S(2)}) collective-permute-start(bf16[144,256]{1,0:T(8,128)(2,1)S(1)} %get-tuple-element.29), channel_id=1, source_target_pairs={{0,6},{1,7},{2,0},{3,1},{4,2},{5,3},{6,4},{7,5},{8,14},{9,15},{10,... | collective-permute-start | bytes 221192 | tf_op jit(solution)/shard_map/ppermute | solution.py:63
  80.9 11.3 %collective-permute-start.26 = (bf16[144,256]{1,0:T(8,128)(2,1)S(1)}, bf16[144,256]{1,0:T(8,128)(2,1)S(1)}, u32[]{:S(2)}, u32[]{:S(2)}) collective-permute-start(bf16[144,256]{1,0:T(8,128)(2,1)S(1)} %get-tuple-element.27), channel_id=1, source_target_pairs={{0,80},{1,81},{2,82},{3,83},{4,84},{5,85},{6,86},{7,87},{8,88},{9,... | collective-permute-start | bytes 221192 | tf_op jit(solution)/shard_map/ppermute | solution.py:63
  83.2 6.5 %collective-permute-start.25 = (bf16[144,256]{1,0:T(8,128)(2,1)S(1)}, bf16[144,256]{1,0:T(8,128)(2,1)S(1)}, u32[]{:S(2)}, u32[]{:S(2)}) collective-permute-start(bf16[144,256]{1,0:T(8,128)(2,1)S(1)} %get-tuple-element.27), channel_id=1, source_target_pairs={{0,56},{1,57},{2,58},{3,59},{4,60},{5,61},{6,62},{7,63},{8,32},{9,... | collective-permute-start | bytes 221192 | tf_op jit(solution)/shard_map/ppermute | solution.py:63
  84.0 9.5 %collective-permute-start.27 = (bf16[144,256]{1,0:T(8,128)(2,1)S(1)}, bf16[144,256]{1,0:T(8,128)(2,1)S(1)}, u32[]{:S(2)}, u32[]{:S(2)}) collective-permute-start(bf16[144,256]{1,0:T(8,128)(2,1)S(1)} %get-tuple-element.27), channel_id=1, source_target_pairs={{0,104},{1,105},{2,106},{3,107},{4,108},{5,109},{6,110},{7,111},{8... | collective-permute-start | bytes 221192 | tf_op jit(solution)/shard_map/ppermute | solution.py:63
  87.4 6.2 %collective-permute-start.31 = (bf16[576,256]{1,0:T(8,128)(2,1)S(1)}, bf16[576,256]{1,0:T(8,128)(2,1)S(1)}, u32[]{:S(2)}, u32[]{:S(2)}) collective-permute-start(bf16[576,256]{1,0:T(8,128)(2,1)S(1)} %bitcast.71), channel_id=1, source_target_pairs={{0,1},{1,0},{2,3},{3,2},{4,5},{5,4},{6,7},{7,6},{8,9},{9,8},{10,11... | collective-permute-start | bytes 884744 | tf_op jit(solution)/shard_map/ppermute | solution.py:63
  87.5 17.2 %collective-permute-start.18 = (bf16[576,256]{1,0:T(8,128)(2,1)S(1)}, bf16[576,256]{1,0:T(8,128)(2,1)S(1)}, u32[]{:S(2)}, u32[]{:S(2)}) collective-permute-start(bf16[576,256]{1,0:T(8,128)(2,1)S(1)} %bitcast.72), channel_id=1, source_target_pairs={{0,104},{1,105},{2,106},{3,107},{4,108},{5,109},{6,110},{7,111},{8... | collective-permute-start | bytes 884744 | tf_op jit(solution)/shard_map/ppermute | solution.py:63
  89.7 16.8 %collective-permute-start.17 = (bf16[576,256]{1,0:T(8,128)(2,1)S(1)}, bf16[576,256]{1,0:T(8,128)(2,1)S(1)}, u32[]{:S(2)}, u32[]{:S(2)}) collective-permute-start(bf16[576,256]{1,0:T(8,128)(2,1)S(1)} %bitcast.73), channel_id=1, source_target_pairs={{0,80},{1,81},{2,82},{3,83},{4,84},{5,85},{6,86},{7,87},{8,88},{9,... | collective-permute-start | bytes 884744 | tf_op jit(solution)/shard_map/ppermute | solution.py:63
  92.2 17.1 %collective-permute-start.16 = (bf16[576,256]{1,0:T(8,128)(2,1)S(1)}, bf16[576,256]{1,0:T(8,128)(2,1)S(1)}, u32[]{:S(2)}, u32[]{:S(2)}) collective-permute-start(bf16[576,256]{1,0:T(8,128)(2,1)S(1)} %bitcast.74), channel_id=1, source_target_pairs={{0,56},{1,57},{2,58},{3,59},{4,60},{5,61},{6,62},{7,63},{8,32},{9,... | collective-permute-start | bytes 884744 | tf_op jit(solution)/shard_map/ppermute | solution.py:63
  93.5 55.5 %copy-start.1 = (f32[4,112,2048]{2,1,0:T(8,128)S(1)}, f32[4,112,2048]{2,1,0:T(8,128)}, u32[]{:S(2)}) copy-start(f32[4,112,2048]{2,1,0:T(8,128)} %weight.1) | copy-start | bytes 11010052
  93.5 15.7 %collective-permute-start.35 = (bf16[576,256]{1,0:T(8,128)(2,1)S(1)}, bf16[576,256]{1,0:T(8,128)(2,1)S(1)}, u32[]{:S(2)}, u32[]{:S(2)}) collective-permute-start(bf16[576,256]{1,0:T(8,128)(2,1)S(1)} %bitcast.66), channel_id=1, source_target_pairs={{0,1},{1,0},{2,3},{3,2},{4,5},{5,4},{6,7},{7,6},{8,9},{9,8},{10,11... | collective-permute-start | bytes 884744 | tf_op jit(solution)/shard_map/ppermute | solution.py:63
  93.6 16.1 %collective-permute-start.30 = (bf16[576,256]{1,0:T(8,128)(2,1)S(1)}, bf16[576,256]{1,0:T(8,128)(2,1)S(1)}, u32[]{:S(2)}, u32[]{:S(2)}) collective-permute-start(bf16[576,256]{1,0:T(8,128)(2,1)S(1)} %bitcast.67), channel_id=1, source_target_pairs={{0,6},{1,7},{2,0},{3,1},{4,2},{5,3},{6,4},{7,5},{8,14},{9,15},{10,... | collective-permute-start | bytes 884744 | tf_op jit(solution)/shard_map/ppermute | solution.py:63
  104.7 11.5 %collective-permute-start.29 = (bf16[576,256]{1,0:T(8,128)(2,1)S(1)}, bf16[576,256]{1,0:T(8,128)(2,1)S(1)}, u32[]{:S(2)}, u32[]{:S(2)}) collective-permute-start(bf16[576,256]{1,0:T(8,128)(2,1)S(1)} %bitcast.68), channel_id=1, source_target_pairs={{0,4},{1,5},{2,6},{3,7},{4,0},{5,1},{6,2},{7,3},{8,12},{9,13},{10,... | collective-permute-start | bytes 884744 | tf_op jit(solution)/shard_map/ppermute | solution.py:63
  106.5 13.7 %collective-permute-start.28 = (bf16[576,256]{1,0:T(8,128)(2,1)S(1)}, bf16[576,256]{1,0:T(8,128)(2,1)S(1)}, u32[]{:S(2)}, u32[]{:S(2)}) collective-permute-start(bf16[576,256]{1,0:T(8,128)(2,1)S(1)} %bitcast.69), channel_id=1, source_target_pairs={{0,2},{1,3},{2,4},{3,5},{4,6},{5,7},{6,0},{7,1},{8,10},{9,11},{10,... | collective-permute-start | bytes 884744 | tf_op jit(solution)/shard_map/ppermute | solution.py:63
  109.3 10.9 %collective-permute-start.34 = (bf16[576,256]{1,0:T(8,128)(2,1)S(1)}, bf16[576,256]{1,0:T(8,128)(2,1)S(1)}, u32[]{:S(2)}, u32[]{:S(2)}) collective-permute-start(bf16[576,256]{1,0:T(8,128)(2,1)S(1)} %collective-permute-done.18.refs_7_), channel_id=1, source_target_pairs={{0,1},{1,0},{2,3},{3,2},{4,5},{5,4},{6,7},{7,6},{8,9},{9,8},{10,11... | collective-permute-start | bytes 884744 | tf_op jit(solution)/shard_map/ppermute | solution.py:63
  109.3 11.4 %collective-permute-start.33 = (bf16[576,256]{1,0:T(8,128)(2,1)S(1)}, bf16[576,256]{1,0:T(8,128)(2,1)S(1)}, u32[]{:S(2)}, u32[]{:S(2)}) collective-permute-start(bf16[576,256]{1,0:T(8,128)(2,1)S(1)} %collective-permute-done.17.refs_6_), channel_id=1, source_target_pairs={{0,1},{1,0},{2,3},{3,2},{4,5},{5,4},{6,7},{7,6},{8,9},{9,8},{10,11... | collective-permute-start | bytes 884744 | tf_op jit(solution)/shard_map/ppermute | solution.py:63
  109.8 10.9 %collective-permute-start.32 = (bf16[576,256]{1,0:T(8,128)(2,1)S(1)}, bf16[576,256]{1,0:T(8,128)(2,1)S(1)}, u32[]{:S(2)}, u32[]{:S(2)}) collective-permute-start(bf16[576,256]{1,0:T(8,128)(2,1)S(1)} %collective-permute-done.16.refs_5_), channel_id=1, source_target_pairs={{0,1},{1,0},{2,3},{3,2},{4,5},{5,4},{6,7},{7,6},{8,9},{9,8},{10,11... | collective-permute-start | bytes 884744 | tf_op jit(solution)/shard_map/ppermute | solution.py:63
  116.2 4.5 %collective-permute-start.38 = (bf16[576,256]{1,0:T(8,128)(2,1)S(1)}, bf16[576,256]{1,0:T(8,128)(2,1)S(1)}, u32[]{:S(2)}, u32[]{:S(2)}) collective-permute-start(bf16[576,256]{1,0:T(8,128)(2,1)S(1)} %collective-permute-done.30.refs_11_), channel_id=1, source_target_pairs={{0,1},{1,0},{2,3},{3,2},{4,5},{5,4},{6,7},{7,6},{8,9},{9,8},{10,11... | collective-permute-start | bytes 884744 | tf_op jit(solution)/shard_map/ppermute | solution.py:63
  120.2 1.6 %collective-permute-start.37 = (bf16[576,256]{1,0:T(8,128)(2,1)S(1)}, bf16[576,256]{1,0:T(8,128)(2,1)S(1)}, u32[]{:S(2)}, u32[]{:S(2)}) collective-permute-start(bf16[576,256]{1,0:T(8,128)(2,1)S(1)} %collective-permute-done.29.refs_10_), channel_id=1, source_target_pairs={{0,1},{1,0},{2,3},{3,2},{4,5},{5,4},{6,7},{7,6},{8,9},{9,8},{10,11... | collective-permute-start | bytes 884744 | tf_op jit(solution)/shard_map/ppermute | solution.py:63
  120.2 2.0 %collective-permute-start.36 = (bf16[576,256]{1,0:T(8,128)(2,1)S(1)}, bf16[576,256]{1,0:T(8,128)(2,1)S(1)}, u32[]{:S(2)}, u32[]{:S(2)}) collective-permute-start(bf16[576,256]{1,0:T(8,128)(2,1)S(1)} %collective-permute-done.28.refs_9_), channel_id=1, source_target_pairs={{0,1},{1,0},{2,3},{3,2},{4,5},{5,4},{6,7},{7,6},{8,9},{9,8},{10,11... | collective-permute-start | bytes 884744 | tf_op jit(solution)/shard_map/ppermute | solution.py:63
  133.6 8.5 %collective-permute-start.39 = (bf16[112,2048]{1,0:T(8,128)(2,1)S(1)}, bf16[112,2048]{1,0:T(8,128)(2,1)S(1)}, u32[]{:S(2)}, u32[]{:S(2)}) collective-permute-start(bf16[112,2048]{1,0:T(8,128)(2,1)S(1)} %get-tuple-element.23), channel_id=1, source_target_pairs={{32,0},{9,1},{34,2},{11,3},{36,4},{13,5},{38,6},{15,7},{40,8},{17,... | collective-permute-start | bytes 1376264 | tf_op jit(solution)/shard_map/ppermute | solution.py:63
  136.0 10.9 %collective-permute-start.40 = (bf16[112,2048]{1,0:T(8,128)(2,1)S(1)}, bf16[112,2048]{1,0:T(8,128)(2,1)S(1)}, u32[]{:S(2)}, u32[]{:S(2)}) collective-permute-start(bf16[112,2048]{1,0:T(8,128)(2,1)S(1)} %get-tuple-element.24), channel_id=1, source_target_pairs={{40,0},{121,1},{42,2},{123,3},{44,4},{125,5},{46,6},{127,7},{48,8}... | collective-permute-start | bytes 1376264 | tf_op jit(solution)/shard_map/ppermute | solution.py:63
  138.0 11.1 %collective-permute-start.41 = (bf16[112,2048]{1,0:T(8,128)(2,1)}, bf16[112,2048]{1,0:T(8,128)(2,1)S(1)}, u32[]{:S(2)}, u32[]{:S(2)}) collective-permute-start(bf16[112,2048]{1,0:T(8,128)(2,1)} %get-tuple-element.25), channel_id=1, source_target_pairs={{96,0},{25,1},{98,2},{27,3},{100,4},{29,5},{102,6},{31,7},{104,8},... | collective-permute-start | bytes 1376264 | tf_op jit(solution)/shard_map/ppermute | solution.py:63

commit v2 on v1

--- a/solution.py
+++ b/solution.py
@@ -26,7 +26,6 @@
 HALF = SLOTS * BLOCK
 ROUTE = HALF // 2
 CHUNK = ROUTE // 4
-PIECE = CHUNK // 4
 SAME = [(a, b) for a in range(4) for b in range(a, 4)]
 
 
@@ -46,10 +45,8 @@
 
 def to_expert(d):
     def move(x, y, z, c):
-        if d == 2:
-            return (x + 1, y + 1, z, c) if c == 0 else (x - 1, y - 1, z, c)
-        d1 = 1 if d == 1 else -1
-        return (x + d1, y, z, c) if c == 0 else (x, y + d1, z, c)
+        along_x = (c == 0) != (d == 2)
+        return (x + d, y, z, c) if along_x else (x, y + d, z, c)
 
     return pairs(move)
 
@@ -61,6 +58,44 @@
 
 def shift(value, steps):
     return lax.ppermute(value, AXES, steps)
+
+
+def live_kernel(place, lengths, momentum, o0, o1, o2, o3, rows, sems):
+    home = place[3]
+    outs = (o0, o1, o2, o3)
+    experts = [lax.rem(home + d, 4) for d in range(4)]
+    loads = [
+        pltpu.make_async_copy(momentum.at[experts[d]], rows.at[d], sems.at[d])
+        for d in range(4)
+    ]
+    for load in loads:
+        load.start()
+    for d in (2, 1, 3, 0):
+        loads[d].wait()
+        slot = lax.broadcasted_iota(jnp.int32, (CAP, 128), 0)
+        keep = slot < lengths[experts[d]]
+        for at in range(0, R, 128):
+            value = rows[d, :, at:at + 128]
+            outs[d][:, at:at + 128] = jnp.where(keep, value, jnp.zeros_like(value))
+
+
+def live(place, lengths, momentum):
+    return pl.pallas_call(
+        live_kernel,
+        out_shape=[jax.ShapeDtypeStruct((CAP, R), jnp.bfloat16)] * 4,
+        in_specs=[
+            pl.BlockSpec(memory_space=pltpu.SMEM),
+            pl.BlockSpec(memory_space=pltpu.SMEM),
+            pl.BlockSpec(memory_space=pl.ANY),
+        ],
+        out_specs=[pl.BlockSpec(memory_space=pltpu.VMEM)] * 4,
+        scratch_shapes=[
+            pltpu.VMEM((4, CAP, R), jnp.bfloat16),
+            pltpu.SemaphoreType.DMA((4,)),
+        ],
+        compiler_params=pltpu.CompilerParams(vmem_limit_bytes=16 << 20),
+        name="live",
+    )(place, lengths, momentum)
 
 
 def gram_kernel(place, *refs):
@@ -260,11 +295,9 @@
     )(home, *returned, weight)
 
 
-def summed(parts, at=None):
+def summed(parts):
     total = None
     for part in parts:
-        if at is not None:
-            part = lax.dynamic_index_in_dim(part, at, 0, keepdims=False)
         part = part.astype(jnp.float32)
         total = part if total is None else total + part
     return total.astype(jnp.bfloat16)
@@ -274,47 +307,28 @@
     x, col = lax.axis_index("group"), lax.axis_index("col")
     y, z, core = col // 8, col // 2 % 4, col % 2
     home = (x + y) % 4
-    place = jnp.stack([core, x, z]).astype(jnp.int32)
-    slot_index = lax.broadcasted_iota(jnp.int32, (CAP, R), 0)
-
-    def live(d):
-        e = (home + d) % 4
-        rows = lax.dynamic_index_in_dim(momentum, e, 0, keepdims=False)
-        limit = lax.dynamic_index_in_dim(lengths, e, 0, keepdims=False)
-        return jnp.where(slot_index < limit, rows, jnp.zeros((), jnp.bfloat16))
+    place = jnp.stack([core, x, z, home]).astype(jnp.int32)
 
     routes = {d: to_expert(d) for d in (1, 2, 3)}
-    rows = [live(0)] + [shift(live(d), routes[d]) for d in (1, 2, 3)]
+    rows = live(place, lengths.reshape(4), momentum)
+    rows = [rows[0]] + [shift(rows[d], routes[d]) for d in (1, 2, 3)]
     other_rows = [shift(part, OTHER_CORE) for part in rows]
 
     parts = gram(place, rows + other_rows)
-    parts = [part.reshape(4, PIECE, BLOCK) for part in parts]
-    ring_of = ((RING_P, RING_Q), (RING_Q, RING_P))
-    own_of = ((x, z), (z, x))
-    summed_one = []
+    rings = (RING_P, RING_Q)
+    chunks = []
     for route in range(2):
         mine = parts[route * 4:route * 4 + 4]
-        summed_one.append([mine[0]] + [shift(mine[k], ring_of[route][0][k]) for k in (1, 2, 3)])
-    pieces = []
-    for route in range(2):
-        own = own_of[route][1]
-        send = [summed(summed_one[route], (own + k) % 4) for k in range(4)]
-        arrived = [send[0]] + [shift(send[k], ring_of[route][1][k]) for k in (1, 2, 3)]
-        pieces.append(arrived)
-    pieces = [summed(arrived) for arrived in pieces]
-
-    chunks = []
-    for route in range(2):
-        own = own_of[route][1]
-        chunk = jnp.zeros((4, PIECE, BLOCK), jnp.bfloat16)
-        got = [pieces[route]] + [shift(pieces[route], ring_of[route][1][k]) for k in (1, 2, 3)]
-        for k in range(4):
-            chunk = lax.dynamic_update_index_in_dim(chunk, got[k], (own + 4 - k) % 4, 0)
-        chunks.append(chunk.reshape(CHUNK, BLOCK))
+        chunks.append([mine[0]] + [shift(mine[k], rings[route][k]) for k in (1, 3, 2)])
+    chunks = [summed(got) for got in chunks]
+    chunks = [
+        [chunks[route]] + [shift(chunks[route], rings[1 - route][k]) for k in (1, 3, 2)]
+        for route in range(2)
+    ]
+    chunks = [summed(got) for got in chunks]
     mine = []
     for route in range(2):
-        mine += [chunks[route]]
-        mine += [shift(chunks[route], ring_of[route][0][k]) for k in (1, 2, 3)]
+        mine += [chunks[route]] + [shift(chunks[route], rings[route][k]) for k in (1, 2, 3)]
     others = [shift(chunk, OTHER_CORE) for chunk in mine]
 
     updates = update(place, rows, mine + others)

time: 153 us -> 134 us (0.88)
  starting transfers between devices: 64.6 us -> 57.2 us
  waiting for transfers between devices: 56 us -> 50.1 us
  other arithmetic: 6.53 us -> 0.69 us
    ppermute x42 -> x36, starting transfers between devices: 64.6 us -> 57.2 us  [shift(): return lax.ppermute(value, AXES, steps)]
    ppermute x42 -> x36, waiting for transfers between devices: 56 us -> 50.1 us  [shift(): return lax.ppermute(value, AXES, steps)]
    lt x2 -> x0, other arithmetic: 2.56 us -> none  [live(): return jnp.where(slot_index < limit, rows, jnp.zeros((), jnp.bfloat16))]
    pallas_call x0 -> x1, Pallas kernels: none -> 2.14 us  [live(): pl.pallas_call(live_kernel, out_shape=[jax.ShapeDtypeStruct((CAP, R), jnp...]
    select_n x1 -> x0, other arithmetic: 1.64 us -> none  [live(): return jnp.where(slot_index < limit, rows, jnp.zeros((), jnp.bfloat16))]
  transfers between devices with their start and end apart: 42 -> 36, of which waited for: 15 -> 22; matrix products, arithmetic and copies ran while one was open for 2% -> 0% of each run, Pallas kernels for 0% -> 0%
where the time goes in v2:
time: 134 us
  starting transfers between devices  57.2 us (43%)
  waiting for transfers between devices  50.1 us (37%)
  Pallas kernels  22.6 us (17%)
  local copies, waits for them, and re-layouts  2.18 us (2%)
    ppermute x36, starting transfers between devices, shift(): return lax.ppermute(value, AXES, steps)  57.2 us
    ppermute x36, waiting for transfers between devices, shift(): return lax.ppermute(value, AXES, steps)  50.1 us
    pallas_call x1, Pallas kernels, update(): pl.pallas_call(update_kernel, out_shape=[jax.ShapeDtypeStruct((CAP, R), j...  11.3 us
    pallas_call x1, Pallas kernels, gram(): pl.pallas_call(gram_kernel, out_shape=[jax.ShapeDtypeStruct((CHUNK, BLOCK...  6.1 us
    pallas_call x1, Pallas kernels, apply(): pl.pallas_call(apply_kernel, out_shape=[jax.ShapeDtypeStruct((4, CAP, R),...  3.02 us
  transfers between devices with their start and end apart: 36, of which 22 were waited for; matrix products, arithmetic and copies ran while one was open for 0% of the time, Pallas kernels for 0%

profile of v2, /device:TPU:0, one launch (start us, length us, event | category | flops | bytes accessed | tf_op | source)
XLA Modules:
  0.0 133.5 jit_solution(8848610708390136961)
XLA Ops:
  0.8 1.5 %copy-done.1 = bf16[4,112,2048]{2,1,0:T(8,128)(2,1)S(1)} copy-done((bf16[4,112,2048]{2,1,0:T(8,128)(2,1)S(1)}, bf16[4,112,2048]{2,1,0:T(8,128)(2,1)}, u32[]{:S(2)}) %copy-start.1) | copy-done | bytes 1835032
  2.3 0.7 copy-done.6
  2.9 2.1 %live.1 = (bf16[112,2048]{1,0:T(8,128)(2,1)S(1)}, bf16[112,2048]{1,0:T(8,128)(2,1)S(1)}, bf16[112,2048]{1,0:T(8,128)(2,1)S(1)}, bf16[112,2048]{1,0:T(8,128)(2,1)S(1)}) custom-call(s32[4]{0:T(128)S(1)} %pad_add_fusion.place, s32[4]{0:T(128)S(1)} %bitcast.5, bf16[4,112,2048]{2,1,0:T(8,128)(2,1)S(1)} %copy-done.1), custom_call_target="tpu_custom_call" | custom-call | tf_op jit(solution)/shard_map/live/pallas_call | solution.py:83
  5.1 1.6 %collective-permute-start = (bf16[112,2048]{1,0:T(8,128)(2,1)S(1)}, bf16[112,2048]{1,0:T(8,128)(2,1)S(1)}, u32[]{:S(2)}, u32[]{:S(2)}) collective-permute-start(bf16[112,2048]{1,0:T(8,128)(2,1)S(1)} %get-tuple-element.19), channel_id=1, source_target_pairs={{0,32},{1,9},{2,34},{3,11},{4,36},{5,13},{6,38},{7,15},{8,40},{9,1... | collective-permute-start | bytes 1376264 | tf_op jit(solution)/shard_map/ppermute | solution.py:60
  6.7 3.2 %collective-permute-start.1 = (bf16[112,2048]{1,0:T(8,128)(2,1)S(1)}, bf16[112,2048]{1,0:T(8,128)(2,1)S(1)}, u32[]{:S(2)}, u32[]{:S(2)}) collective-permute-start(bf16[112,2048]{1,0:T(8,128)(2,1)S(1)} %get-tuple-element.20), channel_id=1, source_target_pairs={{0,16},{1,65},{2,18},{3,67},{4,20},{5,69},{6,22},{7,71},{8,24},{9,... | collective-permute-start | bytes 1376264 | tf_op jit(solution)/shard_map/ppermute | solution.py:60
  9.9 1.7 %collective-permute-start.2 = (bf16[112,2048]{1,0:T(8,128)(2,1)S(1)}, bf16[112,2048]{1,0:T(8,128)(2,1)S(1)}, u32[]{:S(2)}, u32[]{:S(2)}) collective-permute-start(bf16[112,2048]{1,0:T(8,128)(2,1)S(1)} %get-tuple-element.21), channel_id=1, source_target_pairs={{0,96},{1,25},{2,98},{3,27},{4,100},{5,29},{6,102},{7,31},{8,104},... | collective-permute-start | bytes 1376264 | tf_op jit(solution)/shard_map/ppermute | solution.py:60
  11.7 8.0 %collective-permute-done.refs_1_ = bf16[112,2048]{1,0:T(8,128)(2,1)S(1)} collective-permute-done((bf16[112,2048]{1,0:T(8,128)(2,1)S(1)}, bf16[112,2048]{1,0:T(8,128)(2,1)S(1)}, u32[]{:S(2)}, u32[]{:S(2)}) %collective-permute-start) | collective-permute-done | bytes 458784 | tf_op jit(solution)/shard_map/ppermute | solution.py:60
  20.4 0.6 collective-permute-start.6
  21.0 0.5 collective-permute-done.4.refs_5_
  21.5 0.7 collective-permute-done.5.refs_6_
  22.2 0.7 collective-permute-done.6.refs_7_
  22.8 6.1 %gram.1 = (bf16[576,256]{1,0:T(8,128)(2,1)S(1)}, bf16[576,256]{1,0:T(8,128)(2,1)S(1)}, bf16[576,256]{1,0:T(8,128)(2,1)S(1)}, bf16[576,256]{1,0:T(8,128)(2,1)S(1)...) custom-call(s32[4]{0:T(128)S(1)} %pad_add_fusion.place, ...), custom_call_target="tpu_custom_call" | custom-call | tf_op jit(solution)/shard_map/gram/pallas_call | solution.py:149
  28.9 4.1 %collective-permute-start.7 = (bf16[576,256]{1,0:T(8,128)(2,1)S(1)}, bf16[576,256]{1,0:T(8,128)(2,1)S(1)}, u32[]{:S(2)}, u32[]{:S(2)}) collective-permute-start(bf16[576,256]{1,0:T(8,128)(2,1)S(1)} %get-tuple-element.23), channel_id=1, source_target_pairs={{0,56},{1,57},{2,58},{3,59},{4,60},{5,61},{6,62},{7,63},{8,32},{9,... | collective-permute-start | bytes 884744 | tf_op jit(solution)/shard_map/ppermute | solution.py:60
  33.1 2.9 %collective-permute-start.9 = (bf16[576,256]{1,0:T(8,128)(2,1)S(1)}, bf16[576,256]{1,0:T(8,128)(2,1)S(1)}, u32[]{:S(2)}, u32[]{:S(2)}) collective-permute-start(bf16[576,256]{1,0:T(8,128)(2,1)S(1)} %get-tuple-element.25), channel_id=1, source_target_pairs={{0,80},{1,81},{2,82},{3,83},{4,84},{5,85},{6,86},{7,87},{8,88},{9,... | collective-permute-start | bytes 884744 | tf_op jit(solution)/shard_map/ppermute | solution.py:60
  36.0 1.9 %collective-permute-start.16 = (bf16[576,256]{1,0:T(8,128)(2,1)S(1)}, bf16[576,256]{1,0:T(8,128)(2,1)S(1)}, u32[]{:S(2)}, u32[]{:S(2)}) collective-permute-start(bf16[576,256]{1,0:T(8,128)(2,1)S(1)} %get-tuple-element.27), channel_id=1, source_target_pairs={{0,2},{1,3},{2,4},{3,5},{4,6},{5,7},{6,0},{7,1},{8,10},{9,11},{10,... | collective-permute-start | bytes 884744 | tf_op jit(solution)/shard_map/ppermute | solution.py:60
  38.0 2.1 %collective-permute-start.17 = (bf16[576,256]{1,0:T(8,128)(2,1)S(1)}, bf16[576,256]{1,0:T(8,128)(2,1)S(1)}, u32[]{:S(2)}, u32[]{:S(2)}) collective-permute-start(bf16[576,256]{1,0:T(8,128)(2,1)S(1)} %get-tuple-element.28), channel_id=1, source_target_pairs={{0,6},{1,7},{2,0},{3,1},{4,2},{5,3},{6,4},{7,5},{8,14},{9,15},{10,... | collective-permute-start | bytes 884744 | tf_op jit(solution)/shard_map/ppermute | solution.py:60
  40.4 3.9 %collective-permute-start.18 = (bf16[576,256]{1,0:T(8,128)(2,1)S(1)}, bf16[576,256]{1,0:T(8,128)(2,1)S(1)}, u32[]{:S(2)}, u32[]{:S(2)}) collective-permute-start(bf16[576,256]{1,0:T(8,128)(2,1)S(1)} %get-tuple-element.29), channel_id=1, source_target_pairs={{0,4},{1,5},{2,6},{3,7},{4,0},{5,1},{6,2},{7,3},{8,12},{9,13},{10,... | collective-permute-start | bytes 884744 | tf_op jit(solution)/shard_map/ppermute | solution.py:60
  44.3 2.7 %collective-permute-done.8 = bf16[576,256]{1,0:T(8,128)(2,1)S(1)} collective-permute-done((bf16[576,256]{1,0:T(8,128)(2,1)S(1)}, bf16[576,256]{1,0:T(8,128)(2,1)S(1)}, u32[]{:S(2)}, u32[]{:S(2)}) %collective-permute-start.8) | collective-permute-done | bytes 294944 | tf_op jit(solution)/shard_map/ppermute | solution.py:60
  46.9 3.3 %collective-permute-done.9 = bf16[576,256]{1,0:T(8,128)(2,1)S(1)} collective-permute-done((bf16[576,256]{1,0:T(8,128)(2,1)S(1)}, bf16[576,256]{1,0:T(8,128)(2,1)S(1)}, u32[]{:S(2)}, u32[]{:S(2)}) %collective-permute-start.9) | collective-permute-done | bytes 294944 | tf_op jit(solution)/shard_map/ppermute | solution.py:60
  50.4 3.9 %collective-permute-start.12 = (bf16[576,256]{1,0:T(8,128)(2,1)S(1)}, bf16[576,256]{1,0:T(8,128)(2,1)S(1)}, u32[]{:S(2)}, u32[]{:S(2)}) collective-permute-start(bf16[576,256]{1,0:T(8,128)(2,1)S(1)} %add_convert_fusion.3), channel_id=1, source_target_pairs={{0,4},{1,5},{2,6},{3,7},{4,0},{5,1},{6,2},{7,3},{8,12},{9,13},{10,... | collective-permute-start | bytes 884744 | tf_op jit(solution)/shard_map/ppermute | solution.py:60
  54.3 0.7 collective-permute-start.11
  55.0 1.3 collective-permute-start.10
  56.5 2.7 %collective-permute-start.21 = (bf16[576,256]{1,0:T(8,128)(2,1)S(1)}, bf16[576,256]{1,0:T(8,128)(2,1)S(1)}, u32[]{:S(2)}, u32[]{:S(2)}) collective-permute-start(bf16[576,256]{1,0:T(8,128)(2,1)S(1)} %add_convert_fusion.1), channel_id=1, source_target_pairs={{0,80},{1,81},{2,82},{3,83},{4,84},{5,85},{6,86},{7,87},{8,88},{9,... | collective-permute-start | bytes 884744 | tf_op jit(solution)/shard_map/ppermute | solution.py:60
  59.2 2.1 %collective-permute-start.20 = (bf16[576,256]{1,0:T(8,128)(2,1)S(1)}, bf16[576,256]{1,0:T(8,128)(2,1)S(1)}, u32[]{:S(2)}, u32[]{:S(2)}) collective-permute-start(bf16[576,256]{1,0:T(8,128)(2,1)S(1)} %add_convert_fusion.1), channel_id=1, source_target_pairs={{0,104},{1,105},{2,106},{3,107},{4,108},{5,109},{6,110},{7,111},{8... | collective-permute-start | bytes 884744 | tf_op jit(solution)/shard_map/ppermute | solution.py:60
  61.3 1.0 collective-permute-done.12
  62.3 1.9 %collective-permute-start.19 = (bf16[576,256]{1,0:T(8,128)(2,1)S(1)}, bf16[576,256]{1,0:T(8,128)(2,1)S(1)}, u32[]{:S(2)}, u32[]{:S(2)}) collective-permute-start(bf16[576,256]{1,0:T(8,128)(2,1)S(1)} %add_convert_fusion.1), channel_id=1, source_target_pairs={{0,56},{1,57},{2,58},{3,59},{4,60},{5,61},{6,62},{7,63},{8,32},{9,... | collective-permute-start | bytes 884744 | tf_op jit(solution)/shard_map/ppermute | solution.py:60
  64.2 3.4 %collective-permute-done.11 = bf16[576,256]{1,0:T(8,128)(2,1)S(1)} collective-permute-done((bf16[576,256]{1,0:T(8,128)(2,1)S(1)}, bf16[576,256]{1,0:T(8,128)(2,1)S(1)}, u32[]{:S(2)}, u32[]{:S(2)}) %collective-permute-start.11) | collective-permute-done | bytes 294944 | tf_op jit(solution)/shard_map/ppermute | solution.py:60
  67.9 3.2 %collective-permute-start.15 = (bf16[576,256]{1,0:T(8,128)(2,1)S(1)}, bf16[576,256]{1,0:T(8,128)(2,1)S(1)}, u32[]{:S(2)}, u32[]{:S(2)}) collective-permute-start(bf16[576,256]{1,0:T(8,128)(2,1)S(1)} %add_convert_fusion.2.refs_4_), channel_id=1, source_target_pairs={{0,104},{1,105},{2,106},{3,107},{4,108},{5,109},{6,110},{7,111},{8... | collective-permute-start | bytes 884744 | tf_op jit(solution)/shard_map/ppermute | solution.py:60
  71.1 2.0 %collective-permute-start.14 = (bf16[576,256]{1,0:T(8,128)(2,1)S(1)}, bf16[576,256]{1,0:T(8,128)(2,1)S(1)}, u32[]{:S(2)}, u32[]{:S(2)}) collective-permute-start(bf16[576,256]{1,0:T(8,128)(2,1)S(1)} %add_convert_fusion.2.refs_4_), channel_id=1, source_target_pairs={{0,80},{1,81},{2,82},{3,83},{4,84},{5,85},{6,86},{7,87},{8,88},{9,... | collective-permute-start | bytes 884744 | tf_op jit(solution)/shard_map/ppermute | solution.py:60
  73.1 1.7 %collective-permute-done.20 = bf16[576,256]{1,0:T(8,128)(2,1)S(1)} collective-permute-done((bf16[576,256]{1,0:T(8,128)(2,1)S(1)}, bf16[576,256]{1,0:T(8,128)(2,1)S(1)}, u32[]{:S(2)}, u32[]{:S(2)}) %collective-permute-start.20) | collective-permute-done | bytes 294944 | tf_op jit(solution)/shard_map/ppermute | solution.py:60
  74.8 3.4 %collective-permute-start.13 = (bf16[576,256]{1,0:T(8,128)(2,1)S(1)}, bf16[576,256]{1,0:T(8,128)(2,1)S(1)}, u32[]{:S(2)}, u32[]{:S(2)}) collective-permute-start(bf16[576,256]{1,0:T(8,128)(2,1)S(1)} %add_convert_fusion.2.refs_4_), channel_id=1, source_target_pairs={{0,56},{1,57},{2,58},{3,59},{4,60},{5,61},{6,62},{7,63},{8,32},{9,... | collective-permute-start | bytes 884744 | tf_op jit(solution)/shard_map/ppermute | solution.py:60
  78.4 2.0 %collective-permute-start.24 = (bf16[576,256]{1,0:T(8,128)(2,1)S(1)}, bf16[576,256]{1,0:T(8,128)(2,1)S(1)}, u32[]{:S(2)}, u32[]{:S(2)}) collective-permute-start(bf16[576,256]{1,0:T(8,128)(2,1)S(1)} %add_convert_fusion.refs_8_), channel_id=1, source_target_pairs={{0,6},{1,7},{2,0},{3,1},{4,2},{5,3},{6,4},{7,5},{8,14},{9,15},{10,... | collective-permute-start | bytes 884744 | tf_op jit(solution)/shard_map/ppermute | solution.py:60
  80.4 2.3 %collective-permute-done.15.refs_7_ = bf16[576,256]{1,0:T(8,128)(2,1)S(1)} collective-permute-done((bf16[576,256]{1,0:T(8,128)(2,1)S(1)}, bf16[576,256]{1,0:T(8,128)(2,1)S(1)}, u32[]{:S(2)}, u32[]{:S(2)}) %collective-permute-start.15) | collective-permute-done | bytes 294944 | tf_op jit(solution)/shard_map/ppermute | solution.py:60
  82.7 3.9 %collective-permute-start.23 = (bf16[576,256]{1,0:T(8,128)(2,1)S(1)}, bf16[576,256]{1,0:T(8,128)(2,1)S(1)}, u32[]{:S(2)}, u32[]{:S(2)}) collective-permute-start(bf16[576,256]{1,0:T(8,128)(2,1)S(1)} %add_convert_fusion.refs_8_), channel_id=1, source_target_pairs={{0,4},{1,5},{2,6},{3,7},{4,0},{5,1},{6,2},{7,3},{8,12},{9,13},{10,... | collective-permute-start | bytes 884744 | tf_op jit(solution)/shard_map/ppermute | solution.py:60
  86.7 1.0 collective-permute-done.14.refs_6_
  87.7 1.0 collective-permute-start.22
  88.7 3.5 %collective-permute-done.13.refs_5_ = bf16[576,256]{1,0:T(8,128)(2,1)S(1)} collective-permute-done((bf16[576,256]{1,0:T(8,128)(2,1)S(1)}, bf16[576,256]{1,0:T(8,128)(2,1)S(1)}, u32[]{:S(2)}, u32[]{:S(2)}) %collective-permute-start.13) | collective-permute-done | bytes 294944 | tf_op jit(solution)/shard_map/ppermute | solution.py:60
  92.2 0.5 collective-permute-start.27
  92.7 0.8 collective-permute-done.24.refs_11_
  93.5 1.1 collective-permute-done.23.refs_10_
  94.6 5.1 %collective-permute-done.22.refs_9_ = bf16[576,256]{1,0:T(8,128)(2,1)S(1)} collective-permute-done((bf16[576,256]{1,0:T(8,128)(2,1)S(1)}, bf16[576,256]{1,0:T(8,128)(2,1)S(1)}, u32[]{:S(2)}, u32[]{:S(2)}) %collective-permute-start.22) | collective-permute-done | bytes 294944 | tf_op jit(solution)/shard_map/ppermute | solution.py:60
  99.6 0.5 collective-permute-start.30
  100.2 1.1 collective-permute-done.31.refs_18_
  101.6 11.3 %update.1 = (bf16[112,2048]{1,0:T(8,128)(2,1)S(1)}, bf16[112,2048]{1,0:T(8,128)(2,1)S(1)}, bf16[112,2048]{1,0:T(8,128)(2,1)S(1)}, bf16[112,2048]{1,0:T(8,128)(2,1)}) custom-call(s32[4]{0:T(128)S(1)} %pad_add_fusion.place, bf16[112,2048]{1,0:T(8,128)(2,1)} %copy-done.2, bf16[112,2048]{1,0:T(8,128)(2,1)} %copy-done.3, bf16[112,2048]{1,0:T(8,128)(2,1)} %copy-done.4, ...), custom_call_target="tpu_custom_call" | custom-call | tf_op jit(solution)/shard_map/update/pallas_call | solution.py:248
  113.0 5.2 %collective-permute-start.33 = (bf16[112,2048]{1,0:T(8,128)(2,1)S(1)}, bf16[112,2048]{1,0:T(8,128)(2,1)S(1)}, u32[]{:S(2)}, u32[]{:S(2)}) collective-permute-start(bf16[112,2048]{1,0:T(8,128)(2,1)S(1)} %get-tuple-element.31), channel_id=1, source_target_pairs={{32,0},{9,1},{34,2},{11,3},{36,4},{13,5},{38,6},{15,7},{40,8},{17,... | collective-permute-start | bytes 1376264 | tf_op jit(solution)/shard_map/ppermute | solution.py:60
  118.2 10.7 %collective-permute-done.33.a1 = bf16[112,2048]{1,0:T(8,128)(2,1)S(1)} collective-permute-done((bf16[112,2048]{1,0:T(8,128)(2,1)S(1)}, bf16[112,2048]{1,0:T(8,128)(2,1)S(1)}, u32[]{:S(2)}, u32[]{:S(2)}) %collective-permute-start.33) | collective-permute-done | bytes 458784 | tf_op jit(solution)/shard_map/ppermute | solution.py:60
  129.0 1.5 %collective-permute-done.34.a2 = bf16[112,2048]{1,0:T(8,128)(2,1)S(1)} collective-permute-done((bf16[112,2048]{1,0:T(8,128)(2,1)S(1)}, bf16[112,2048]{1,0:T(8,128)(2,1)S(1)}, u32[]{:S(2)}, u32[]{:S(2)}) %collective-permute-start.34) | collective-permute-done | bytes 458784 | tf_op jit(solution)/shard_map/ppermute | solution.py:60
  130.5 3.0 %apply.1 = (bf16[4,112,2048]{2,1,0:T(8,128)(2,1)}, f32[4,112,2048]{2,1,0:T(8,128)}) custom-call(s32[1]{0:T(128)} %bitcast.home, bf16[112,2048]{1,0:T(8,128)(2,1)S(1)} %get-tuple-element.30.a0, bf16[112,2048]{1,0:T(8,128)(2,1)S(1)} %collective-permute-done.33.a1, bf16[112,2048]{1,0:T(8,128)(2,1)S(1)} %collective-permute-done.34.a2, ...), custom_call_target="tpu_custom_call" | custom-call | tf_op jit(solution)/shard_map/apply/pallas_call | solution.py:281
  (47 shorter events, 2.5 us)
Async XLA Ops:
  0.8 1.5 %copy-start.1 = (bf16[4,112,2048]{2,1,0:T(8,128)(2,1)S(1)}, bf16[4,112,2048]{2,1,0:T(8,128)(2,1)}, u32[]{:S(2)}) copy-start(bf16[4,112,2048]{2,1,0:T(8,128)(2,1)} %momentum.1) | copy-start | bytes 5505028
  2.3 0.7 copy-start.6
  5.1 62.7 %copy-start.2 = (bf16[112,2048]{1,0:T(8,128)(2,1)}, bf16[112,2048]{1,0:T(8,128)(2,1)S(1)}, u32[]{:S(2)}) copy-start(bf16[112,2048]{1,0:T(8,128)(2,1)S(1)} %get-tuple-element.18.refs_0_) | copy-start | bytes 1376260
  5.1 14.6 %collective-permute-start = (bf16[112,2048]{1,0:T(8,128)(2,1)S(1)}, bf16[112,2048]{1,0:T(8,128)(2,1)S(1)}, u32[]{:S(2)}, u32[]{:S(2)}) collective-permute-start(bf16[112,2048]{1,0:T(8,128)(2,1)S(1)} %get-tuple-element.19), channel_id=1, source_target_pairs={{0,32},{1,9},{2,34},{3,11},{4,36},{5,13},{6,38},{7,15},{8,40},{9,1... | collective-permute-start | bytes 1376264 | tf_op jit(solution)/shard_map/ppermute | solution.py:60
  6.7 13.2 %collective-permute-start.1 = (bf16[112,2048]{1,0:T(8,128)(2,1)S(1)}, bf16[112,2048]{1,0:T(8,128)(2,1)S(1)}, u32[]{:S(2)}, u32[]{:S(2)}) collective-permute-start(bf16[112,2048]{1,0:T(8,128)(2,1)S(1)} %get-tuple-element.20), channel_id=1, source_target_pairs={{0,16},{1,65},{2,18},{3,67},{4,20},{5,69},{6,22},{7,71},{8,24},{9,... | collective-permute-start | bytes 1376264 | tf_op jit(solution)/shard_map/ppermute | solution.py:60
  9.9 10.5 %collective-permute-start.2 = (bf16[112,2048]{1,0:T(8,128)(2,1)S(1)}, bf16[112,2048]{1,0:T(8,128)(2,1)S(1)}, u32[]{:S(2)}, u32[]{:S(2)}) collective-permute-start(bf16[112,2048]{1,0:T(8,128)(2,1)S(1)} %get-tuple-element.21), channel_id=1, source_target_pairs={{0,96},{1,25},{2,98},{3,27},{4,100},{5,29},{6,102},{7,31},{8,104},... | collective-permute-start | bytes 1376264 | tf_op jit(solution)/shard_map/ppermute | solution.py:60
  11.7 9.3 %collective-permute-start.3 = (bf16[112,2048]{1,0:T(8,128)(2,1)S(1)}, bf16[112,2048]{1,0:T(8,128)(2,1)S(1)}, u32[]{:S(2)}, u32[]{:S(2)}) collective-permute-start(bf16[112,2048]{1,0:T(8,128)(2,1)S(1)} %get-tuple-element.18.refs_0_), channel_id=1, source_target_pairs={{0,1},{1,0},{2,3},{3,2},{4,5},{5,4},{6,7},{7,6},{8,9},{9,8},{10,11... | collective-permute-start | bytes 1376264 | tf_op jit(solution)/shard_map/ppermute | solution.py:60
  19.7 48.1 %copy-start.3 = (bf16[112,2048]{1,0:T(8,128)(2,1)}, bf16[112,2048]{1,0:T(8,128)(2,1)S(1)}, u32[]{:S(2)}) copy-start(bf16[112,2048]{1,0:T(8,128)(2,1)S(1)} %collective-permute-done.refs_1_) | copy-start | bytes 1376260
  19.7 1.8 %collective-permute-start.4 = (bf16[112,2048]{1,0:T(8,128)(2,1)S(1)}, bf16[112,2048]{1,0:T(8,128)(2,1)S(1)}, u32[]{:S(2)}, u32[]{:S(2)}) collective-permute-start(bf16[112,2048]{1,0:T(8,128)(2,1)S(1)} %collective-permute-done.refs_1_), channel_id=1, source_target_pairs={{0,1},{1,0},{2,3},{3,2},{4,5},{5,4},{6,7},{7,6},{8,9},{9,8},{10,11... | collective-permute-start | bytes 1376264 | tf_op jit(solution)/shard_map/ppermute | solution.py:60
  19.9 47.9 %copy-start.4 = (bf16[112,2048]{1,0:T(8,128)(2,1)}, bf16[112,2048]{1,0:T(8,128)(2,1)S(1)}, u32[]{:S(2)}) copy-start(bf16[112,2048]{1,0:T(8,128)(2,1)S(1)} %collective-permute-done.1.refs_2_) | copy-start | bytes 1376260
  19.9 2.2 %collective-permute-start.5 = (bf16[112,2048]{1,0:T(8,128)(2,1)S(1)}, bf16[112,2048]{1,0:T(8,128)(2,1)S(1)}, u32[]{:S(2)}, u32[]{:S(2)}) collective-permute-start(bf16[112,2048]{1,0:T(8,128)(2,1)S(1)} %collective-permute-done.1.refs_2_), channel_id=1, source_target_pairs={{0,1},{1,0},{2,3},{3,2},{4,5},{5,4},{6,7},{7,6},{8,9},{9,8},{10,11... | collective-permute-start | bytes 1376264 | tf_op jit(solution)/shard_map/ppermute | solution.py:60
  20.4 47.4 %copy-start.5 = (bf16[112,2048]{1,0:T(8,128)(2,1)}, bf16[112,2048]{1,0:T(8,128)(2,1)S(1)}, u32[]{:S(2)}) copy-start(bf16[112,2048]{1,0:T(8,128)(2,1)S(1)} %collective-permute-done.2.refs_3_) | copy-start | bytes 1376260
  20.4 2.4 %collective-permute-start.6 = (bf16[112,2048]{1,0:T(8,128)(2,1)S(1)}, bf16[112,2048]{1,0:T(8,128)(2,1)S(1)}, u32[]{:S(2)}, u32[]{:S(2)}) collective-permute-start(bf16[112,2048]{1,0:T(8,128)(2,1)S(1)} %collective-permute-done.2.refs_3_), channel_id=1, source_target_pairs={{0,1},{1,0},{2,3},{3,2},{4,5},{5,4},{6,7},{7,6},{8,9},{9,8},{10,11... | collective-permute-start | bytes 1376264 | tf_op jit(solution)/shard_map/ppermute | solution.py:60
  28.9 11.5 %collective-permute-start.7 = (bf16[576,256]{1,0:T(8,128)(2,1)S(1)}, bf16[576,256]{1,0:T(8,128)(2,1)S(1)}, u32[]{:S(2)}, u32[]{:S(2)}) collective-permute-start(bf16[576,256]{1,0:T(8,128)(2,1)S(1)} %get-tuple-element.23), channel_id=1, source_target_pairs={{0,56},{1,57},{2,58},{3,59},{4,60},{5,61},{6,62},{7,63},{8,32},{9,... | collective-permute-start | bytes 884744 | tf_op jit(solution)/shard_map/ppermute | solution.py:60
  33.0 13.9 %collective-permute-start.8 = (bf16[576,256]{1,0:T(8,128)(2,1)S(1)}, bf16[576,256]{1,0:T(8,128)(2,1)S(1)}, u32[]{:S(2)}, u32[]{:S(2)}) collective-permute-start(bf16[576,256]{1,0:T(8,128)(2,1)S(1)} %get-tuple-element.24), channel_id=1, source_target_pairs={{0,104},{1,105},{2,106},{3,107},{4,108},{5,109},{6,110},{7,111},{8... | collective-permute-start | bytes 884744 | tf_op jit(solution)/shard_map/ppermute | solution.py:60
  33.1 17.1 %collective-permute-start.9 = (bf16[576,256]{1,0:T(8,128)(2,1)S(1)}, bf16[576,256]{1,0:T(8,128)(2,1)S(1)}, u32[]{:S(2)}, u32[]{:S(2)}) collective-permute-start(bf16[576,256]{1,0:T(8,128)(2,1)S(1)} %get-tuple-element.25), channel_id=1, source_target_pairs={{0,80},{1,81},{2,82},{3,83},{4,84},{5,85},{6,86},{7,87},{8,88},{9,... | collective-permute-start | bytes 884744 | tf_op jit(solution)/shard_map/ppermute | solution.py:60
  36.0 19.0 %collective-permute-start.16 = (bf16[576,256]{1,0:T(8,128)(2,1)S(1)}, bf16[576,256]{1,0:T(8,128)(2,1)S(1)}, u32[]{:S(2)}, u32[]{:S(2)}) collective-permute-start(bf16[576,256]{1,0:T(8,128)(2,1)S(1)} %get-tuple-element.27), channel_id=1, source_target_pairs={{0,2},{1,3},{2,4},{3,5},{4,6},{5,7},{6,0},{7,1},{8,10},{9,11},{10,... | collective-permute-start | bytes 884744 | tf_op jit(solution)/shard_map/ppermute | solution.py:60
  38.0 18.4 %collective-permute-start.17 = (bf16[576,256]{1,0:T(8,128)(2,1)S(1)}, bf16[576,256]{1,0:T(8,128)(2,1)S(1)}, u32[]{:S(2)}, u32[]{:S(2)}) collective-permute-start(bf16[576,256]{1,0:T(8,128)(2,1)S(1)} %get-tuple-element.28), channel_id=1, source_target_pairs={{0,6},{1,7},{2,0},{3,1},{4,2},{5,3},{6,4},{7,5},{8,14},{9,15},{10,... | collective-permute-start | bytes 884744 | tf_op jit(solution)/shard_map/ppermute | solution.py:60
  40.4 16.0 %collective-permute-start.18 = (bf16[576,256]{1,0:T(8,128)(2,1)S(1)}, bf16[576,256]{1,0:T(8,128)(2,1)S(1)}, u32[]{:S(2)}, u32[]{:S(2)}) collective-permute-start(bf16[576,256]{1,0:T(8,128)(2,1)S(1)} %get-tuple-element.29), channel_id=1, source_target_pairs={{0,4},{1,5},{2,6},{3,7},{4,0},{5,1},{6,2},{7,3},{8,12},{9,13},{10,... | collective-permute-start | bytes 884744 | tf_op jit(solution)/shard_map/ppermute | solution.py:60
  50.4 11.9 %collective-permute-start.12 = (bf16[576,256]{1,0:T(8,128)(2,1)S(1)}, bf16[576,256]{1,0:T(8,128)(2,1)S(1)}, u32[]{:S(2)}, u32[]{:S(2)}) collective-permute-start(bf16[576,256]{1,0:T(8,128)(2,1)S(1)} %add_convert_fusion.3), channel_id=1, source_target_pairs={{0,4},{1,5},{2,6},{3,7},{4,0},{5,1},{6,2},{7,3},{8,12},{9,13},{10,... | collective-permute-start | bytes 884744 | tf_op jit(solution)/shard_map/ppermute | solution.py:60
  54.3 13.3 %collective-permute-start.11 = (bf16[576,256]{1,0:T(8,128)(2,1)S(1)}, bf16[576,256]{1,0:T(8,128)(2,1)S(1)}, u32[]{:S(2)}, u32[]{:S(2)}) collective-permute-start(bf16[576,256]{1,0:T(8,128)(2,1)S(1)} %add_convert_fusion.3), channel_id=1, source_target_pairs={{0,6},{1,7},{2,0},{3,1},{4,2},{5,3},{6,4},{7,5},{8,14},{9,15},{10,... | collective-permute-start | bytes 884744 | tf_op jit(solution)/shard_map/ppermute | solution.py:60
  55.0 12.6 %collective-permute-start.10 = (bf16[576,256]{1,0:T(8,128)(2,1)S(1)}, bf16[576,256]{1,0:T(8,128)(2,1)S(1)}, u32[]{:S(2)}, u32[]{:S(2)}) collective-permute-start(bf16[576,256]{1,0:T(8,128)(2,1)S(1)} %add_convert_fusion.3), channel_id=1, source_target_pairs={{0,2},{1,3},{2,4},{3,5},{4,6},{5,7},{6,0},{7,1},{8,10},{9,11},{10,... | collective-permute-start | bytes 884744 | tf_op jit(solution)/shard_map/ppermute | solution.py:60
  56.5 14.6 %collective-permute-start.21 = (bf16[576,256]{1,0:T(8,128)(2,1)S(1)}, bf16[576,256]{1,0:T(8,128)(2,1)S(1)}, u32[]{:S(2)}, u32[]{:S(2)}) collective-permute-start(bf16[576,256]{1,0:T(8,128)(2,1)S(1)} %add_convert_fusion.1), channel_id=1, source_target_pairs={{0,80},{1,81},{2,82},{3,83},{4,84},{5,85},{6,86},{7,87},{8,88},{9,... | collective-permute-start | bytes 884744 | tf_op jit(solution)/shard_map/ppermute | solution.py:60
  59.2 15.6 %collective-permute-start.20 = (bf16[576,256]{1,0:T(8,128)(2,1)S(1)}, bf16[576,256]{1,0:T(8,128)(2,1)S(1)}, u32[]{:S(2)}, u32[]{:S(2)}) collective-permute-start(bf16[576,256]{1,0:T(8,128)(2,1)S(1)} %add_convert_fusion.1), channel_id=1, source_target_pairs={{0,104},{1,105},{2,106},{3,107},{4,108},{5,109},{6,110},{7,111},{8... | collective-permute-start | bytes 884744 | tf_op jit(solution)/shard_map/ppermute | solution.py:60
  62.3 15.8 %collective-permute-start.19 = (bf16[576,256]{1,0:T(8,128)(2,1)S(1)}, bf16[576,256]{1,0:T(8,128)(2,1)S(1)}, u32[]{:S(2)}, u32[]{:S(2)}) collective-permute-start(bf16[576,256]{1,0:T(8,128)(2,1)S(1)} %add_convert_fusion.1), channel_id=1, source_target_pairs={{0,56},{1,57},{2,58},{3,59},{4,60},{5,61},{6,62},{7,63},{8,32},{9,... | collective-permute-start | bytes 884744 | tf_op jit(solution)/shard_map/ppermute | solution.py:60
  67.8 62.7 %copy-start = (f32[4,112,2048]{2,1,0:T(8,128)S(1)}, f32[4,112,2048]{2,1,0:T(8,128)}, u32[]{:S(2)}) copy-start(f32[4,112,2048]{2,1,0:T(8,128)} %weight.1) | copy-start | bytes 11010052
  67.8 10.6 %collective-permute-start.25 = (bf16[576,256]{1,0:T(8,128)(2,1)S(1)}, bf16[576,256]{1,0:T(8,128)(2,1)S(1)}, u32[]{:S(2)}, u32[]{:S(2)}) collective-permute-start(bf16[576,256]{1,0:T(8,128)(2,1)S(1)} %add_convert_fusion.2.refs_4_), channel_id=1, source_target_pairs={{0,1},{1,0},{2,3},{3,2},{4,5},{5,4},{6,7},{7,6},{8,9},{9,8},{10,11... | collective-permute-start | bytes 884744 | tf_op jit(solution)/shard_map/ppermute | solution.py:60
  67.9 14.8 %collective-permute-start.15 = (bf16[576,256]{1,0:T(8,128)(2,1)S(1)}, bf16[576,256]{1,0:T(8,128)(2,1)S(1)}, u32[]{:S(2)}, u32[]{:S(2)}) collective-permute-start(bf16[576,256]{1,0:T(8,128)(2,1)S(1)} %add_convert_fusion.2.refs_4_), channel_id=1, source_target_pairs={{0,104},{1,105},{2,106},{3,107},{4,108},{5,109},{6,110},{7,111},{8... | collective-permute-start | bytes 884744 | tf_op jit(solution)/shard_map/ppermute | solution.py:60
  71.1 16.5 %collective-permute-start.14 = (bf16[576,256]{1,0:T(8,128)(2,1)S(1)}, bf16[576,256]{1,0:T(8,128)(2,1)S(1)}, u32[]{:S(2)}, u32[]{:S(2)}) collective-permute-start(bf16[576,256]{1,0:T(8,128)(2,1)S(1)} %add_convert_fusion.2.refs_4_), channel_id=1, source_target_pairs={{0,80},{1,81},{2,82},{3,83},{4,84},{5,85},{6,86},{7,87},{8,88},{9,... | collective-permute-start | bytes 884744 | tf_op jit(solution)/shard_map/ppermute | solution.py:60
  74.8 17.4 %collective-permute-start.13 = (bf16[576,256]{1,0:T(8,128)(2,1)S(1)}, bf16[576,256]{1,0:T(8,128)(2,1)S(1)}, u32[]{:S(2)}, u32[]{:S(2)}) collective-permute-start(bf16[576,256]{1,0:T(8,128)(2,1)S(1)} %add_convert_fusion.2.refs_4_), channel_id=1, source_target_pairs={{0,56},{1,57},{2,58},{3,59},{4,60},{5,61},{6,62},{7,63},{8,32},{9,... | collective-permute-start | bytes 884744 | tf_op jit(solution)/shard_map/ppermute | solution.py:60
  78.3 13.9 %collective-permute-start.29 = (bf16[576,256]{1,0:T(8,128)(2,1)S(1)}, bf16[576,256]{1,0:T(8,128)(2,1)S(1)}, u32[]{:S(2)}, u32[]{:S(2)}) collective-permute-start(bf16[576,256]{1,0:T(8,128)(2,1)S(1)} %add_convert_fusion.refs_8_), channel_id=1, source_target_pairs={{0,1},{1,0},{2,3},{3,2},{4,5},{5,4},{6,7},{7,6},{8,9},{9,8},{10,11... | collective-permute-start | bytes 884744 | tf_op jit(solution)/shard_map/ppermute | solution.py:60
  78.4 15.1 %collective-permute-start.24 = (bf16[576,256]{1,0:T(8,128)(2,1)S(1)}, bf16[576,256]{1,0:T(8,128)(2,1)S(1)}, u32[]{:S(2)}, u32[]{:S(2)}) collective-permute-start(bf16[576,256]{1,0:T(8,128)(2,1)S(1)} %add_convert_fusion.refs_8_), channel_id=1, source_target_pairs={{0,6},{1,7},{2,0},{3,1},{4,2},{5,3},{6,4},{7,5},{8,14},{9,15},{10,... | collective-permute-start | bytes 884744 | tf_op jit(solution)/shard_map/ppermute | solution.py:60
  82.7 11.8 %collective-permute-start.23 = (bf16[576,256]{1,0:T(8,128)(2,1)S(1)}, bf16[576,256]{1,0:T(8,128)(2,1)S(1)}, u32[]{:S(2)}, u32[]{:S(2)}) collective-permute-start(bf16[576,256]{1,0:T(8,128)(2,1)S(1)} %add_convert_fusion.refs_8_), channel_id=1, source_target_pairs={{0,4},{1,5},{2,6},{3,7},{4,0},{5,1},{6,2},{7,3},{8,12},{9,13},{10,... | collective-permute-start | bytes 884744 | tf_op jit(solution)/shard_map/ppermute | solution.py:60
  87.7 12.0 %collective-permute-start.22 = (bf16[576,256]{1,0:T(8,128)(2,1)S(1)}, bf16[576,256]{1,0:T(8,128)(2,1)S(1)}, u32[]{:S(2)}, u32[]{:S(2)}) collective-permute-start(bf16[576,256]{1,0:T(8,128)(2,1)S(1)} %add_convert_fusion.refs_8_), channel_id=1, source_target_pairs={{0,2},{1,3},{2,4},{3,5},{4,6},{5,7},{6,0},{7,1},{8,10},{9,11},{10,... | collective-permute-start | bytes 884744 | tf_op jit(solution)/shard_map/ppermute | solution.py:60
  92.2 7.4 %collective-permute-start.28 = (bf16[576,256]{1,0:T(8,128)(2,1)S(1)}, bf16[576,256]{1,0:T(8,128)(2,1)S(1)}, u32[]{:S(2)}, u32[]{:S(2)}) collective-permute-start(bf16[576,256]{1,0:T(8,128)(2,1)S(1)} %collective-permute-done.15.refs_7_), channel_id=1, source_target_pairs={{0,1},{1,0},{2,3},{3,2},{4,5},{5,4},{6,7},{7,6},{8,9},{9,8},{10,11... | collective-permute-start | bytes 884744 | tf_op jit(solution)/shard_map/ppermute | solution.py:60
  92.2 7.9 %collective-permute-start.27 = (bf16[576,256]{1,0:T(8,128)(2,1)S(1)}, bf16[576,256]{1,0:T(8,128)(2,1)S(1)}, u32[]{:S(2)}, u32[]{:S(2)}) collective-permute-start(bf16[576,256]{1,0:T(8,128)(2,1)S(1)} %collective-permute-done.14.refs_6_), channel_id=1, source_target_pairs={{0,1},{1,0},{2,3},{3,2},{4,5},{5,4},{6,7},{7,6},{8,9},{9,8},{10,11... | collective-permute-start | bytes 884744 | tf_op jit(solution)/shard_map/ppermute | solution.py:60
  93.5 6.7 %collective-permute-start.26 = (bf16[576,256]{1,0:T(8,128)(2,1)S(1)}, bf16[576,256]{1,0:T(8,128)(2,1)S(1)}, u32[]{:S(2)}, u32[]{:S(2)}) collective-permute-start(bf16[576,256]{1,0:T(8,128)(2,1)S(1)} %collective-permute-done.13.refs_5_), channel_id=1, source_target_pairs={{0,1},{1,0},{2,3},{3,2},{4,5},{5,4},{6,7},{7,6},{8,9},{9,8},{10,11... | collective-permute-start | bytes 884744 | tf_op jit(solution)/shard_map/ppermute | solution.py:60
  94.6 5.6 %collective-permute-start.32 = (bf16[576,256]{1,0:T(8,128)(2,1)S(1)}, bf16[576,256]{1,0:T(8,128)(2,1)S(1)}, u32[]{:S(2)}, u32[]{:S(2)}) collective-permute-start(bf16[576,256]{1,0:T(8,128)(2,1)S(1)} %collective-permute-done.24.refs_11_), channel_id=1, source_target_pairs={{0,1},{1,0},{2,3},{3,2},{4,5},{5,4},{6,7},{7,6},{8,9},{9,8},{10,11... | collective-permute-start | bytes 884744 | tf_op jit(solution)/shard_map/ppermute | solution.py:60
  99.6 1.6 %collective-permute-start.31 = (bf16[576,256]{1,0:T(8,128)(2,1)S(1)}, bf16[576,256]{1,0:T(8,128)(2,1)S(1)}, u32[]{:S(2)}, u32[]{:S(2)}) collective-permute-start(bf16[576,256]{1,0:T(8,128)(2,1)S(1)} %collective-permute-done.23.refs_10_), channel_id=1, source_target_pairs={{0,1},{1,0},{2,3},{3,2},{4,5},{5,4},{6,7},{7,6},{8,9},{9,8},{10,11... | collective-permute-start | bytes 884744 | tf_op jit(solution)/shard_map/ppermute | solution.py:60
  99.6 2.0 %collective-permute-start.30 = (bf16[576,256]{1,0:T(8,128)(2,1)S(1)}, bf16[576,256]{1,0:T(8,128)(2,1)S(1)}, u32[]{:S(2)}, u32[]{:S(2)}) collective-permute-start(bf16[576,256]{1,0:T(8,128)(2,1)S(1)} %collective-permute-done.22.refs_9_), channel_id=1, source_target_pairs={{0,1},{1,0},{2,3},{3,2},{4,5},{5,4},{6,7},{7,6},{8,9},{9,8},{10,11... | collective-permute-start | bytes 884744 | tf_op jit(solution)/shard_map/ppermute | solution.py:60
  113.0 16.0 %collective-permute-start.33 = (bf16[112,2048]{1,0:T(8,128)(2,1)S(1)}, bf16[112,2048]{1,0:T(8,128)(2,1)S(1)}, u32[]{:S(2)}, u32[]{:S(2)}) collective-permute-start(bf16[112,2048]{1,0:T(8,128)(2,1)S(1)} %get-tuple-element.31), channel_id=1, source_target_pairs={{32,0},{9,1},{34,2},{11,3},{36,4},{13,5},{38,6},{15,7},{40,8},{17,... | collective-permute-start | bytes 1376264 | tf_op jit(solution)/shard_map/ppermute | solution.py:60
  118.2 12.3 %collective-permute-start.34 = (bf16[112,2048]{1,0:T(8,128)(2,1)S(1)}, bf16[112,2048]{1,0:T(8,128)(2,1)S(1)}, u32[]{:S(2)}, u32[]{:S(2)}) collective-permute-start(bf16[112,2048]{1,0:T(8,128)(2,1)S(1)} %get-tuple-element.32), channel_id=1, source_target_pairs={{16,0},{65,1},{18,2},{67,3},{20,4},{69,5},{22,6},{71,7},{24,8},{73... | collective-permute-start | bytes 1376264 | tf_op jit(solution)/shard_map/ppermute | solution.py:60
  118.2 12.3 %collective-permute-start.35 = (bf16[112,2048]{1,0:T(8,128)(2,1)}, bf16[112,2048]{1,0:T(8,128)(2,1)S(1)}, u32[]{:S(2)}, u32[]{:S(2)}) collective-permute-start(bf16[112,2048]{1,0:T(8,128)(2,1)} %get-tuple-element.33), channel_id=1, source_target_pairs={{96,0},{25,1},{98,2},{27,3},{100,4},{29,5},{102,6},{31,7},{104,8},... | collective-permute-start | bytes 1376264 | tf_op jit(solution)/shard_map/ppermute | solution.py:60

commit v3 on v2

v3 whole, which is shorter than its diff:
```python
import functools
import math

import jax
import jax.numpy as jnp
from jax import lax
from jax.experimental import pallas as pl
from jax.experimental.pallas import tpu as pltpu
from jax.sharding import PartitionSpec as P

C = 7168
R = 2048
CAP = 112
AXES = ("group", "col")

quintic_first = 3.4445
quintic_second = -4.775
quintic_third = 2.0315
margin_square = 2.25
epsilon_norm = 1e-06
learn_rate = 0.02
decay_rate = 0.1

BLOCK = 256
HALF_BLOCK = BLOCK // 2
SAME = [(a, b) for a in range(4) for b in range(a + 1, 4)]
OFF = 14
SLOTS = OFF + 4
TOPS = OFF * BLOCK
CORNERS = TOPS + 4 * HALF_BLOCK
HALF = CORNERS + 2 * HALF_BLOCK
ROUTE = HALF // 2
CHUNK = ROUTE // 4


def pairs(move):
    def place(x, y, z, c):
        return (x % 4) * 32 + (y % 4) * 8 + (z % 4) * 2 + c

    return [
        (place(x, y, z, c), place(*move(x, y, z, c)))
        for x in range(4) for y in range(4) for z in range(4) for c in range(2)
    ]


def flipped(steps):
    return [(b, a) for a, b in steps]


def to_expert(d):
    def move(x, y, z, c):
        along_x = (c == 0) != (d == 2)
        return (x + d, y, z, c) if along_x else (x, y + d, z, c)

    return pairs(move)


RING_P = {k: pairs(lambda x, y, z, c, k=k: (x + k, y - k, z, c)) for k in (1, 2, 3)}
RING_Q = {k: pairs(lambda x, y, z, c, k=k: (x, y, z + k, c)) for k in (1, 2, 3)}
OTHER_CORE = pairs(lambda x, y, z, c: (x, y, z, 1 - c))


def shift(value, steps):
    return lax.ppermute(value, AXES, steps)


def places():
    x, col = lax.axis_index("group"), lax.axis_index("col")
    return col % 2, x, col // 2 % 4, (x + col // 8) % 4


def live_kernel(lengths, momentum, o0, o1, o2, o3, rows, sems):
    home = places()[3]
    outs = (o0, o1, o2, o3)
    experts = [lax.rem(home + d, 4) for d in range(4)]
    loads = [
        pltpu.make_async_copy(momentum.at[experts[d]], rows.at[d], sems.at[d])
        for d in range(4)
    ]
    for load in loads:
        load.start()
    lane = lax.broadcasted_iota(jnp.int32, (1, 4), 1)
    for d in (1, 2, 3, 0):
        loads[d].wait()
        slot = lax.broadcasted_iota(jnp.int32, (CAP, 128), 0)
        keep = slot < jnp.sum(jnp.where(lane == experts[d], lengths[...], 0))
        for at in range(0, R, 128):
            value = rows[d, :, at:at + 128]
            outs[d][:, at:at + 128] = jnp.where(keep, value, jnp.zeros_like(value))


def live(lengths, momentum):
    return pl.pallas_call(
        live_kernel,
        out_shape=[jax.ShapeDtypeStruct((CAP, R), jnp.bfloat16)] * 4,
        in_specs=[
            pl.BlockSpec(memory_space=pltpu.VMEM),
            pl.BlockSpec(memory_space=pltpu.HBM),
        ],
        out_specs=[pl.BlockSpec(memory_space=pltpu.VMEM)] * 4,
        scratch_shapes=[
            pltpu.VMEM((4, CAP, R), jnp.bfloat16),
            pltpu.SemaphoreType.DMA((4,)),
        ],
        compiler_params=pltpu.CompilerParams(vmem_limit_bytes=61 << 20),
        name="live",
    )(lengths, momentum)


def gram_kernel(count, first_stage, last_stage, *refs):
    rows, rest = refs[:count], refs[count:]
    if not first_stage:
        before, rest = rest[0], rest[1:]
    if last_stage:
        outs, rest = rest[:8], rest[8:]
        blocks, out_sems = rest[-2:]
    else:
        total, rest = rest[0], rest[1:]
    x_all, x_turned, in_sems = rest[:3]
    core, p, q, _ = places()
    loads = [
        pltpu.make_async_copy(rows[i], x_all.at[pl.ds(CAP * i, CAP)], in_sems.at[i])
        for i in range(count)
    ]
    for load in loads:
        load.start()
    for load in loads:
        load.wait()

    def columns(at):
        return pl.ds(pl.multiple_of(at * BLOCK, BLOCK), BLOCK)

    for a in range(4):
        x_turned[a * BLOCK:(a + 1) * BLOCK, :] = x_all[:, columns(core * 4 + a)].T
    for slot in range(SLOTS):
        a, b = SAME[slot] if slot < 6 else (slot - OFF, slot - OFF)
        at = core * 4 + b
        if 6 <= slot < OFF:
            s = slot - 6
            a = jnp.where(core == 0, s // 2, 2 + s // 4)
            at = jnp.where(core == 0, 4 + s % 2, s % 4)
        value = jnp.dot(
            x_turned[columns(a), :], x_all[:, columns(at)], preferred_element_type=jnp.float32
        )
        here = slice(slot * BLOCK, (slot + 1) * BLOCK)
        if not first_stage:
            value = value + before[here, :]
        if not last_stage:
            total[here, :] = value
            continue
        value = value.astype(jnp.bfloat16)
        if slot < OFF:
            blocks[here, :] = value
        else:
            top = TOPS + a * HALF_BLOCK
            blocks[top:top + HALF_BLOCK, :] = value[:HALF_BLOCK]
            corner, side = CORNERS + a // 2 * HALF_BLOCK, a % 2 * HALF_BLOCK
            blocks[corner:corner + HALF_BLOCK, side:side + HALF_BLOCK] = value[HALF_BLOCK:, HALF_BLOCK:]
    if not last_stage:
        return
    stores = []
    for route, own in ((0, p), (1, q)):
        for k in range(4):
            start = route * ROUTE + lax.rem(own + k, 4) * CHUNK
            stores.append(pltpu.make_async_copy(
                blocks.at[pl.ds(pl.multiple_of(start, 16), CHUNK)],
                outs[route * 4 + k],
                out_sems.at[route * 4 + k],
            ))
    for store in stores:
        store.start()
    for store in stores:
        store.wait()


def gram(rows, before=None, last=False, weight=1):
    count, depth = len(rows), len(rows) * CAP
    vmem = pl.BlockSpec(memory_space=pltpu.VMEM)
    anywhere = pl.BlockSpec(memory_space=pl.ANY)
    scratch = [
        pltpu.VMEM((depth, R), jnp.bfloat16),
        pltpu.VMEM((4 * BLOCK, depth), jnp.bfloat16),
        pltpu.SemaphoreType.DMA((count,)),
    ]
    if last:
        out_shape = [jax.ShapeDtypeStruct((CHUNK, BLOCK), jnp.bfloat16)] * 8
        scratch += [pltpu.VMEM((HALF, BLOCK), jnp.bfloat16), pltpu.SemaphoreType.DMA((8,))]
    else:
        out_shape = jax.ShapeDtypeStruct((SLOTS * BLOCK, BLOCK), jnp.float32)
    operands = list(rows) + ([] if before is None else [before])
    return pl.pallas_call(
        functools.partial(gram_kernel, count, before is None, last),
        out_shape=out_shape,
        in_specs=[anywhere] * count + [vmem] * (before is not None),
        out_specs=[anywhere] * 8 if last else vmem,
        scratch_shapes=scratch,
        input_output_aliases={count: 0} if before is not None and not last else {},
        compiler_params=pltpu.CompilerParams(vmem_limit_bytes=16 << 20),
        cost_estimate=pl.CostEstimate(
            flops=2 * SLOTS * BLOCK * BLOCK * depth * weight,
            bytes_accessed=depth * R * 2 + 2 * SLOTS * BLOCK * BLOCK * 4,
            transcendentals=0,
        ),
        name="gram",
    )(*operands)


def stored_at(i, j):
    if i // 4 == j // 4:
        a, b = i % 4, j % 4
        return i // 4, SAME.index((min(a, b), max(a, b))), a > b
    low, high = min(i, j), max(i, j)
    if high < 6:
        return 0, 6 + 2 * low + (high - 4), i > j
    return 1, 6 + 4 * (high - 6) + low, i < j


def update_kernel(*refs):
    rows, chunks, outs = refs[:4], refs[4:18], refs[18:22]
    x_all, blocks, diagonal, first, first_round, in_sems, chunk_sems = refs[22:]
    core, p, q, _ = places()
    loads = [
        pltpu.make_async_copy(rows[i], x_all.at[pl.ds(CAP * i, CAP)], in_sems.at[i])
        for i in range(4)
    ]
    for side in range(2):
        half = core if side == 0 else 1 - core
        for route, own in ((0, p), (1, q)):
            for k in range(4):
                if side == 0:
                    chunk = chunks[route * 4 + k]
                elif k in (0, 3):
                    chunk = chunks[8 + route * 3].at[pl.ds(k // 3 * CHUNK, CHUNK)]
                else:
                    chunk = chunks[8 + route * 3 + 3 - k]
                number = half * 8 + route * 4 + lax.rem(own + 4 - k, 4)
                loads.append(pltpu.make_async_copy(
                    chunk,
                    blocks.at[pl.ds(pl.multiple_of(number * CHUNK, 16), CHUNK)],
                    chunk_sems.at[number],
                ))
    for load in loads:
        load.start()

    def block(half, slot):
        start = half * HALF + slot * BLOCK
        return blocks[start:start + BLOCK, :]

    def times_gram(left, j):
        total = None
        for i in range(8):
            if i == j:
                part, turned = diagonal[j * BLOCK:(j + 1) * BLOCK, :], False
            else:
                half, slot, turned = stored_at(i, j)
                part = block(half, slot)
            term = lax.dot_general(
                left[:, i * BLOCK:(i + 1) * BLOCK],
                part,
                (((1,), (1 if turned else 0,)), ((), ())),
                preferred_element_type=jnp.float32,
            )
            total = term if total is None else total + term
        return total

    def squared(value):
        value = value.astype(jnp.float32)
        return value * value

    twice = jnp.zeros((16, BLOCK), jnp.float32)
    once = jnp.zeros((HALF_BLOCK, HALF_BLOCK), jnp.float32)
    for number in range(16):
        here = blocks.at[pl.ds(number * CHUNK, CHUNK)]
        pltpu.make_async_copy(here, here, chunk_sems.at[number]).wait()
        for at in range(number * CHUNK, (number + 1) * CHUNK, 16):
            if at % HALF < TOPS:
                twice += squared(blocks[at:at + 16, :])
    for i in range(8):
        half, a = i // 4, i % 4
        start = half * HALF + TOPS + a * HALF_BLOCK
        corner, side = half * HALF + CORNERS + a // 2 * HALF_BLOCK, a % 2 * HALF_BLOCK
        top = blocks[start:start + HALF_BLOCK, :]
        last = blocks[corner:corner + HALF_BLOCK, side:side + HALF_BLOCK]
        diagonal[i * BLOCK:i * BLOCK + HALF_BLOCK, :] = top
        diagonal[i * BLOCK + HALF_BLOCK:(i + 1) * BLOCK, :HALF_BLOCK] = top[:, HALF_BLOCK:].T
        diagonal[i * BLOCK + HALF_BLOCK:(i + 1) * BLOCK, HALF_BLOCK:] = last
        once += squared(top[:, :HALF_BLOCK]) + squared(last) + 2.0 * squared(top[:, HALF_BLOCK:])
    total = 2.0 * jnp.sum(twice, axis=(0, 1), keepdims=True) + jnp.sum(once, axis=(0, 1), keepdims=True)
    norm_scale = margin_square / (jnp.sqrt(total) + epsilon_norm)
    root = jnp.sqrt(norm_scale)
    for load in loads[:4]:
        load.wait()

    for j in range(8):
        at = slice(j * BLOCK, (j + 1) * BLOCK)
        value = times_gram(x_all, j)
        first[:, at] = value
        first_round[:, at] = value.astype(jnp.bfloat16)
    for j in range(8):
        at = slice(j * BLOCK, (j + 1) * BLOCK)
        second = times_gram(first_round, j)
        scaled = (x_all[:, at].astype(jnp.float32) * root).astype(jnp.bfloat16)
        combined = (
            quintic_first * scaled.astype(jnp.float32)
            + (quintic_second * norm_scale * root) * first[:, at]
            + (quintic_third * norm_scale * norm_scale * root) * second
        )
        value = (math.sqrt(C) * combined).astype(jnp.bfloat16)
        for d in range(4):
            outs[d][:, at] = value[CAP * d:CAP * (d + 1)]


def update(rows, chunks):
    anywhere = pl.BlockSpec(memory_space=pl.ANY)
    return pl.pallas_call(
        update_kernel,
        out_shape=[jax.ShapeDtypeStruct((CAP, R), jnp.bfloat16)] * 4,
        in_specs=[anywhere] * 18,
        out_specs=[pl.BlockSpec(memory_space=pltpu.VMEM)] * 4,
        scratch_shapes=[
            pltpu.VMEM((4 * CAP, R), jnp.bfloat16),
            pltpu.VMEM((2 * HALF, BLOCK), jnp.bfloat16),
            pltpu.VMEM((R, BLOCK), jnp.bfloat16),
            pltpu.VMEM((4 * CAP, R), jnp.float32),
            pltpu.VMEM((4 * CAP, R), jnp.bfloat16),
            pltpu.SemaphoreType.DMA((4,)),
            pltpu.SemaphoreType.DMA((16,)),
        ],
        compiler_params=pltpu.CompilerParams(vmem_limit_bytes=24 << 20),
        name="update",
    )(*rows, *chunks)


def apply_kernel(d, value, weight, *refs):
    out, new_weight, rows, weights, in_sems, out_sems = refs[-6:]
    expert = lax.rem(places()[3] + d, 4)
    parts = [slice(at, at + R // 4) for at in range(0, R, R // 4)]
    loads = [
        pltpu.make_async_copy(weight.at[expert, :, part], weights.at[:, part], in_sems.at[i])
        for i, part in enumerate(parts)
    ]
    for load in loads:
        load.start()
    stores = [pltpu.make_async_copy(value, out.at[expert], out_sems.at[4])]
    stores[0].start()
    for i, part in enumerate(parts):
        loads[i].wait()
        rows[:, part] = (
            weights[:, part] * (1.0 - learn_rate * decay_rate)
            - learn_rate * value[:, part].astype(jnp.float32)
        )
        stores.append(pltpu.make_async_copy(
            rows.at[:, part], new_weight.at[expert, :, part], out_sems.at[i]
        ))
        stores[-1].start()
    for store in stores:
        store.wait()


def apply(d, value, weight, outs):
    anywhere = pl.BlockSpec(memory_space=pltpu.HBM)
    return pl.pallas_call(
        functools.partial(apply_kernel, d),
        out_shape=[
            jax.ShapeDtypeStruct((4, CAP, R), jnp.bfloat16),
            jax.ShapeDtypeStruct((4, CAP, R), jnp.float32),
        ],
        in_specs=[pl.BlockSpec(memory_space=pltpu.VMEM), anywhere] + [anywhere] * len(outs),
        out_specs=[anywhere, anywhere],
        scratch_shapes=[
            pltpu.VMEM((CAP, R), jnp.float32),
            pltpu.VMEM((CAP, R), jnp.float32),
            pltpu.SemaphoreType.DMA((4,)),
            pltpu.SemaphoreType.DMA((5,)),
        ],
        input_output_aliases={2: 0, 3: 1} if outs else {},
        compiler_params=pltpu.CompilerParams(vmem_limit_bytes=8 << 20),
        cost_estimate=pl.CostEstimate(flops=CAP * R * 3, bytes_accessed=CAP * R * 12, transcendentals=0),
        name="apply",
    )(value, weight, *outs)


def summed(parts):
    total = None
    for part in parts:
        part = part.astype(jnp.float32)
        total = part if total is None else total + part
    return total.astype(jnp.bfloat16)


def on_device(momentum, lengths, weight):
    routes = {d: to_expert(d) for d in (1, 2, 3)}
    rows = live(lengths.reshape(1, 4), momentum)
    rows = [rows[0]] + [shift(rows[d], routes[d]) for d in (1, 2, 3)]
    other_rows = [shift(part, OTHER_CORE) for part in rows]

    total = gram([rows[0]])
    total = gram(rows[1:], total, weight=40)
    parts = gram(other_rows, total, last=True)
    rings = (RING_P, RING_Q)
    chunks = []
    for route in range(2):
        mine = parts[route * 4:route * 4 + 4]
        chunks.append([mine[0]] + [shift(mine[k], rings[route][k]) for k in (2, 1, 3)])
    chunks = [summed(got) for got in chunks]
    chunks = [
        [chunks[route]] + [shift(chunks[route], rings[1 - route][k]) for k in (2, 1, 3)]
        for route in range(2)
    ]
    chunks = [summed(got) for got in chunks]
    mine, others = [], []
    for route in range(2):
        got = [chunks[route]] + [shift(chunks[route], rings[route][k]) for k in (1, 2, 3)]
        mine += got
        others += [
            shift(part, OTHER_CORE)
            for part in (jnp.concatenate([got[0], got[3]], 0), got[2], got[1])
        ]

    updates = update(rows, mine + others)
    outs = apply(0, updates[0], weight, [])
    for d in (1, 2, 3):
        outs = apply(d, shift(updates[d], flipped(routes[d])), weight, outs)
    return tuple(outs)


def solution(mesh):
    placed = (
        P(None, ("group", "col"), None),
        P(None, ("group", "col")),
        P(None, ("group", "col"), None),
    )
    return jax.shard_map(
        on_device,
        mesh=mesh,
        in_specs=placed,
        out_specs=(P(None, ("group", "col"), None), P(None, ("group", "col"), None)),
        check_vma=False,
    )
```

time: 134 us -> 123 us (0.918)
  waiting for transfers between devices: 50.1 us -> 41 us
  starting transfers between devices: 57.2 us -> 51.5 us
  Pallas kernels: 22.6 us -> 26.6 us
    ppermute x36 -> x34, waiting for transfers between devices: 50.1 us -> 41 us  [shift(): return lax.ppermute(value, AXES, steps)]
    ppermute x36 -> x34, starting transfers between devices: 57.2 us -> 51.5 us  [shift(): return lax.ppermute(value, AXES, steps)]
    pallas_call x2 -> x7, Pallas kernels: 9.12 us -> 12.2 us  [the longest x3 7.07 us: gram(): pl.pallas_call(functools.partial(gram_kernel, count, before is None, last...]
    pallas_call x1, Pallas kernels: 2.14 us -> 3.8 us  [live(): pl.pallas_call(live_kernel, out_shape=[jax.ShapeDtypeStruct((CAP, R), jnp...]
  transfers between devices with their start and end apart: 36 -> 34, of which waited for: 22 -> 20; matrix products, arithmetic and copies ran while one was open for 0% -> 1% of each run, Pallas kernels for 0% -> 6%
where the time goes in v3:
time: 123 us; the launch traced here: 122 us
  starting transfers between devices  51.5 us (42%)
  waiting for transfers between devices  41 us (33%)
  Pallas kernels  26.6 us (22%)
    ppermute x34, starting transfers between devices, shift(): return lax.ppermute(value, AXES, steps)  51.5 us
    ppermute x34, waiting for transfers between devices, shift(): return lax.ppermute(value, AXES, steps)  41 us
    pallas_call x1, Pallas kernels, update(): pl.pallas_call(update_kernel, out_shape=[jax.ShapeDtypeStruct((CAP, R), j...  10.6 us
    pallas_call x3, Pallas kernels, gram(): pl.pallas_call(functools.partial(gram_kernel, count, before is None, last...  7.07 us
    pallas_call x4, Pallas kernels, apply(): pl.pallas_call(functools.partial(apply_kernel, d), out_shape=[jax.ShapeDt...  5.15 us
    pallas_call x1, Pallas kernels, live(): pl.pallas_call(live_kernel, out_shape=[jax.ShapeDtypeStruct((CAP, R), jnp...  3.8 us
  transfers between devices with their start and end apart: 34, of which 20 were waited for; matrix products, arithmetic and copies ran while one was open for 1% of the time, Pallas kernels for 6%

profile of v3, /device:TPU:0, one launch (start us, length us, event | category | flops | bytes accessed | tf_op | source)
XLA Modules:
  0.0 121.8 jit_solution(13538633546893464692)
XLA Ops:
  0.6 3.8 %live.1 = (bf16[112,2048]{1,0:T(8,128)(2,1)}, bf16[112,2048]{1,0:T(8,128)(2,1)}, bf16[112,2048]{1,0:T(8,128)(2,1)}, bf16[112,2048]{1,0:T(8,128)(2,1)}) custom-call(s32[1,4]{1,0:T(1,128)} %bitcast.1, bf16[4,112,2048]{2,1,0:T(8,128)(2,1)} %momentum.1), custom_call_target="tpu_custom_call" | custom-call | tf_op jit(solution)/shard_map/live/pallas_call | solution.py:93
  4.4 1.6 %collective-permute-start = (bf16[112,2048]{1,0:T(8,128)(2,1)}, bf16[112,2048]{1,0:T(8,128)(2,1)S(1)}, u32[]{:S(2)}, u32[]{:S(2)}) collective-permute-start(bf16[112,2048]{1,0:T(8,128)(2,1)} %get-tuple-element.25), channel_id=1, source_target_pairs={{0,32},{1,9},{2,34},{3,11},{4,36},{5,13},{6,38},{7,15},{8,40},{9,1... | collective-permute-start | bytes 1376264 | tf_op jit(solution)/shard_map/ppermute | solution.py:64
  6.1 3.2 %collective-permute-start.1 = (bf16[112,2048]{1,0:T(8,128)(2,1)}, bf16[112,2048]{1,0:T(8,128)(2,1)S(1)}, u32[]{:S(2)}, u32[]{:S(2)}) collective-permute-start(bf16[112,2048]{1,0:T(8,128)(2,1)} %get-tuple-element.26), channel_id=1, source_target_pairs={{0,16},{1,65},{2,18},{3,67},{4,20},{5,69},{6,22},{7,71},{8,24},{9,... | collective-permute-start | bytes 1376264 | tf_op jit(solution)/shard_map/ppermute | solution.py:64
  9.3 1.7 %collective-permute-start.2 = (bf16[112,2048]{1,0:T(8,128)(2,1)}, bf16[112,2048]{1,0:T(8,128)(2,1)S(1)}, u32[]{:S(2)}, u32[]{:S(2)}) collective-permute-start(bf16[112,2048]{1,0:T(8,128)(2,1)} %get-tuple-element.27), channel_id=1, source_target_pairs={{0,96},{1,25},{2,98},{3,27},{4,100},{5,29},{6,102},{7,31},{8,104},... | collective-permute-start | bytes 1376264 | tf_op jit(solution)/shard_map/ppermute | solution.py:64
  11.0 1.0 copy-done.1
  12.0 1.1 gram.3.refs_3_
  13.1 6.1 %collective-permute-done.refs_0_.refs_1_ = bf16[112,2048]{1,0:T(8,128)(2,1)S(1)} collective-permute-done((bf16[112,2048]{1,0:T(8,128)(2,1)}, bf16[112,2048]{1,0:T(8,128)(2,1)S(1)}, u32[]{:S(2)}, u32[]{:S(2)}) %collective-permute-start) | collective-permute-done | bytes 458784 | tf_op jit(solution)/shard_map/ppermute | solution.py:64
  19.9 0.7 collective-permute-start.6
  20.7 2.9 %gram.4.refs_4_ = f32[4608,256]{1,0:T(8,128)S(1)} custom-call(bf16[112,2048]{1,0:T(8,128)(2,1)S(1)} %collective-permute-done.refs_0_.refs_1_, bf16[112,2048]{1,0:T(8,128)(2,1)S(1)} %collective-permute-done.1.refs_1_.refs_2_, bf16[112,2048]{1,0:T(8,128)(2,1)S(1)} %collective-permute-done.2.refs_2_.refs_3_, ...), custom_call_target="tpu_custom_call", output_to_operand_aliasing={{}: (3, {})} | custom-call | flops 31708938240 | bytes 10813440 | tf_op jit(solution)/shard_map/gram/pallas_call | solution.py:191
  23.6 3.1 %gram.5 = (bf16[544,256]{1,0:T(8,128)(2,1)S(1)}, bf16[544,256]{1,0:T(8,128)(2,1)S(1)}, bf16[544,256]{1,0:T(8,128)(2,1)S(1)}, bf16[544,256]{1,0:T(8,128)(2,1)S(1)...) custom-call(bf16[112,2048]{1,0:T(8,128)(2,1)S(1)} %collective-permut, ...), custom_call_target="tpu_custom_call" | custom-call | flops 1056964608 | bytes 11272192 | tf_op jit(solution)/shard_map/gram/pallas_call | solution.py:191
  26.7 4.0 %collective-permute-start.16 = (bf16[544,256]{1,0:T(8,128)(2,1)S(1)}, bf16[544,256]{1,0:T(8,128)(2,1)S(1)}, u32[]{:S(2)}, u32[]{:S(2)}) collective-permute-start(bf16[544,256]{1,0:T(8,128)(2,1)S(1)} %get-tuple-element.33), channel_id=1, source_target_pairs={{0,4},{1,5},{2,6},{3,7},{4,0},{5,1},{6,2},{7,3},{8,12},{9,13},{10,... | collective-permute-start | bytes 835592 | tf_op jit(solution)/shard_map/ppermute | solution.py:64
  30.7 1.0 collective-permute-start.17
  31.7 2.2 %collective-permute-start.18 = (bf16[544,256]{1,0:T(8,128)(2,1)S(1)}, bf16[544,256]{1,0:T(8,128)(2,1)S(1)}, u32[]{:S(2)}, u32[]{:S(2)}) collective-permute-start(bf16[544,256]{1,0:T(8,128)(2,1)S(1)} %get-tuple-element.35), channel_id=1, source_target_pairs={{0,6},{1,7},{2,0},{3,1},{4,2},{5,3},{6,4},{7,5},{8,14},{9,15},{10,... | collective-permute-start | bytes 835592 | tf_op jit(solution)/shard_map/ppermute | solution.py:64
  33.9 3.6 %collective-permute-start.7 = (bf16[544,256]{1,0:T(8,128)(2,1)S(1)}, bf16[544,256]{1,0:T(8,128)(2,1)S(1)}, u32[]{:S(2)}, u32[]{:S(2)}) collective-permute-start(bf16[544,256]{1,0:T(8,128)(2,1)S(1)} %get-tuple-element.29), channel_id=1, source_target_pairs={{0,80},{1,81},{2,82},{3,83},{4,84},{5,85},{6,86},{7,87},{8,88},{9,... | collective-permute-start | bytes 835592 | tf_op jit(solution)/shard_map/ppermute | solution.py:64
  37.5 3.1 %collective-permute-start.8 = (bf16[544,256]{1,0:T(8,128)(2,1)S(1)}, bf16[544,256]{1,0:T(8,128)(2,1)S(1)}, u32[]{:S(2)}, u32[]{:S(2)}) collective-permute-start(bf16[544,256]{1,0:T(8,128)(2,1)S(1)} %get-tuple-element.30), channel_id=1, source_target_pairs={{0,56},{1,57},{2,58},{3,59},{4,60},{5,61},{6,62},{7,63},{8,32},{9,... | collective-permute-start | bytes 835592 | tf_op jit(solution)/shard_map/ppermute | solution.py:64
  40.6 1.3 %collective-permute-start.9 = (bf16[544,256]{1,0:T(8,128)(2,1)S(1)}, bf16[544,256]{1,0:T(8,128)(2,1)S(1)}, u32[]{:S(2)}, u32[]{:S(2)}) collective-permute-start(bf16[544,256]{1,0:T(8,128)(2,1)S(1)} %get-tuple-element.31), channel_id=1, source_target_pairs={{0,104},{1,105},{2,106},{3,107},{4,108},{5,109},{6,110},{7,111},{8... | collective-permute-start | bytes 835592 | tf_op jit(solution)/shard_map/ppermute | solution.py:64
  41.9 1.6 %collective-permute-done.17 = bf16[544,256]{1,0:T(8,128)(2,1)S(1)} collective-permute-done((bf16[544,256]{1,0:T(8,128)(2,1)S(1)}, bf16[544,256]{1,0:T(8,128)(2,1)S(1)}, u32[]{:S(2)}, u32[]{:S(2)}) %collective-permute-start.17) | collective-permute-done | bytes 278560 | tf_op jit(solution)/shard_map/ppermute | solution.py:64
  43.5 0.8 collective-permute-done.18
  44.4 4.2 %collective-permute-start.19 = (bf16[544,256]{1,0:T(8,128)(2,1)S(1)}, bf16[544,256]{1,0:T(8,128)(2,1)S(1)}, u32[]{:S(2)}, u32[]{:S(2)}) collective-permute-start(bf16[544,256]{1,0:T(8,128)(2,1)S(1)} %add_convert_fusion.1), channel_id=1, source_target_pairs={{0,80},{1,81},{2,82},{3,83},{4,84},{5,85},{6,86},{7,87},{8,88},{9,... | collective-permute-start | bytes 835592 | tf_op jit(solution)/shard_map/ppermute | solution.py:64
  48.6 2.6 %collective-permute-start.20 = (bf16[544,256]{1,0:T(8,128)(2,1)S(1)}, bf16[544,256]{1,0:T(8,128)(2,1)S(1)}, u32[]{:S(2)}, u32[]{:S(2)}) collective-permute-start(bf16[544,256]{1,0:T(8,128)(2,1)S(1)} %add_convert_fusion.1), channel_id=1, source_target_pairs={{0,56},{1,57},{2,58},{3,59},{4,60},{5,61},{6,62},{7,63},{8,32},{9,... | collective-permute-start | bytes 835592 | tf_op jit(solution)/shard_map/ppermute | solution.py:64
  51.2 1.8 %collective-permute-start.21 = (bf16[544,256]{1,0:T(8,128)(2,1)S(1)}, bf16[544,256]{1,0:T(8,128)(2,1)S(1)}, u32[]{:S(2)}, u32[]{:S(2)}) collective-permute-start(bf16[544,256]{1,0:T(8,128)(2,1)S(1)} %add_convert_fusion.1), channel_id=1, source_target_pairs={{0,104},{1,105},{2,106},{3,107},{4,108},{5,109},{6,110},{7,111},{8... | collective-permute-start | bytes 835592 | tf_op jit(solution)/shard_map/ppermute | solution.py:64
  53.0 0.9 collective-permute-done.8
  54.1 0.9 collective-permute-start.10
  55.0 1.5 %collective-permute-start.11 = (bf16[544,256]{1,0:T(8,128)(2,1)S(1)}, bf16[544,256]{1,0:T(8,128)(2,1)S(1)}, u32[]{:S(2)}, u32[]{:S(2)}) collective-permute-start(bf16[544,256]{1,0:T(8,128)(2,1)S(1)} %add_convert_fusion.3), channel_id=1, source_target_pairs={{0,2},{1,3},{2,4},{3,5},{4,6},{5,7},{6,0},{7,1},{8,10},{9,11},{10,... | collective-permute-start | bytes 835592 | tf_op jit(solution)/shard_map/ppermute | solution.py:64
  56.4 7.5 %collective-permute-done.19 = bf16[544,256]{1,0:T(8,128)(2,1)S(1)} collective-permute-done((bf16[544,256]{1,0:T(8,128)(2,1)S(1)}, bf16[544,256]{1,0:T(8,128)(2,1)S(1)}, u32[]{:S(2)}, u32[]{:S(2)}) %collective-permute-start.19) | collective-permute-done | bytes 278560 | tf_op jit(solution)/shard_map/ppermute | solution.py:64
  64.4 2.4 %collective-permute-done.21 = bf16[544,256]{1,0:T(8,128)(2,1)S(1)} collective-permute-done((bf16[544,256]{1,0:T(8,128)(2,1)S(1)}, bf16[544,256]{1,0:T(8,128)(2,1)S(1)}, u32[]{:S(2)}, u32[]{:S(2)}) %collective-permute-start.21) | collective-permute-done | bytes 278560 | tf_op jit(solution)/shard_map/ppermute | solution.py:64
  67.0 1.2 %collective-permute-start.24 = (bf16[544,256]{1,0:T(8,128)(2,1)S(1)}, bf16[544,256]{1,0:T(8,128)(2,1)S(1)}, u32[]{:S(2)}, u32[]{:S(2)}) collective-permute-start(bf16[544,256]{1,0:T(8,128)(2,1)S(1)} %add_convert_fusion.refs_8_), channel_id=1, source_target_pairs={{0,6},{1,7},{2,0},{3,1},{4,2},{5,3},{6,4},{7,5},{8,14},{9,15},{10,... | collective-permute-start | bytes 835592 | tf_op jit(solution)/shard_map/ppermute | solution.py:64
  68.2 1.5 %collective-permute-done.11 = bf16[544,256]{1,0:T(8,128)(2,1)S(1)} collective-permute-done((bf16[544,256]{1,0:T(8,128)(2,1)S(1)}, bf16[544,256]{1,0:T(8,128)(2,1)S(1)}, u32[]{:S(2)}, u32[]{:S(2)}) %collective-permute-start.11) | collective-permute-done | bytes 278560 | tf_op jit(solution)/shard_map/ppermute | solution.py:64
  69.7 2.7 %collective-permute-done.12 = bf16[544,256]{1,0:T(8,128)(2,1)S(1)} collective-permute-done((bf16[544,256]{1,0:T(8,128)(2,1)S(1)}, bf16[544,256]{1,0:T(8,128)(2,1)S(1)}, u32[]{:S(2)}, u32[]{:S(2)}) %collective-permute-start.12) | collective-permute-done | bytes 278560 | tf_op jit(solution)/shard_map/ppermute | solution.py:64
  73.0 1.8 %collective-permute-start.22 = (bf16[544,256]{1,0:T(8,128)(2,1)S(1)}, bf16[544,256]{1,0:T(8,128)(2,1)S(1)}, u32[]{:S(2)}, u32[]{:S(2)}) collective-permute-start(bf16[544,256]{1,0:T(8,128)(2,1)S(1)} %add_convert_fusion.refs_8_), channel_id=1, source_target_pairs={{0,2},{1,3},{2,4},{3,5},{4,6},{5,7},{6,0},{7,1},{8,10},{9,11},{10,... | collective-permute-start | bytes 835592 | tf_op jit(solution)/shard_map/ppermute | solution.py:64
  74.8 4.7 %collective-permute-start.14 = (bf16[544,256]{1,0:T(8,128)(2,1)S(1)}, bf16[544,256]{1,0:T(8,128)(2,1)S(1)}, u32[]{:S(2)}, u32[]{:S(2)}) collective-permute-start(bf16[544,256]{1,0:T(8,128)(2,1)S(1)} %add_convert_fusion.2.refs_4_), channel_id=1, source_target_pairs={{0,80},{1,81},{2,82},{3,83},{4,84},{5,85},{6,86},{7,87},{8,88},{9,... | collective-permute-start | bytes 835592 | tf_op jit(solution)/shard_map/ppermute | solution.py:64
  79.5 2.9 %collective-permute-start.13 = (bf16[544,256]{1,0:T(8,128)(2,1)S(1)}, bf16[544,256]{1,0:T(8,128)(2,1)S(1)}, u32[]{:S(2)}, u32[]{:S(2)}) collective-permute-start(bf16[544,256]{1,0:T(8,128)(2,1)S(1)} %add_convert_fusion.2.refs_4_), channel_id=1, source_target_pairs={{0,56},{1,57},{2,58},{3,59},{4,60},{5,61},{6,62},{7,63},{8,32},{9,... | collective-permute-start | bytes 835592 | tf_op jit(solution)/shard_map/ppermute | solution.py:64
  82.4 2.7 %collective-permute-done.15.refs_7_ = bf16[544,256]{1,0:T(8,128)(2,1)S(1)} collective-permute-done((bf16[544,256]{1,0:T(8,128)(2,1)S(1)}, bf16[544,256]{1,0:T(8,128)(2,1)S(1)}, u32[]{:S(2)}, u32[]{:S(2)}) %collective-permute-start.15) | collective-permute-done | bytes 278560 | tf_op jit(solution)/shard_map/ppermute | solution.py:64
  85.2 0.5 collective-permute-start.29
  85.7 2.3 %collective-permute-done.22.refs_9_ = bf16[544,256]{1,0:T(8,128)(2,1)S(1)} collective-permute-done((bf16[544,256]{1,0:T(8,128)(2,1)S(1)}, bf16[544,256]{1,0:T(8,128)(2,1)S(1)}, u32[]{:S(2)}, u32[]{:S(2)}) %collective-permute-start.22) | collective-permute-done | bytes 278560 | tf_op jit(solution)/shard_map/ppermute | solution.py:64
  88.1 0.5 collective-permute-start.30
  88.6 0.9 collective-permute-done.13.refs_5_
  89.4 0.5 collective-permute-start.27
  90.4 0.6 collective-permute-done.26.refs_13_
  91.4 10.6 %update.1 = (bf16[112,2048]{1,0:T(8,128)(2,1)S(1)}, bf16[112,2048]{1,0:T(8,128)(2,1)S(1)}, bf16[112,2048]{1,0:T(8,128)(2,1)S(1)}, bf16[112,2048]{1,0:T(8,128)(2,1)S(1)}) custom-call(bf16[112,2048]{1,0:T(8,128)(2,1)S(1)} %copy-done.2, bf16[112,2048]{1,0:T(8,128)(2,1)S(1)} %collective-permute-done.refs_0_.refs_1_, ...), custom_call_target="tpu_custom_call" | custom-call | tf_op jit(solution)/shard_map/update/pallas_call | solution.py:315
  102.0 2.0 %collective-permute-start.33 = (bf16[112,2048]{1,0:T(8,128)(2,1)S(1)}, bf16[112,2048]{1,0:T(8,128)(2,1)S(1)}, u32[]{:S(2)}, u32[]{:S(2)}) collective-permute-start(bf16[112,2048]{1,0:T(8,128)(2,1)S(1)} %get-tuple-element.38), channel_id=1, source_target_pairs={{32,0},{9,1},{34,2},{11,3},{36,4},{13,5},{38,6},{15,7},{40,8},{17,... | collective-permute-start | bytes 1376264 | tf_op jit(solution)/shard_map/ppermute | solution.py:64
  104.0 2.8 %collective-permute-start.32 = (bf16[112,2048]{1,0:T(8,128)(2,1)S(1)}, bf16[112,2048]{1,0:T(8,128)(2,1)S(1)}, u32[]{:S(2)}, u32[]{:S(2)}) collective-permute-start(bf16[112,2048]{1,0:T(8,128)(2,1)S(1)} %get-tuple-element.37), channel_id=1, source_target_pairs={{16,0},{65,1},{18,2},{67,3},{20,4},{69,5},{22,6},{71,7},{24,8},{73... | collective-permute-start | bytes 1376264 | tf_op jit(solution)/shard_map/ppermute | solution.py:64
  106.8 1.3 %apply.4 = (bf16[4,112,2048]{2,1,0:T(8,128)(2,1)}, f32[4,112,2048]{2,1,0:T(8,128)}) custom-call(bf16[112,2048]{1,0:T(8,128)(2,1)S(1)} %get-tuple-element.39.value, f32[4,112,2048]{2,1,0:T(8,128)S(1)} %copy-done), custom_call_target="tpu_custom_call" | custom-call | flops 688128 | bytes 2752512 | tf_op jit(solution)/shard_map/apply/pallas_call | solution.py:362
  108.1 6.9 %collective-permute-done.33.value = bf16[112,2048]{1,0:T(8,128)(2,1)S(1)} collective-permute-done((bf16[112,2048]{1,0:T(8,128)(2,1)S(1)}, bf16[112,2048]{1,0:T(8,128)(2,1)S(1)}, u32[]{:S(2)}, u32[]{:S(2)}) %collective-permute-start.33) | collective-permute-done | bytes 458784 | tf_op jit(solution)/shard_map/ppermute | solution.py:64
  115.0 1.3 %apply.5 = (bf16[4,112,2048]{2,1,0:T(8,128)(2,1)}, f32[4,112,2048]{2,1,0:T(8,128)}) custom-call(bf16[112,2048]{1,0:T(8,128)(2,1)S(1)} %collective-permute-done.33.value, f32[4,112,2048]{2,1,0:T(8,128)S(1)} %copy-done, bf16[4,112,2048]{2,1,0:T(8,128)(2,1)} %get-tuple-element.40.refs_0_, ...), custom_call_target="tpu_custom_call", output_to_operand_aliasing={{0}: (2, {}), {1}: (3, {})} | custom-call | flops 688128 | bytes 2752512 | tf_op jit(solution)/shard_map/apply/pallas_call | solution.py:362
  116.3 2.6 %collective-permute-done.32.value = bf16[112,2048]{1,0:T(8,128)(2,1)S(1)} collective-permute-done((bf16[112,2048]{1,0:T(8,128)(2,1)S(1)}, bf16[112,2048]{1,0:T(8,128)(2,1)S(1)}, u32[]{:S(2)}, u32[]{:S(2)}) %collective-permute-start.32) | collective-permute-done | bytes 458784 | tf_op jit(solution)/shard_map/ppermute | solution.py:64
  118.9 1.3 %apply.6 = (bf16[4,112,2048]{2,1,0:T(8,128)(2,1)}, f32[4,112,2048]{2,1,0:T(8,128)}) custom-call(bf16[112,2048]{1,0:T(8,128)(2,1)S(1)} %collective-permute-done.32.value, f32[4,112,2048]{2,1,0:T(8,128)S(1)} %copy-done, bf16[4,112,2048]{2,1,0:T(8,128)(2,1)} %get-tuple-element.42.refs_0_, ...), custom_call_target="tpu_custom_call", output_to_operand_aliasing={{0}: (2, {}), {1}: (3, {})} | custom-call | flops 688128 | bytes 2752512 | tf_op jit(solution)/shard_map/apply/pallas_call | solution.py:362
  120.3 1.3 %apply.7 = (bf16[4,112,2048]{2,1,0:T(8,128)(2,1)}, f32[4,112,2048]{2,1,0:T(8,128)}) custom-call(bf16[112,2048]{1,0:T(8,128)(2,1)S(1)} %collective-permute-done.31.value, f32[4,112,2048]{2,1,0:T(8,128)S(1)} %copy-done, bf16[4,112,2048]{2,1,0:T(8,128)(2,1)} %get-tuple-element.44.refs_0_, ...), custom_call_target="tpu_custom_call", output_to_operand_aliasing={{0}: (2, {}), {1}: (3, {})} | custom-call | flops 688128 | bytes 2752512 | tf_op jit(solution)/shard_map/apply/pallas_call | solution.py:362
  (41 shorter events, 3.3 us)
Async XLA Ops:
  4.4 14.8 %collective-permute-start = (bf16[112,2048]{1,0:T(8,128)(2,1)}, bf16[112,2048]{1,0:T(8,128)(2,1)S(1)}, u32[]{:S(2)}, u32[]{:S(2)}) collective-permute-start(bf16[112,2048]{1,0:T(8,128)(2,1)} %get-tuple-element.25), channel_id=1, source_target_pairs={{0,32},{1,9},{2,34},{3,11},{4,36},{5,13},{6,38},{7,15},{8,40},{9,1... | collective-permute-start | bytes 1376264 | tf_op jit(solution)/shard_map/ppermute | solution.py:64
  6.1 13.4 %collective-permute-start.1 = (bf16[112,2048]{1,0:T(8,128)(2,1)}, bf16[112,2048]{1,0:T(8,128)(2,1)S(1)}, u32[]{:S(2)}, u32[]{:S(2)}) collective-permute-start(bf16[112,2048]{1,0:T(8,128)(2,1)} %get-tuple-element.26), channel_id=1, source_target_pairs={{0,16},{1,65},{2,18},{3,67},{4,20},{5,69},{6,22},{7,71},{8,24},{9,... | collective-permute-start | bytes 1376264 | tf_op jit(solution)/shard_map/ppermute | solution.py:64
  9.3 10.7 %collective-permute-start.2 = (bf16[112,2048]{1,0:T(8,128)(2,1)}, bf16[112,2048]{1,0:T(8,128)(2,1)S(1)}, u32[]{:S(2)}, u32[]{:S(2)}) collective-permute-start(bf16[112,2048]{1,0:T(8,128)(2,1)} %get-tuple-element.27), channel_id=1, source_target_pairs={{0,96},{1,25},{2,98},{3,27},{4,100},{5,29},{6,102},{7,31},{8,104},... | collective-permute-start | bytes 1376264 | tf_op jit(solution)/shard_map/ppermute | solution.py:64
  11.0 12.6 %collective-permute-start.3 = (bf16[112,2048]{1,0:T(8,128)(2,1)}, bf16[112,2048]{1,0:T(8,128)(2,1)S(1)}, u32[]{:S(2)}, u32[]{:S(2)}) collective-permute-start(bf16[112,2048]{1,0:T(8,128)(2,1)} %get-tuple-element.24.refs_0_), channel_id=1, source_target_pairs={{0,1},{1,0},{2,3},{3,2},{4,5},{5,4},{6,7},{7,6},{8,9},{9,8},{10,11... | collective-permute-start | bytes 1376264 | tf_op jit(solution)/shard_map/ppermute | solution.py:64
  11.0 1.0 copy-start.1
  19.2 4.4 %collective-permute-start.4 = (bf16[112,2048]{1,0:T(8,128)(2,1)S(1)}, bf16[112,2048]{1,0:T(8,128)(2,1)S(1)}, u32[]{:S(2)}, u32[]{:S(2)}) collective-permute-start(bf16[112,2048]{1,0:T(8,128)(2,1)S(1)} %collective-permute-done.refs_0_.refs_1_), channel_id=1, source_target_pairs={{0,1},{1,0},{2,3},{3,2},{4,5},{5,4},{6,7},{7,6},{8,9},{9,8},{10,11... | collective-permute-start | bytes 1376264 | tf_op jit(solution)/shard_map/ppermute | solution.py:64
  19.5 4.1 %collective-permute-start.5 = (bf16[112,2048]{1,0:T(8,128)(2,1)S(1)}, bf16[112,2048]{1,0:T(8,128)(2,1)S(1)}, u32[]{:S(2)}, u32[]{:S(2)}) collective-permute-start(bf16[112,2048]{1,0:T(8,128)(2,1)S(1)} %collective-permute-done.1.refs_1_.refs_2_), channel_id=1, source_target_pairs={{0,1},{1,0},{2,3},{3,2},{4,5},{5,4},{6,7},{7,6},{8,9},{9,8},{10,11... | collective-permute-start | bytes 1376264 | tf_op jit(solution)/shard_map/ppermute | solution.py:64
  19.9 3.7 %collective-permute-start.6 = (bf16[112,2048]{1,0:T(8,128)(2,1)S(1)}, bf16[112,2048]{1,0:T(8,128)(2,1)S(1)}, u32[]{:S(2)}, u32[]{:S(2)}) collective-permute-start(bf16[112,2048]{1,0:T(8,128)(2,1)S(1)} %collective-permute-done.2.refs_2_.refs_3_), channel_id=1, source_target_pairs={{0,1},{1,0},{2,3},{3,2},{4,5},{5,4},{6,7},{7,6},{8,9},{9,8},{10,11... | collective-permute-start | bytes 1376264 | tf_op jit(solution)/shard_map/ppermute | solution.py:64
  26.7 13.9 %collective-permute-start.16 = (bf16[544,256]{1,0:T(8,128)(2,1)S(1)}, bf16[544,256]{1,0:T(8,128)(2,1)S(1)}, u32[]{:S(2)}, u32[]{:S(2)}) collective-permute-start(bf16[544,256]{1,0:T(8,128)(2,1)S(1)} %get-tuple-element.33), channel_id=1, source_target_pairs={{0,4},{1,5},{2,6},{3,7},{4,0},{5,1},{6,2},{7,3},{8,12},{9,13},{10,... | collective-permute-start | bytes 835592 | tf_op jit(solution)/shard_map/ppermute | solution.py:64
  30.7 12.8 %collective-permute-start.17 = (bf16[544,256]{1,0:T(8,128)(2,1)S(1)}, bf16[544,256]{1,0:T(8,128)(2,1)S(1)}, u32[]{:S(2)}, u32[]{:S(2)}) collective-permute-start(bf16[544,256]{1,0:T(8,128)(2,1)S(1)} %get-tuple-element.34), channel_id=1, source_target_pairs={{0,2},{1,3},{2,4},{3,5},{4,6},{5,7},{6,0},{7,1},{8,10},{9,11},{10,... | collective-permute-start | bytes 835592 | tf_op jit(solution)/shard_map/ppermute | solution.py:64
  31.7 12.6 %collective-permute-start.18 = (bf16[544,256]{1,0:T(8,128)(2,1)S(1)}, bf16[544,256]{1,0:T(8,128)(2,1)S(1)}, u32[]{:S(2)}, u32[]{:S(2)}) collective-permute-start(bf16[544,256]{1,0:T(8,128)(2,1)S(1)} %get-tuple-element.35), channel_id=1, source_target_pairs={{0,6},{1,7},{2,0},{3,1},{4,2},{5,3},{6,4},{7,5},{8,14},{9,15},{10,... | collective-permute-start | bytes 835592 | tf_op jit(solution)/shard_map/ppermute | solution.py:64
  33.9 17.3 %collective-permute-start.7 = (bf16[544,256]{1,0:T(8,128)(2,1)S(1)}, bf16[544,256]{1,0:T(8,128)(2,1)S(1)}, u32[]{:S(2)}, u32[]{:S(2)}) collective-permute-start(bf16[544,256]{1,0:T(8,128)(2,1)S(1)} %get-tuple-element.29), channel_id=1, source_target_pairs={{0,80},{1,81},{2,82},{3,83},{4,84},{5,85},{6,86},{7,87},{8,88},{9,... | collective-permute-start | bytes 835592 | tf_op jit(solution)/shard_map/ppermute | solution.py:64
  37.5 16.4 %collective-permute-start.8 = (bf16[544,256]{1,0:T(8,128)(2,1)S(1)}, bf16[544,256]{1,0:T(8,128)(2,1)S(1)}, u32[]{:S(2)}, u32[]{:S(2)}) collective-permute-start(bf16[544,256]{1,0:T(8,128)(2,1)S(1)} %get-tuple-element.30), channel_id=1, source_target_pairs={{0,56},{1,57},{2,58},{3,59},{4,60},{5,61},{6,62},{7,63},{8,32},{9,... | collective-permute-start | bytes 835592 | tf_op jit(solution)/shard_map/ppermute | solution.py:64
  40.6 13.3 %collective-permute-start.9 = (bf16[544,256]{1,0:T(8,128)(2,1)S(1)}, bf16[544,256]{1,0:T(8,128)(2,1)S(1)}, u32[]{:S(2)}, u32[]{:S(2)}) collective-permute-start(bf16[544,256]{1,0:T(8,128)(2,1)S(1)} %get-tuple-element.31), channel_id=1, source_target_pairs={{0,104},{1,105},{2,106},{3,107},{4,108},{5,109},{6,110},{7,111},{8... | collective-permute-start | bytes 835592 | tf_op jit(solution)/shard_map/ppermute | solution.py:64
  44.4 19.6 %collective-permute-start.19 = (bf16[544,256]{1,0:T(8,128)(2,1)S(1)}, bf16[544,256]{1,0:T(8,128)(2,1)S(1)}, u32[]{:S(2)}, u32[]{:S(2)}) collective-permute-start(bf16[544,256]{1,0:T(8,128)(2,1)S(1)} %add_convert_fusion.1), channel_id=1, source_target_pairs={{0,80},{1,81},{2,82},{3,83},{4,84},{5,85},{6,86},{7,87},{8,88},{9,... | collective-permute-start | bytes 835592 | tf_op jit(solution)/shard_map/ppermute | solution.py:64
  48.6 15.8 %collective-permute-start.20 = (bf16[544,256]{1,0:T(8,128)(2,1)S(1)}, bf16[544,256]{1,0:T(8,128)(2,1)S(1)}, u32[]{:S(2)}, u32[]{:S(2)}) collective-permute-start(bf16[544,256]{1,0:T(8,128)(2,1)S(1)} %add_convert_fusion.1), channel_id=1, source_target_pairs={{0,56},{1,57},{2,58},{3,59},{4,60},{5,61},{6,62},{7,63},{8,32},{9,... | collective-permute-start | bytes 835592 | tf_op jit(solution)/shard_map/ppermute | solution.py:64
  51.2 15.6 %collective-permute-start.21 = (bf16[544,256]{1,0:T(8,128)(2,1)S(1)}, bf16[544,256]{1,0:T(8,128)(2,1)S(1)}, u32[]{:S(2)}, u32[]{:S(2)}) collective-permute-start(bf16[544,256]{1,0:T(8,128)(2,1)S(1)} %add_convert_fusion.1), channel_id=1, source_target_pairs={{0,104},{1,105},{2,106},{3,107},{4,108},{5,109},{6,110},{7,111},{8... | collective-permute-start | bytes 835592 | tf_op jit(solution)/shard_map/ppermute | solution.py:64
  54.1 14.1 %collective-permute-start.10 = (bf16[544,256]{1,0:T(8,128)(2,1)S(1)}, bf16[544,256]{1,0:T(8,128)(2,1)S(1)}, u32[]{:S(2)}, u32[]{:S(2)}) collective-permute-start(bf16[544,256]{1,0:T(8,128)(2,1)S(1)} %add_convert_fusion.3), channel_id=1, source_target_pairs={{0,4},{1,5},{2,6},{3,7},{4,0},{5,1},{6,2},{7,3},{8,12},{9,13},{10,... | collective-permute-start | bytes 835592 | tf_op jit(solution)/shard_map/ppermute | solution.py:64
  55.0 14.7 %collective-permute-start.11 = (bf16[544,256]{1,0:T(8,128)(2,1)S(1)}, bf16[544,256]{1,0:T(8,128)(2,1)S(1)}, u32[]{:S(2)}, u32[]{:S(2)}) collective-permute-start(bf16[544,256]{1,0:T(8,128)(2,1)S(1)} %add_convert_fusion.3), channel_id=1, source_target_pairs={{0,2},{1,3},{2,4},{3,5},{4,6},{5,7},{6,0},{7,1},{8,10},{9,11},{10,... | collective-permute-start | bytes 835592 | tf_op jit(solution)/shard_map/ppermute | solution.py:64
  64.0 8.5 %collective-permute-start.12 = (bf16[544,256]{1,0:T(8,128)(2,1)S(1)}, bf16[544,256]{1,0:T(8,128)(2,1)S(1)}, u32[]{:S(2)}, u32[]{:S(2)}) collective-permute-start(bf16[544,256]{1,0:T(8,128)(2,1)S(1)} %add_convert_fusion.3), channel_id=1, source_target_pairs={{0,6},{1,7},{2,0},{3,1},{4,2},{5,3},{6,4},{7,5},{8,14},{9,15},{10,... | collective-permute-start | bytes 835592 | tf_op jit(solution)/shard_map/ppermute | solution.py:64
  66.9 24.5 %copy-start.2 = (bf16[112,2048]{1,0:T(8,128)(2,1)S(1)}, bf16[112,2048]{1,0:T(8,128)(2,1)}, u32[]{:S(2)}) copy-start(bf16[112,2048]{1,0:T(8,128)(2,1)} %get-tuple-element.24.refs_0_) | copy-start | bytes 1376260
  67.0 12.5 %collective-permute-start.24 = (bf16[544,256]{1,0:T(8,128)(2,1)S(1)}, bf16[544,256]{1,0:T(8,128)(2,1)S(1)}, u32[]{:S(2)}, u32[]{:S(2)}) collective-permute-start(bf16[544,256]{1,0:T(8,128)(2,1)S(1)} %add_convert_fusion.refs_8_), channel_id=1, source_target_pairs={{0,6},{1,7},{2,0},{3,1},{4,2},{5,3},{6,4},{7,5},{8,14},{9,15},{10,... | collective-permute-start | bytes 835592 | tf_op jit(solution)/shard_map/ppermute | solution.py:64
  72.6 12.6 %collective-permute-start.15 = (bf16[544,256]{1,0:T(8,128)(2,1)S(1)}, bf16[544,256]{1,0:T(8,128)(2,1)S(1)}, u32[]{:S(2)}, u32[]{:S(2)}) collective-permute-start(bf16[544,256]{1,0:T(8,128)(2,1)S(1)} %add_convert_fusion.2.refs_4_), channel_id=1, source_target_pairs={{0,104},{1,105},{2,106},{3,107},{4,108},{5,109},{6,110},{7,111},{8... | collective-permute-start | bytes 835592 | tf_op jit(solution)/shard_map/ppermute | solution.py:64
  72.7 12.5 %collective-permute-start.23 = (bf16[544,256]{1,0:T(8,128)(2,1)S(1)}, bf16[544,256]{1,0:T(8,128)(2,1)S(1)}, u32[]{:S(2)}, u32[]{:S(2)}) collective-permute-start(bf16[544,256]{1,0:T(8,128)(2,1)S(1)} %add_convert_fusion.refs_8_), channel_id=1, source_target_pairs={{0,4},{1,5},{2,6},{3,7},{4,0},{5,1},{6,2},{7,3},{8,12},{9,13},{10,... | collective-permute-start | bytes 835592 | tf_op jit(solution)/shard_map/ppermute | solution.py:64
  73.0 15.1 %collective-permute-start.22 = (bf16[544,256]{1,0:T(8,128)(2,1)S(1)}, bf16[544,256]{1,0:T(8,128)(2,1)S(1)}, u32[]{:S(2)}, u32[]{:S(2)}) collective-permute-start(bf16[544,256]{1,0:T(8,128)(2,1)S(1)} %add_convert_fusion.refs_8_), channel_id=1, source_target_pairs={{0,2},{1,3},{2,4},{3,5},{4,6},{5,7},{6,0},{7,1},{8,10},{9,11},{10,... | collective-permute-start | bytes 835592 | tf_op jit(solution)/shard_map/ppermute | solution.py:64
  74.8 13.3 %collective-permute-start.14 = (bf16[544,256]{1,0:T(8,128)(2,1)S(1)}, bf16[544,256]{1,0:T(8,128)(2,1)S(1)}, u32[]{:S(2)}, u32[]{:S(2)}) collective-permute-start(bf16[544,256]{1,0:T(8,128)(2,1)S(1)} %add_convert_fusion.2.refs_4_), channel_id=1, source_target_pairs={{0,80},{1,81},{2,82},{3,83},{4,84},{5,85},{6,86},{7,87},{8,88},{9,... | collective-permute-start | bytes 835592 | tf_op jit(solution)/shard_map/ppermute | solution.py:64
  79.5 9.9 %collective-permute-start.13 = (bf16[544,256]{1,0:T(8,128)(2,1)S(1)}, bf16[544,256]{1,0:T(8,128)(2,1)S(1)}, u32[]{:S(2)}, u32[]{:S(2)}) collective-permute-start(bf16[544,256]{1,0:T(8,128)(2,1)S(1)} %add_convert_fusion.2.refs_4_), channel_id=1, source_target_pairs={{0,56},{1,57},{2,58},{3,59},{4,60},{5,61},{6,62},{7,63},{8,32},{9,... | collective-permute-start | bytes 835592 | tf_op jit(solution)/shard_map/ppermute | solution.py:64
  85.2 6.2 %collective-permute-start.28 = (bf16[1088,256]{1,0:T(8,128)(2,1)S(1)}, bf16[1088,256]{1,0:T(8,128)(2,1)S(1)}, u32[]{:S(2)}, u32[]{:S(2)}) collective-permute-start(bf16[1088,256]{1,0:T(8,128)(2,1)S(1)} %pad_maximum_fusion.1), channel_id=1, source_target_pairs={{0,1},{1,0},{2,3},{3,2},{4,5},{5,4},{6,7},{7,6},{8,9},{9,8},{10,11... | collective-permute-start | bytes 1671176 | tf_op jit(solution)/shard_map/ppermute | solution.py:64
  85.2 4.3 %collective-permute-start.29 = (bf16[544,256]{1,0:T(8,128)(2,1)S(1)}, bf16[544,256]{1,0:T(8,128)(2,1)S(1)}, u32[]{:S(2)}, u32[]{:S(2)}) collective-permute-start(bf16[544,256]{1,0:T(8,128)(2,1)S(1)} %collective-permute-done.23.refs_10_), channel_id=1, source_target_pairs={{0,1},{1,0},{2,3},{3,2},{4,5},{5,4},{6,7},{7,6},{8,9},{9,8},{10,11... | collective-permute-start | bytes 835592 | tf_op jit(solution)/shard_map/ppermute | solution.py:64
  85.7 21.1 %copy-start = (f32[4,112,2048]{2,1,0:T(8,128)S(1)}, f32[4,112,2048]{2,1,0:T(8,128)}, u32[]{:S(2)}) copy-start(f32[4,112,2048]{2,1,0:T(8,128)} %weight.7) | copy-start | bytes 11010052
  88.0 3.4 %collective-permute-start.25 = (bf16[1088,256]{1,0:T(8,128)(2,1)S(1)}, bf16[1088,256]{1,0:T(8,128)(2,1)S(1)}, u32[]{:S(2)}, u32[]{:S(2)}) collective-permute-start(bf16[1088,256]{1,0:T(8,128)(2,1)S(1)} %pad_maximum_fusion), channel_id=1, source_target_pairs={{0,1},{1,0},{2,3},{3,2},{4,5},{5,4},{6,7},{7,6},{8,9},{9,8},{10,11... | collective-permute-start | bytes 1671176 | tf_op jit(solution)/shard_map/ppermute | solution.py:64
  88.1 2.3 %collective-permute-start.30 = (bf16[544,256]{1,0:T(8,128)(2,1)S(1)}, bf16[544,256]{1,0:T(8,128)(2,1)S(1)}, u32[]{:S(2)}, u32[]{:S(2)}) collective-permute-start(bf16[544,256]{1,0:T(8,128)(2,1)S(1)} %collective-permute-done.22.refs_9_), channel_id=1, source_target_pairs={{0,1},{1,0},{2,3},{3,2},{4,5},{5,4},{6,7},{7,6},{8,9},{9,8},{10,11... | collective-permute-start | bytes 835592 | tf_op jit(solution)/shard_map/ppermute | solution.py:64
  89.4 1.6 %collective-permute-start.26 = (bf16[544,256]{1,0:T(8,128)(2,1)S(1)}, bf16[544,256]{1,0:T(8,128)(2,1)S(1)}, u32[]{:S(2)}, u32[]{:S(2)}) collective-permute-start(bf16[544,256]{1,0:T(8,128)(2,1)S(1)} %collective-permute-done.14.refs_6_), channel_id=1, source_target_pairs={{0,1},{1,0},{2,3},{3,2},{4,5},{5,4},{6,7},{7,6},{8,9},{9,8},{10,11... | collective-permute-start | bytes 835592 | tf_op jit(solution)/shard_map/ppermute | solution.py:64
  89.4 2.0 %collective-permute-start.27 = (bf16[544,256]{1,0:T(8,128)(2,1)S(1)}, bf16[544,256]{1,0:T(8,128)(2,1)S(1)}, u32[]{:S(2)}, u32[]{:S(2)}) collective-permute-start(bf16[544,256]{1,0:T(8,128)(2,1)S(1)} %collective-permute-done.13.refs_5_), channel_id=1, source_target_pairs={{0,1},{1,0},{2,3},{3,2},{4,5},{5,4},{6,7},{7,6},{8,9},{9,8},{10,11... | collective-permute-start | bytes 835592 | tf_op jit(solution)/shard_map/ppermute | solution.py:64
  102.0 13.0 %collective-permute-start.33 = (bf16[112,2048]{1,0:T(8,128)(2,1)S(1)}, bf16[112,2048]{1,0:T(8,128)(2,1)S(1)}, u32[]{:S(2)}, u32[]{:S(2)}) collective-permute-start(bf16[112,2048]{1,0:T(8,128)(2,1)S(1)} %get-tuple-element.38), channel_id=1, source_target_pairs={{32,0},{9,1},{34,2},{11,3},{36,4},{13,5},{38,6},{15,7},{40,8},{17,... | collective-permute-start | bytes 1376264 | tf_op jit(solution)/shard_map/ppermute | solution.py:64
  104.0 14.8 %collective-permute-start.32 = (bf16[112,2048]{1,0:T(8,128)(2,1)S(1)}, bf16[112,2048]{1,0:T(8,128)(2,1)S(1)}, u32[]{:S(2)}, u32[]{:S(2)}) collective-permute-start(bf16[112,2048]{1,0:T(8,128)(2,1)S(1)} %get-tuple-element.37), channel_id=1, source_target_pairs={{16,0},{65,1},{18,2},{67,3},{20,4},{69,5},{22,6},{71,7},{24,8},{73... | collective-permute-start | bytes 1376264 | tf_op jit(solution)/shard_map/ppermute | solution.py:64
  106.8 13.5 %collective-permute-start.31 = (bf16[112,2048]{1,0:T(8,128)(2,1)S(1)}, bf16[112,2048]{1,0:T(8,128)(2,1)S(1)}, u32[]{:S(2)}, u32[]{:S(2)}) collective-permute-start(bf16[112,2048]{1,0:T(8,128)(2,1)S(1)} %get-tuple-element.36), channel_id=1, source_target_pairs={{96,0},{25,1},{98,2},{27,3},{100,4},{29,5},{102,6},{31,7},{104,8},... | collective-permute-start | bytes 1376264 | tf_op jit(solution)/shard_map/ppermute | solution.py:64

commit v4 on v3

--- a/solution.py
+++ b/solution.py
@@ -12,6 +12,7 @@
 R = 2048
 CAP = 112
 AXES = ("group", "col")
+OFFSETS = (0, 2, 1, 3)
 
 quintic_first = 3.4445
 quintic_second = -4.775
@@ -72,7 +73,7 @@
 def live_kernel(lengths, momentum, o0, o1, o2, o3, rows, sems):
     home = places()[3]
     outs = (o0, o1, o2, o3)
-    experts = [lax.rem(home + d, 4) for d in range(4)]
+    experts = [lax.rem(home + d, 4) for d in OFFSETS]
     loads = [
         pltpu.make_async_copy(momentum.at[experts[d]], rows.at[d], sems.at[d])
         for d in range(4)
@@ -84,9 +85,10 @@
         loads[d].wait()
         slot = lax.broadcasted_iota(jnp.int32, (CAP, 128), 0)
         keep = slot < jnp.sum(jnp.where(lane == experts[d], lengths[...], 0))
+        keep = jnp.where(keep, 1.0, 0.0).astype(jnp.bfloat16)
         for at in range(0, R, 128):
             value = rows[d, :, at:at + 128]
-            outs[d][:, at:at + 128] = jnp.where(keep, value, jnp.zeros_like(value))
+            outs[d][:, at:at + 128] = value * keep
 
 
 def live(lengths, momentum):
@@ -229,10 +231,10 @@
             for k in range(4):
                 if side == 0:
                     chunk = chunks[route * 4 + k]
-                elif k in (0, 3):
-                    chunk = chunks[8 + route * 3].at[pl.ds(k // 3 * CHUNK, CHUNK)]
+                elif k in (0, 2):
+                    chunk = chunks[8 + route * 3].at[pl.ds(k // 2 * CHUNK, CHUNK)]
                 else:
-                    chunk = chunks[8 + route * 3 + 3 - k]
+                    chunk = chunks[8 + route * 3 + 2 - k // 3]
                 number = half * 8 + route * 4 + lax.rem(own + 4 - k, 4)
                 loads.append(pltpu.make_async_copy(
                     chunk,
@@ -267,14 +269,11 @@
         value = value.astype(jnp.float32)
         return value * value
 
-    twice = jnp.zeros((16, BLOCK), jnp.float32)
-    once = jnp.zeros((HALF_BLOCK, HALF_BLOCK), jnp.float32)
     for number in range(16):
         here = blocks.at[pl.ds(number * CHUNK, CHUNK)]
         pltpu.make_async_copy(here, here, chunk_sems.at[number]).wait()
-        for at in range(number * CHUNK, (number + 1) * CHUNK, 16):
-            if at % HALF < TOPS:
-                twice += squared(blocks[at:at + 16, :])
+    twice = jnp.zeros((16, BLOCK), jnp.float32)
+    once = jnp.zeros((HALF_BLOCK, HALF_BLOCK), jnp.float32)
     for i in range(8):
         half, a = i // 4, i % 4
         start = half * HALF + TOPS + a * HALF_BLOCK
@@ -285,9 +284,6 @@
         diagonal[i * BLOCK + HALF_BLOCK:(i + 1) * BLOCK, :HALF_BLOCK] = top[:, HALF_BLOCK:].T
         diagonal[i * BLOCK + HALF_BLOCK:(i + 1) * BLOCK, HALF_BLOCK:] = last
         once += squared(top[:, :HALF_BLOCK]) + squared(last) + 2.0 * squared(top[:, HALF_BLOCK:])
-    total = 2.0 * jnp.sum(twice, axis=(0, 1), keepdims=True) + jnp.sum(once, axis=(0, 1), keepdims=True)
-    norm_scale = margin_square / (jnp.sqrt(total) + epsilon_norm)
-    root = jnp.sqrt(norm_scale)
     for load in loads[:4]:
         load.wait()
 
@@ -296,6 +292,12 @@
         value = times_gram(x_all, j)
         first[:, at] = value
         first_round[:, at] = value.astype(jnp.bfloat16)
+        for at in range(2 * j * CHUNK, 2 * (j + 1) * CHUNK, 16):
+            if at % HALF < TOPS:
+                twice += squared(blocks[at:at + 16, :])
+    total = 2.0 * jnp.sum(twice, axis=(0, 1), keepdims=True) + jnp.sum(once, axis=(0, 1), keepdims=True)
+    norm_scale = margin_square / (jnp.sqrt(total) + epsilon_norm)
+    root = jnp.sqrt(norm_scale)
     for j in range(8):
         at = slice(j * BLOCK, (j + 1) * BLOCK)
         second = times_gram(first_round, j)
@@ -333,7 +335,7 @@
 
 def apply_kernel(d, value, weight, *refs):
     out, new_weight, rows, weights, in_sems, out_sems = refs[-6:]
-    expert = lax.rem(places()[3] + d, 4)
+    expert = lax.rem(places()[3] + OFFSETS[d], 4)
     parts = [slice(at, at + R // 4) for at in range(0, R, R // 4)]
     loads = [
         pltpu.make_async_copy(weight.at[expert, :, part], weights.at[:, part], in_sems.at[i])
@@ -389,7 +391,7 @@
 
 
 def on_device(momentum, lengths, weight):
-    routes = {d: to_expert(d) for d in (1, 2, 3)}
+    routes = {d: to_expert(OFFSETS[d]) for d in (1, 2, 3)}
     rows = live(lengths.reshape(1, 4), momentum)
     rows = [rows[0]] + [shift(rows[d], routes[d]) for d in (1, 2, 3)]
     other_rows = [shift(part, OTHER_CORE) for part in rows]
@@ -414,7 +416,7 @@
         mine += got
         others += [
             shift(part, OTHER_CORE)
-            for part in (jnp.concatenate([got[0], got[3]], 0), got[2], got[1])
+            for part in (jnp.concatenate([got[0], got[2]], 0), got[3], got[1])
         ]
 
     updates = update(rows, mine + others)

time: 123 us -> 122 us (level)
  transfers between devices with their start and end apart: 34 -> 34, of which waited for: 20 -> 13; matrix products, arithmetic and copies ran while one was open for 1% -> 1% of each run, Pallas kernels for 6% -> 6%
where the time goes in v4:
time: 122 us
  starting transfers between devices  50.9 us (42%)
  waiting for transfers between devices  42.1 us (35%)
  Pallas kernels  26.4 us (22%)
    ppermute x34, starting transfers between devices, shift(): return lax.ppermute(value, AXES, steps)  50.9 us
    ppermute x34, waiting for transfers between devices, shift(): return lax.ppermute(value, AXES, steps)  42.1 us
    pallas_call x1, Pallas kernels, update(): pl.pallas_call(update_kernel, out_shape=[jax.ShapeDtypeStruct((CAP, R), j...  10.3 us
    pallas_call x3, Pallas kernels, gram(): pl.pallas_call(functools.partial(gram_kernel, count, before is None, last...  7.07 us
    pallas_call x4, Pallas kernels, apply(): pl.pallas_call(functools.partial(apply_kernel, d), out_shape=[jax.ShapeDt...  5.21 us
    pallas_call x1, Pallas kernels, live(): pl.pallas_call(live_kernel, out_shape=[jax.ShapeDtypeStruct((CAP, R), jnp...  3.78 us
  transfers between devices with their start and end apart: 34, of which 13 were waited for; matrix products, arithmetic and copies ran while one was open for 1% of the time, Pallas kernels for 6%

profile of v4, /device:TPU:0, one launch (start us, length us, event | category | flops | bytes accessed | tf_op | source)
XLA Modules:
  0.0 121.9 jit_solution(7987839479010197731)
XLA Ops:
  0.6 3.8 %live.1 = (bf16[112,2048]{1,0:T(8,128)(2,1)}, bf16[112,2048]{1,0:T(8,128)(2,1)}, bf16[112,2048]{1,0:T(8,128)(2,1)}, bf16[112,2048]{1,0:T(8,128)(2,1)}) custom-call(s32[1,4]{1,0:T(1,128)} %bitcast.1, bf16[4,112,2048]{2,1,0:T(8,128)(2,1)} %momentum.1), custom_call_target="tpu_custom_call" | custom-call | tf_op jit(solution)/shard_map/live/pallas_call | solution.py:95
  4.4 3.4 %collective-permute-start = (bf16[112,2048]{1,0:T(8,128)(2,1)}, bf16[112,2048]{1,0:T(8,128)(2,1)S(1)}, u32[]{:S(2)}, u32[]{:S(2)}) collective-permute-start(bf16[112,2048]{1,0:T(8,128)(2,1)} %get-tuple-element.25), channel_id=1, source_target_pairs={{0,16},{1,65},{2,18},{3,67},{4,20},{5,69},{6,22},{7,71},{8,24},{9,... | collective-permute-start | bytes 1376264 | tf_op jit(solution)/shard_map/ppermute | solution.py:65
  7.8 1.5 %collective-permute-start.1 = (bf16[112,2048]{1,0:T(8,128)(2,1)}, bf16[112,2048]{1,0:T(8,128)(2,1)S(1)}, u32[]{:S(2)}, u32[]{:S(2)}) collective-permute-start(bf16[112,2048]{1,0:T(8,128)(2,1)} %get-tuple-element.26), channel_id=1, source_target_pairs={{0,32},{1,9},{2,34},{3,11},{4,36},{5,13},{6,38},{7,15},{8,40},{9,1... | collective-permute-start | bytes 1376264 | tf_op jit(solution)/shard_map/ppermute | solution.py:65
  9.3 1.7 %collective-permute-start.2 = (bf16[112,2048]{1,0:T(8,128)(2,1)}, bf16[112,2048]{1,0:T(8,128)(2,1)S(1)}, u32[]{:S(2)}, u32[]{:S(2)}) collective-permute-start(bf16[112,2048]{1,0:T(8,128)(2,1)} %get-tuple-element.27), channel_id=1, source_target_pairs={{0,96},{1,25},{2,98},{3,27},{4,100},{5,29},{6,102},{7,31},{8,104},... | collective-permute-start | bytes 1376264 | tf_op jit(solution)/shard_map/ppermute | solution.py:65
  11.0 1.0 copy-done.1
  12.0 1.1 gram.3.refs_3_
  13.1 5.9 %collective-permute-done.refs_0_.refs_1_ = bf16[112,2048]{1,0:T(8,128)(2,1)S(1)} collective-permute-done((bf16[112,2048]{1,0:T(8,128)(2,1)}, bf16[112,2048]{1,0:T(8,128)(2,1)S(1)}, u32[]{:S(2)}, u32[]{:S(2)}) %collective-permute-start) | collective-permute-done | bytes 458784 | tf_op jit(solution)/shard_map/ppermute | solution.py:65
  19.0 0.5 collective-permute-start.5
  19.5 0.3 collective-permute-start.6
  19.9 2.9 %gram.4.refs_4_ = f32[4608,256]{1,0:T(8,128)S(1)} custom-call(bf16[112,2048]{1,0:T(8,128)(2,1)S(1)} %collective-permute-done.refs_0_.refs_1_, bf16[112,2048]{1,0:T(8,128)(2,1)S(1)} %collective-permute-done.1.refs_1_.refs_2_, bf16[112,2048]{1,0:T(8,128)(2,1)S(1)} %collective-permute-done.2.refs_2_.refs_3_, ...), custom_call_target="tpu_custom_call", output_to_operand_aliasing={{}: (3, {})} | custom-call | flops 31708938240 | bytes 10813440 | tf_op jit(solution)/shard_map/gram/pallas_call | solution.py:193
  22.8 3.1 %gram.5 = (bf16[544,256]{1,0:T(8,128)(2,1)S(1)}, bf16[544,256]{1,0:T(8,128)(2,1)S(1)}, bf16[544,256]{1,0:T(8,128)(2,1)S(1)}, bf16[544,256]{1,0:T(8,128)(2,1)S(1)...) custom-call(bf16[112,2048]{1,0:T(8,128)(2,1)S(1)} %collective-permut, ...), custom_call_target="tpu_custom_call" | custom-call | flops 1056964608 | bytes 11272192 | tf_op jit(solution)/shard_map/gram/pallas_call | solution.py:193
  25.9 4.0 %collective-permute-start.16 = (bf16[544,256]{1,0:T(8,128)(2,1)S(1)}, bf16[544,256]{1,0:T(8,128)(2,1)S(1)}, u32[]{:S(2)}, u32[]{:S(2)}) collective-permute-start(bf16[544,256]{1,0:T(8,128)(2,1)S(1)} %get-tuple-element.33), channel_id=1, source_target_pairs={{0,4},{1,5},{2,6},{3,7},{4,0},{5,1},{6,2},{7,3},{8,12},{9,13},{10,... | collective-permute-start | bytes 835592 | tf_op jit(solution)/shard_map/ppermute | solution.py:65
  29.8 1.0 collective-permute-start.17
  30.9 2.2 %collective-permute-start.18 = (bf16[544,256]{1,0:T(8,128)(2,1)S(1)}, bf16[544,256]{1,0:T(8,128)(2,1)S(1)}, u32[]{:S(2)}, u32[]{:S(2)}) collective-permute-start(bf16[544,256]{1,0:T(8,128)(2,1)S(1)} %get-tuple-element.35), channel_id=1, source_target_pairs={{0,6},{1,7},{2,0},{3,1},{4,2},{5,3},{6,4},{7,5},{8,14},{9,15},{10,... | collective-permute-start | bytes 835592 | tf_op jit(solution)/shard_map/ppermute | solution.py:65
  33.1 4.8 %collective-permute-start.7 = (bf16[544,256]{1,0:T(8,128)(2,1)S(1)}, bf16[544,256]{1,0:T(8,128)(2,1)S(1)}, u32[]{:S(2)}, u32[]{:S(2)}) collective-permute-start(bf16[544,256]{1,0:T(8,128)(2,1)S(1)} %get-tuple-element.29), channel_id=1, source_target_pairs={{0,80},{1,81},{2,82},{3,83},{4,84},{5,85},{6,86},{7,87},{8,88},{9,... | collective-permute-start | bytes 835592 | tf_op jit(solution)/shard_map/ppermute | solution.py:65
  37.9 2.0 %collective-permute-start.8 = (bf16[544,256]{1,0:T(8,128)(2,1)S(1)}, bf16[544,256]{1,0:T(8,128)(2,1)S(1)}, u32[]{:S(2)}, u32[]{:S(2)}) collective-permute-start(bf16[544,256]{1,0:T(8,128)(2,1)S(1)} %get-tuple-element.30), channel_id=1, source_target_pairs={{0,56},{1,57},{2,58},{3,59},{4,60},{5,61},{6,62},{7,63},{8,32},{9,... | collective-permute-start | bytes 835592 | tf_op jit(solution)/shard_map/ppermute | solution.py:65
  39.8 2.2 %collective-permute-start.9 = (bf16[544,256]{1,0:T(8,128)(2,1)S(1)}, bf16[544,256]{1,0:T(8,128)(2,1)S(1)}, u32[]{:S(2)}, u32[]{:S(2)}) collective-permute-start(bf16[544,256]{1,0:T(8,128)(2,1)S(1)} %get-tuple-element.31), channel_id=1, source_target_pairs={{0,104},{1,105},{2,106},{3,107},{4,108},{5,109},{6,110},{7,111},{8... | collective-permute-start | bytes 835592 | tf_op jit(solution)/shard_map/ppermute | solution.py:65
  42.0 0.8 collective-permute-done.17
  42.8 0.8 collective-permute-done.18
  43.7 4.7 %collective-permute-start.19 = (bf16[544,256]{1,0:T(8,128)(2,1)S(1)}, bf16[544,256]{1,0:T(8,128)(2,1)S(1)}, u32[]{:S(2)}, u32[]{:S(2)}) collective-permute-start(bf16[544,256]{1,0:T(8,128)(2,1)S(1)} %add_convert_fusion.1), channel_id=1, source_target_pairs={{0,80},{1,81},{2,82},{3,83},{4,84},{5,85},{6,86},{7,87},{8,88},{9,... | collective-permute-start | bytes 835592 | tf_op jit(solution)/shard_map/ppermute | solution.py:65
  48.4 2.4 %collective-permute-start.20 = (bf16[544,256]{1,0:T(8,128)(2,1)S(1)}, bf16[544,256]{1,0:T(8,128)(2,1)S(1)}, u32[]{:S(2)}, u32[]{:S(2)}) collective-permute-start(bf16[544,256]{1,0:T(8,128)(2,1)S(1)} %add_convert_fusion.1), channel_id=1, source_target_pairs={{0,56},{1,57},{2,58},{3,59},{4,60},{5,61},{6,62},{7,63},{8,32},{9,... | collective-permute-start | bytes 835592 | tf_op jit(solution)/shard_map/ppermute | solution.py:65
  50.8 1.8 %collective-permute-start.21 = (bf16[544,256]{1,0:T(8,128)(2,1)S(1)}, bf16[544,256]{1,0:T(8,128)(2,1)S(1)}, u32[]{:S(2)}, u32[]{:S(2)}) collective-permute-start(bf16[544,256]{1,0:T(8,128)(2,1)S(1)} %add_convert_fusion.1), channel_id=1, source_target_pairs={{0,104},{1,105},{2,106},{3,107},{4,108},{5,109},{6,110},{7,111},{8... | collective-permute-start | bytes 835592 | tf_op jit(solution)/shard_map/ppermute | solution.py:65
  52.8 0.1 add_convert_fusion.3
  52.9 1.9 %collective-permute-start.10 = (bf16[544,256]{1,0:T(8,128)(2,1)S(1)}, bf16[544,256]{1,0:T(8,128)(2,1)S(1)}, u32[]{:S(2)}, u32[]{:S(2)}) collective-permute-start(bf16[544,256]{1,0:T(8,128)(2,1)S(1)} %add_convert_fusion.3), channel_id=1, source_target_pairs={{0,4},{1,5},{2,6},{3,7},{4,0},{5,1},{6,2},{7,3},{8,12},{9,13},{10,... | collective-permute-start | bytes 835592 | tf_op jit(solution)/shard_map/ppermute | solution.py:65
  54.8 1.5 %collective-permute-start.11 = (bf16[544,256]{1,0:T(8,128)(2,1)S(1)}, bf16[544,256]{1,0:T(8,128)(2,1)S(1)}, u32[]{:S(2)}, u32[]{:S(2)}) collective-permute-start(bf16[544,256]{1,0:T(8,128)(2,1)S(1)} %add_convert_fusion.3), channel_id=1, source_target_pairs={{0,2},{1,3},{2,4},{3,5},{4,6},{5,7},{6,0},{7,1},{8,10},{9,11},{10,... | collective-permute-start | bytes 835592 | tf_op jit(solution)/shard_map/ppermute | solution.py:65
  56.3 7.7 %collective-permute-done.19 = bf16[544,256]{1,0:T(8,128)(2,1)S(1)} collective-permute-done((bf16[544,256]{1,0:T(8,128)(2,1)S(1)}, bf16[544,256]{1,0:T(8,128)(2,1)S(1)}, u32[]{:S(2)}, u32[]{:S(2)}) %collective-permute-start.19) | collective-permute-done | bytes 278560 | tf_op jit(solution)/shard_map/ppermute | solution.py:65
  64.0 2.9 %collective-permute-done.21 = bf16[544,256]{1,0:T(8,128)(2,1)S(1)} collective-permute-done((bf16[544,256]{1,0:T(8,128)(2,1)S(1)}, bf16[544,256]{1,0:T(8,128)(2,1)S(1)}, u32[]{:S(2)}, u32[]{:S(2)}) %collective-permute-start.21) | collective-permute-done | bytes 278560 | tf_op jit(solution)/shard_map/ppermute | solution.py:65
  67.1 0.4 collective-permute-start.23
  67.5 5.2 %collective-permute-done.12 = bf16[544,256]{1,0:T(8,128)(2,1)S(1)} collective-permute-done((bf16[544,256]{1,0:T(8,128)(2,1)S(1)}, bf16[544,256]{1,0:T(8,128)(2,1)S(1)}, u32[]{:S(2)}, u32[]{:S(2)}) %collective-permute-start.12) | collective-permute-done | bytes 278560 | tf_op jit(solution)/shard_map/ppermute | solution.py:65
  72.8 2.8 %collective-permute-start.14 = (bf16[544,256]{1,0:T(8,128)(2,1)S(1)}, bf16[544,256]{1,0:T(8,128)(2,1)S(1)}, u32[]{:S(2)}, u32[]{:S(2)}) collective-permute-start(bf16[544,256]{1,0:T(8,128)(2,1)S(1)} %add_convert_fusion.2.refs_4_), channel_id=1, source_target_pairs={{0,80},{1,81},{2,82},{3,83},{4,84},{5,85},{6,86},{7,87},{8,88},{9,... | collective-permute-start | bytes 835592 | tf_op jit(solution)/shard_map/ppermute | solution.py:65
  75.6 2.0 %collective-permute-start.22 = (bf16[544,256]{1,0:T(8,128)(2,1)S(1)}, bf16[544,256]{1,0:T(8,128)(2,1)S(1)}, u32[]{:S(2)}, u32[]{:S(2)}) collective-permute-start(bf16[544,256]{1,0:T(8,128)(2,1)S(1)} %add_convert_fusion.refs_8_), channel_id=1, source_target_pairs={{0,2},{1,3},{2,4},{3,5},{4,6},{5,7},{6,0},{7,1},{8,10},{9,11},{10,... | collective-permute-start | bytes 835592 | tf_op jit(solution)/shard_map/ppermute | solution.py:65
  77.6 4.4 %collective-permute-start.15 = (bf16[544,256]{1,0:T(8,128)(2,1)S(1)}, bf16[544,256]{1,0:T(8,128)(2,1)S(1)}, u32[]{:S(2)}, u32[]{:S(2)}) collective-permute-start(bf16[544,256]{1,0:T(8,128)(2,1)S(1)} %add_convert_fusion.2.refs_4_), channel_id=1, source_target_pairs={{0,104},{1,105},{2,106},{3,107},{4,108},{5,109},{6,110},{7,111},{8... | collective-permute-start | bytes 835592 | tf_op jit(solution)/shard_map/ppermute | solution.py:65
  82.0 0.8 collective-permute-start.13
  82.8 3.8 %collective-permute-done.14.refs_6_ = bf16[544,256]{1,0:T(8,128)(2,1)S(1)} collective-permute-done((bf16[544,256]{1,0:T(8,128)(2,1)S(1)}, bf16[544,256]{1,0:T(8,128)(2,1)S(1)}, u32[]{:S(2)}, u32[]{:S(2)}) %collective-permute-start.14) | collective-permute-done | bytes 278560 | tf_op jit(solution)/shard_map/ppermute | solution.py:65
  86.7 0.5 collective-permute-start.29
  87.3 1.3 %collective-permute-done.15.refs_7_ = bf16[544,256]{1,0:T(8,128)(2,1)S(1)} collective-permute-done((bf16[544,256]{1,0:T(8,128)(2,1)S(1)}, bf16[544,256]{1,0:T(8,128)(2,1)S(1)}, u32[]{:S(2)}, u32[]{:S(2)}) %collective-permute-start.15) | collective-permute-done | bytes 278560 | tf_op jit(solution)/shard_map/ppermute | solution.py:65
  88.7 2.0 %collective-permute-done.13.refs_5_ = bf16[544,256]{1,0:T(8,128)(2,1)S(1)} collective-permute-done((bf16[544,256]{1,0:T(8,128)(2,1)S(1)}, bf16[544,256]{1,0:T(8,128)(2,1)S(1)}, u32[]{:S(2)}, u32[]{:S(2)}) %collective-permute-start.13) | collective-permute-done | bytes 278560 | tf_op jit(solution)/shard_map/ppermute | solution.py:65
  90.7 0.5 collective-permute-start.27
  91.2 1.0 collective-permute-done.26.refs_13_
  92.2 0.4 collective-permute-done.27.refs_14_
  92.7 10.3 %update.1 = (bf16[112,2048]{1,0:T(8,128)(2,1)S(1)}, bf16[112,2048]{1,0:T(8,128)(2,1)S(1)}, bf16[112,2048]{1,0:T(8,128)(2,1)S(1)}, bf16[112,2048]{1,0:T(8,128)(2,1)S(1)}) custom-call(bf16[112,2048]{1,0:T(8,128)(2,1)S(1)} %copy-done.2, bf16[112,2048]{1,0:T(8,128)(2,1)S(1)} %collective-permute-done.refs_0_.refs_1_, ...), custom_call_target="tpu_custom_call" | custom-call | tf_op jit(solution)/shard_map/update/pallas_call | solution.py:317
  103.0 1.6 %collective-permute-start.33 = (bf16[112,2048]{1,0:T(8,128)(2,1)S(1)}, bf16[112,2048]{1,0:T(8,128)(2,1)S(1)}, u32[]{:S(2)}, u32[]{:S(2)}) collective-permute-start(bf16[112,2048]{1,0:T(8,128)(2,1)S(1)} %get-tuple-element.38), channel_id=1, source_target_pairs={{16,0},{65,1},{18,2},{67,3},{20,4},{69,5},{22,6},{71,7},{24,8},{73... | collective-permute-start | bytes 1376264 | tf_op jit(solution)/shard_map/ppermute | solution.py:65
  104.5 2.0 %collective-permute-start.31 = (bf16[112,2048]{1,0:T(8,128)(2,1)S(1)}, bf16[112,2048]{1,0:T(8,128)(2,1)S(1)}, u32[]{:S(2)}, u32[]{:S(2)}) collective-permute-start(bf16[112,2048]{1,0:T(8,128)(2,1)S(1)} %get-tuple-element.36), channel_id=1, source_target_pairs={{96,0},{25,1},{98,2},{27,3},{100,4},{29,5},{102,6},{31,7},{104,8},... | collective-permute-start | bytes 1376264 | tf_op jit(solution)/shard_map/ppermute | solution.py:65
  106.5 1.3 %apply.4 = (bf16[4,112,2048]{2,1,0:T(8,128)(2,1)}, f32[4,112,2048]{2,1,0:T(8,128)}) custom-call(bf16[112,2048]{1,0:T(8,128)(2,1)S(1)} %get-tuple-element.39.value, f32[4,112,2048]{2,1,0:T(8,128)S(1)} %copy-done), custom_call_target="tpu_custom_call" | custom-call | flops 688128 | bytes 2752512 | tf_op jit(solution)/shard_map/apply/pallas_call | solution.py:364
  107.8 10.0 %collective-permute-done.33.value = bf16[112,2048]{1,0:T(8,128)(2,1)S(1)} collective-permute-done((bf16[112,2048]{1,0:T(8,128)(2,1)S(1)}, bf16[112,2048]{1,0:T(8,128)(2,1)S(1)}, u32[]{:S(2)}, u32[]{:S(2)}) %collective-permute-start.33) | collective-permute-done | bytes 458784 | tf_op jit(solution)/shard_map/ppermute | solution.py:65
  117.8 1.3 %apply.5 = (bf16[4,112,2048]{2,1,0:T(8,128)(2,1)}, f32[4,112,2048]{2,1,0:T(8,128)}) custom-call(bf16[112,2048]{1,0:T(8,128)(2,1)S(1)} %collective-permute-done.33.value, f32[4,112,2048]{2,1,0:T(8,128)S(1)} %copy-done, bf16[4,112,2048]{2,1,0:T(8,128)(2,1)} %get-tuple-element.40.refs_0_, ...), custom_call_target="tpu_custom_call", output_to_operand_aliasing={{0}: (2, {}), {1}: (3, {})} | custom-call | flops 688128 | bytes 2752512 | tf_op jit(solution)/shard_map/apply/pallas_call | solution.py:364
  119.1 1.3 %apply.6 = (bf16[4,112,2048]{2,1,0:T(8,128)(2,1)}, f32[4,112,2048]{2,1,0:T(8,128)}) custom-call(bf16[112,2048]{1,0:T(8,128)(2,1)S(1)} %collective-permute-done.32.value, f32[4,112,2048]{2,1,0:T(8,128)S(1)} %copy-done, bf16[4,112,2048]{2,1,0:T(8,128)(2,1)} %get-tuple-element.42.refs_0_, ...), custom_call_target="tpu_custom_call", output_to_operand_aliasing={{0}: (2, {}), {1}: (3, {})} | custom-call | flops 688128 | bytes 2752512 | tf_op jit(solution)/shard_map/apply/pallas_call | solution.py:364
  120.5 1.3 %apply.7 = (bf16[4,112,2048]{2,1,0:T(8,128)(2,1)}, f32[4,112,2048]{2,1,0:T(8,128)}) custom-call(bf16[112,2048]{1,0:T(8,128)(2,1)S(1)} %collective-permute-done.31.value, f32[4,112,2048]{2,1,0:T(8,128)S(1)} %copy-done, bf16[4,112,2048]{2,1,0:T(8,128)(2,1)} %get-tuple-element.44.refs_0_, ...), custom_call_target="tpu_custom_call", output_to_operand_aliasing={{0}: (2, {}), {1}: (3, {})} | custom-call | flops 688128 | bytes 2752512 | tf_op jit(solution)/shard_map/apply/pallas_call | solution.py:364
  (41 shorter events, 0.9 us)
Async XLA Ops:
  4.4 14.6 %collective-permute-start = (bf16[112,2048]{1,0:T(8,128)(2,1)}, bf16[112,2048]{1,0:T(8,128)(2,1)S(1)}, u32[]{:S(2)}, u32[]{:S(2)}) collective-permute-start(bf16[112,2048]{1,0:T(8,128)(2,1)} %get-tuple-element.25), channel_id=1, source_target_pairs={{0,16},{1,65},{2,18},{3,67},{4,20},{5,69},{6,22},{7,71},{8,24},{9,... | collective-permute-start | bytes 1376264 | tf_op jit(solution)/shard_map/ppermute | solution.py:65
  7.8 11.2 %collective-permute-start.1 = (bf16[112,2048]{1,0:T(8,128)(2,1)}, bf16[112,2048]{1,0:T(8,128)(2,1)S(1)}, u32[]{:S(2)}, u32[]{:S(2)}) collective-permute-start(bf16[112,2048]{1,0:T(8,128)(2,1)} %get-tuple-element.26), channel_id=1, source_target_pairs={{0,32},{1,9},{2,34},{3,11},{4,36},{5,13},{6,38},{7,15},{8,40},{9,1... | collective-permute-start | bytes 1376264 | tf_op jit(solution)/shard_map/ppermute | solution.py:65
  9.3 10.2 %collective-permute-start.2 = (bf16[112,2048]{1,0:T(8,128)(2,1)}, bf16[112,2048]{1,0:T(8,128)(2,1)S(1)}, u32[]{:S(2)}, u32[]{:S(2)}) collective-permute-start(bf16[112,2048]{1,0:T(8,128)(2,1)} %get-tuple-element.27), channel_id=1, source_target_pairs={{0,96},{1,25},{2,98},{3,27},{4,100},{5,29},{6,102},{7,31},{8,104},... | collective-permute-start | bytes 1376264 | tf_op jit(solution)/shard_map/ppermute | solution.py:65
  11.0 11.8 %collective-permute-start.3 = (bf16[112,2048]{1,0:T(8,128)(2,1)}, bf16[112,2048]{1,0:T(8,128)(2,1)S(1)}, u32[]{:S(2)}, u32[]{:S(2)}) collective-permute-start(bf16[112,2048]{1,0:T(8,128)(2,1)} %get-tuple-element.24.refs_0_), channel_id=1, source_target_pairs={{0,1},{1,0},{2,3},{3,2},{4,5},{5,4},{6,7},{7,6},{8,9},{9,8},{10,11... | collective-permute-start | bytes 1376264 | tf_op jit(solution)/shard_map/ppermute | solution.py:65
  11.0 1.0 copy-start.1
  19.0 3.8 %collective-permute-start.4 = (bf16[112,2048]{1,0:T(8,128)(2,1)S(1)}, bf16[112,2048]{1,0:T(8,128)(2,1)S(1)}, u32[]{:S(2)}, u32[]{:S(2)}) collective-permute-start(bf16[112,2048]{1,0:T(8,128)(2,1)S(1)} %collective-permute-done.refs_0_.refs_1_), channel_id=1, source_target_pairs={{0,1},{1,0},{2,3},{3,2},{4,5},{5,4},{6,7},{7,6},{8,9},{9,8},{10,11... | collective-permute-start | bytes 1376264 | tf_op jit(solution)/shard_map/ppermute | solution.py:65
  19.0 3.8 %collective-permute-start.5 = (bf16[112,2048]{1,0:T(8,128)(2,1)S(1)}, bf16[112,2048]{1,0:T(8,128)(2,1)S(1)}, u32[]{:S(2)}, u32[]{:S(2)}) collective-permute-start(bf16[112,2048]{1,0:T(8,128)(2,1)S(1)} %collective-permute-done.1.refs_1_.refs_2_), channel_id=1, source_target_pairs={{0,1},{1,0},{2,3},{3,2},{4,5},{5,4},{6,7},{7,6},{8,9},{9,8},{10,11... | collective-permute-start | bytes 1376264 | tf_op jit(solution)/shard_map/ppermute | solution.py:65
  19.5 3.3 %collective-permute-start.6 = (bf16[112,2048]{1,0:T(8,128)(2,1)S(1)}, bf16[112,2048]{1,0:T(8,128)(2,1)S(1)}, u32[]{:S(2)}, u32[]{:S(2)}) collective-permute-start(bf16[112,2048]{1,0:T(8,128)(2,1)S(1)} %collective-permute-done.2.refs_2_.refs_3_), channel_id=1, source_target_pairs={{0,1},{1,0},{2,3},{3,2},{4,5},{5,4},{6,7},{7,6},{8,9},{9,8},{10,11... | collective-permute-start | bytes 1376264 | tf_op jit(solution)/shard_map/ppermute | solution.py:65
  25.9 13.9 %collective-permute-start.16 = (bf16[544,256]{1,0:T(8,128)(2,1)S(1)}, bf16[544,256]{1,0:T(8,128)(2,1)S(1)}, u32[]{:S(2)}, u32[]{:S(2)}) collective-permute-start(bf16[544,256]{1,0:T(8,128)(2,1)S(1)} %get-tuple-element.33), channel_id=1, source_target_pairs={{0,4},{1,5},{2,6},{3,7},{4,0},{5,1},{6,2},{7,3},{8,12},{9,13},{10,... | collective-permute-start | bytes 835592 | tf_op jit(solution)/shard_map/ppermute | solution.py:65
  29.8 13.0 %collective-permute-start.17 = (bf16[544,256]{1,0:T(8,128)(2,1)S(1)}, bf16[544,256]{1,0:T(8,128)(2,1)S(1)}, u32[]{:S(2)}, u32[]{:S(2)}) collective-permute-start(bf16[544,256]{1,0:T(8,128)(2,1)S(1)} %get-tuple-element.34), channel_id=1, source_target_pairs={{0,2},{1,3},{2,4},{3,5},{4,6},{5,7},{6,0},{7,1},{8,10},{9,11},{10,... | collective-permute-start | bytes 835592 | tf_op jit(solution)/shard_map/ppermute | solution.py:65
  30.9 12.7 %collective-permute-start.18 = (bf16[544,256]{1,0:T(8,128)(2,1)S(1)}, bf16[544,256]{1,0:T(8,128)(2,1)S(1)}, u32[]{:S(2)}, u32[]{:S(2)}) collective-permute-start(bf16[544,256]{1,0:T(8,128)(2,1)S(1)} %get-tuple-element.35), channel_id=1, source_target_pairs={{0,6},{1,7},{2,0},{3,1},{4,2},{5,3},{6,4},{7,5},{8,14},{9,15},{10,... | collective-permute-start | bytes 835592 | tf_op jit(solution)/shard_map/ppermute | solution.py:65
  33.1 17.7 %collective-permute-start.7 = (bf16[544,256]{1,0:T(8,128)(2,1)S(1)}, bf16[544,256]{1,0:T(8,128)(2,1)S(1)}, u32[]{:S(2)}, u32[]{:S(2)}) collective-permute-start(bf16[544,256]{1,0:T(8,128)(2,1)S(1)} %get-tuple-element.29), channel_id=1, source_target_pairs={{0,80},{1,81},{2,82},{3,83},{4,84},{5,85},{6,86},{7,87},{8,88},{9,... | collective-permute-start | bytes 835592 | tf_op jit(solution)/shard_map/ppermute | solution.py:65
  37.9 14.8 %collective-permute-start.8 = (bf16[544,256]{1,0:T(8,128)(2,1)S(1)}, bf16[544,256]{1,0:T(8,128)(2,1)S(1)}, u32[]{:S(2)}, u32[]{:S(2)}) collective-permute-start(bf16[544,256]{1,0:T(8,128)(2,1)S(1)} %get-tuple-element.30), channel_id=1, source_target_pairs={{0,56},{1,57},{2,58},{3,59},{4,60},{5,61},{6,62},{7,63},{8,32},{9,... | collective-permute-start | bytes 835592 | tf_op jit(solution)/shard_map/ppermute | solution.py:65
  39.8 12.9 %collective-permute-start.9 = (bf16[544,256]{1,0:T(8,128)(2,1)S(1)}, bf16[544,256]{1,0:T(8,128)(2,1)S(1)}, u32[]{:S(2)}, u32[]{:S(2)}) collective-permute-start(bf16[544,256]{1,0:T(8,128)(2,1)S(1)} %get-tuple-element.31), channel_id=1, source_target_pairs={{0,104},{1,105},{2,106},{3,107},{4,108},{5,109},{6,110},{7,111},{8... | collective-permute-start | bytes 835592 | tf_op jit(solution)/shard_map/ppermute | solution.py:65
  43.7 20.2 %collective-permute-start.19 = (bf16[544,256]{1,0:T(8,128)(2,1)S(1)}, bf16[544,256]{1,0:T(8,128)(2,1)S(1)}, u32[]{:S(2)}, u32[]{:S(2)}) collective-permute-start(bf16[544,256]{1,0:T(8,128)(2,1)S(1)} %add_convert_fusion.1), channel_id=1, source_target_pairs={{0,80},{1,81},{2,82},{3,83},{4,84},{5,85},{6,86},{7,87},{8,88},{9,... | collective-permute-start | bytes 835592 | tf_op jit(solution)/shard_map/ppermute | solution.py:65
  48.4 15.6 %collective-permute-start.20 = (bf16[544,256]{1,0:T(8,128)(2,1)S(1)}, bf16[544,256]{1,0:T(8,128)(2,1)S(1)}, u32[]{:S(2)}, u32[]{:S(2)}) collective-permute-start(bf16[544,256]{1,0:T(8,128)(2,1)S(1)} %add_convert_fusion.1), channel_id=1, source_target_pairs={{0,56},{1,57},{2,58},{3,59},{4,60},{5,61},{6,62},{7,63},{8,32},{9,... | collective-permute-start | bytes 835592 | tf_op jit(solution)/shard_map/ppermute | solution.py:65
  50.8 16.1 %collective-permute-start.21 = (bf16[544,256]{1,0:T(8,128)(2,1)S(1)}, bf16[544,256]{1,0:T(8,128)(2,1)S(1)}, u32[]{:S(2)}, u32[]{:S(2)}) collective-permute-start(bf16[544,256]{1,0:T(8,128)(2,1)S(1)} %add_convert_fusion.1), channel_id=1, source_target_pairs={{0,104},{1,105},{2,106},{3,107},{4,108},{5,109},{6,110},{7,111},{8... | collective-permute-start | bytes 835592 | tf_op jit(solution)/shard_map/ppermute | solution.py:65
  52.9 14.6 %collective-permute-start.10 = (bf16[544,256]{1,0:T(8,128)(2,1)S(1)}, bf16[544,256]{1,0:T(8,128)(2,1)S(1)}, u32[]{:S(2)}, u32[]{:S(2)}) collective-permute-start(bf16[544,256]{1,0:T(8,128)(2,1)S(1)} %add_convert_fusion.3), channel_id=1, source_target_pairs={{0,4},{1,5},{2,6},{3,7},{4,0},{5,1},{6,2},{7,3},{8,12},{9,13},{10,... | collective-permute-start | bytes 835592 | tf_op jit(solution)/shard_map/ppermute | solution.py:65
  54.8 12.7 %collective-permute-start.11 = (bf16[544,256]{1,0:T(8,128)(2,1)S(1)}, bf16[544,256]{1,0:T(8,128)(2,1)S(1)}, u32[]{:S(2)}, u32[]{:S(2)}) collective-permute-start(bf16[544,256]{1,0:T(8,128)(2,1)S(1)} %add_convert_fusion.3), channel_id=1, source_target_pairs={{0,2},{1,3},{2,4},{3,5},{4,6},{5,7},{6,0},{7,1},{8,10},{9,11},{10,... | collective-permute-start | bytes 835592 | tf_op jit(solution)/shard_map/ppermute | solution.py:65
  64.0 8.7 %collective-permute-start.12 = (bf16[544,256]{1,0:T(8,128)(2,1)S(1)}, bf16[544,256]{1,0:T(8,128)(2,1)S(1)}, u32[]{:S(2)}, u32[]{:S(2)}) collective-permute-start(bf16[544,256]{1,0:T(8,128)(2,1)S(1)} %add_convert_fusion.3), channel_id=1, source_target_pairs={{0,6},{1,7},{2,0},{3,1},{4,2},{5,3},{6,4},{7,5},{8,14},{9,15},{10,... | collective-permute-start | bytes 835592 | tf_op jit(solution)/shard_map/ppermute | solution.py:65
  67.1 25.6 %copy-start.2 = (bf16[112,2048]{1,0:T(8,128)(2,1)S(1)}, bf16[112,2048]{1,0:T(8,128)(2,1)}, u32[]{:S(2)}) copy-start(bf16[112,2048]{1,0:T(8,128)(2,1)} %get-tuple-element.24.refs_0_) | copy-start | bytes 1376260
  67.1 14.9 %collective-permute-start.23 = (bf16[544,256]{1,0:T(8,128)(2,1)S(1)}, bf16[544,256]{1,0:T(8,128)(2,1)S(1)}, u32[]{:S(2)}, u32[]{:S(2)}) collective-permute-start(bf16[544,256]{1,0:T(8,128)(2,1)S(1)} %add_convert_fusion.refs_8_), channel_id=1, source_target_pairs={{0,4},{1,5},{2,6},{3,7},{4,0},{5,1},{6,2},{7,3},{8,12},{9,13},{10,... | collective-permute-start | bytes 835592 | tf_op jit(solution)/shard_map/ppermute | solution.py:65
  72.8 13.8 %collective-permute-start.14 = (bf16[544,256]{1,0:T(8,128)(2,1)S(1)}, bf16[544,256]{1,0:T(8,128)(2,1)S(1)}, u32[]{:S(2)}, u32[]{:S(2)}) collective-permute-start(bf16[544,256]{1,0:T(8,128)(2,1)S(1)} %add_convert_fusion.2.refs_4_), channel_id=1, source_target_pairs={{0,80},{1,81},{2,82},{3,83},{4,84},{5,85},{6,86},{7,87},{8,88},{9,... | collective-permute-start | bytes 835592 | tf_op jit(solution)/shard_map/ppermute | solution.py:65
  75.6 11.1 %collective-permute-start.24 = (bf16[544,256]{1,0:T(8,128)(2,1)S(1)}, bf16[544,256]{1,0:T(8,128)(2,1)S(1)}, u32[]{:S(2)}, u32[]{:S(2)}) collective-permute-start(bf16[544,256]{1,0:T(8,128)(2,1)S(1)} %add_convert_fusion.refs_8_), channel_id=1, source_target_pairs={{0,6},{1,7},{2,0},{3,1},{4,2},{5,3},{6,4},{7,5},{8,14},{9,15},{10,... | collective-permute-start | bytes 835592 | tf_op jit(solution)/shard_map/ppermute | solution.py:65
  75.6 11.6 %collective-permute-start.22 = (bf16[544,256]{1,0:T(8,128)(2,1)S(1)}, bf16[544,256]{1,0:T(8,128)(2,1)S(1)}, u32[]{:S(2)}, u32[]{:S(2)}) collective-permute-start(bf16[544,256]{1,0:T(8,128)(2,1)S(1)} %add_convert_fusion.refs_8_), channel_id=1, source_target_pairs={{0,2},{1,3},{2,4},{3,5},{4,6},{5,7},{6,0},{7,1},{8,10},{9,11},{10,... | collective-permute-start | bytes 835592 | tf_op jit(solution)/shard_map/ppermute | solution.py:65
  77.6 11.0 %collective-permute-start.15 = (bf16[544,256]{1,0:T(8,128)(2,1)S(1)}, bf16[544,256]{1,0:T(8,128)(2,1)S(1)}, u32[]{:S(2)}, u32[]{:S(2)}) collective-permute-start(bf16[544,256]{1,0:T(8,128)(2,1)S(1)} %add_convert_fusion.2.refs_4_), channel_id=1, source_target_pairs={{0,104},{1,105},{2,106},{3,107},{4,108},{5,109},{6,110},{7,111},{8... | collective-permute-start | bytes 835592 | tf_op jit(solution)/shard_map/ppermute | solution.py:65
  82.0 8.7 %collective-permute-start.13 = (bf16[544,256]{1,0:T(8,128)(2,1)S(1)}, bf16[544,256]{1,0:T(8,128)(2,1)S(1)}, u32[]{:S(2)}, u32[]{:S(2)}) collective-permute-start(bf16[544,256]{1,0:T(8,128)(2,1)S(1)} %add_convert_fusion.2.refs_4_), channel_id=1, source_target_pairs={{0,56},{1,57},{2,58},{3,59},{4,60},{5,61},{6,62},{7,63},{8,32},{9,... | collective-permute-start | bytes 835592 | tf_op jit(solution)/shard_map/ppermute | solution.py:65
  86.7 6.0 %collective-permute-start.28 = (bf16[1088,256]{1,0:T(8,128)(2,1)S(1)}, bf16[1088,256]{1,0:T(8,128)(2,1)S(1)}, u32[]{:S(2)}, u32[]{:S(2)}) collective-permute-start(bf16[1088,256]{1,0:T(8,128)(2,1)S(1)} %pad_maximum_fusion.1), channel_id=1, source_target_pairs={{0,1},{1,0},{2,3},{3,2},{4,5},{5,4},{6,7},{7,6},{8,9},{9,8},{10,11... | collective-permute-start | bytes 1671176 | tf_op jit(solution)/shard_map/ppermute | solution.py:65
  86.7 4.0 %collective-permute-start.29 = (bf16[544,256]{1,0:T(8,128)(2,1)S(1)}, bf16[544,256]{1,0:T(8,128)(2,1)S(1)}, u32[]{:S(2)}, u32[]{:S(2)}) collective-permute-start(bf16[544,256]{1,0:T(8,128)(2,1)S(1)} %collective-permute-done.24.refs_11_), channel_id=1, source_target_pairs={{0,1},{1,0},{2,3},{3,2},{4,5},{5,4},{6,7},{7,6},{8,9},{9,8},{10,11... | collective-permute-start | bytes 835592 | tf_op jit(solution)/shard_map/ppermute | solution.py:65
  87.2 19.3 %copy-start = (f32[4,112,2048]{2,1,0:T(8,128)S(1)}, f32[4,112,2048]{2,1,0:T(8,128)}, u32[]{:S(2)}) copy-start(f32[4,112,2048]{2,1,0:T(8,128)} %weight.7) | copy-start | bytes 11010052
  87.2 5.4 %collective-permute-start.25 = (bf16[1088,256]{1,0:T(8,128)(2,1)S(1)}, bf16[1088,256]{1,0:T(8,128)(2,1)S(1)}, u32[]{:S(2)}, u32[]{:S(2)}) collective-permute-start(bf16[1088,256]{1,0:T(8,128)(2,1)S(1)} %pad_maximum_fusion), channel_id=1, source_target_pairs={{0,1},{1,0},{2,3},{3,2},{4,5},{5,4},{6,7},{7,6},{8,9},{9,8},{10,11... | collective-permute-start | bytes 1671176 | tf_op jit(solution)/shard_map/ppermute | solution.py:65
  88.7 2.5 %collective-permute-start.30 = (bf16[544,256]{1,0:T(8,128)(2,1)S(1)}, bf16[544,256]{1,0:T(8,128)(2,1)S(1)}, u32[]{:S(2)}, u32[]{:S(2)}) collective-permute-start(bf16[544,256]{1,0:T(8,128)(2,1)S(1)} %collective-permute-done.22.refs_9_), channel_id=1, source_target_pairs={{0,1},{1,0},{2,3},{3,2},{4,5},{5,4},{6,7},{7,6},{8,9},{9,8},{10,11... | collective-permute-start | bytes 835592 | tf_op jit(solution)/shard_map/ppermute | solution.py:65
  90.7 1.6 %collective-permute-start.26 = (bf16[544,256]{1,0:T(8,128)(2,1)S(1)}, bf16[544,256]{1,0:T(8,128)(2,1)S(1)}, u32[]{:S(2)}, u32[]{:S(2)}) collective-permute-start(bf16[544,256]{1,0:T(8,128)(2,1)S(1)} %collective-permute-done.15.refs_7_), channel_id=1, source_target_pairs={{0,1},{1,0},{2,3},{3,2},{4,5},{5,4},{6,7},{7,6},{8,9},{9,8},{10,11... | collective-permute-start | bytes 835592 | tf_op jit(solution)/shard_map/ppermute | solution.py:65
  90.7 2.0 %collective-permute-start.27 = (bf16[544,256]{1,0:T(8,128)(2,1)S(1)}, bf16[544,256]{1,0:T(8,128)(2,1)S(1)}, u32[]{:S(2)}, u32[]{:S(2)}) collective-permute-start(bf16[544,256]{1,0:T(8,128)(2,1)S(1)} %collective-permute-done.13.refs_5_), channel_id=1, source_target_pairs={{0,1},{1,0},{2,3},{3,2},{4,5},{5,4},{6,7},{7,6},{8,9},{9,8},{10,11... | collective-permute-start | bytes 835592 | tf_op jit(solution)/shard_map/ppermute | solution.py:65
  103.0 14.9 %collective-permute-start.33 = (bf16[112,2048]{1,0:T(8,128)(2,1)S(1)}, bf16[112,2048]{1,0:T(8,128)(2,1)S(1)}, u32[]{:S(2)}, u32[]{:S(2)}) collective-permute-start(bf16[112,2048]{1,0:T(8,128)(2,1)S(1)} %get-tuple-element.38), channel_id=1, source_target_pairs={{16,0},{65,1},{18,2},{67,3},{20,4},{69,5},{22,6},{71,7},{24,8},{73... | collective-permute-start | bytes 1376264 | tf_op jit(solution)/shard_map/ppermute | solution.py:65
  104.5 14.6 %collective-permute-start.32 = (bf16[112,2048]{1,0:T(8,128)(2,1)S(1)}, bf16[112,2048]{1,0:T(8,128)(2,1)S(1)}, u32[]{:S(2)}, u32[]{:S(2)}) collective-permute-start(bf16[112,2048]{1,0:T(8,128)(2,1)S(1)} %get-tuple-element.37), channel_id=1, source_target_pairs={{32,0},{9,1},{34,2},{11,3},{36,4},{13,5},{38,6},{15,7},{40,8},{17,... | collective-permute-start | bytes 1376264 | tf_op jit(solution)/shard_map/ppermute | solution.py:65
  104.5 16.0 %collective-permute-start.31 = (bf16[112,2048]{1,0:T(8,128)(2,1)S(1)}, bf16[112,2048]{1,0:T(8,128)(2,1)S(1)}, u32[]{:S(2)}, u32[]{:S(2)}) collective-permute-start(bf16[112,2048]{1,0:T(8,128)(2,1)S(1)} %get-tuple-element.36), channel_id=1, source_target_pairs={{96,0},{25,1},{98,2},{27,3},{100,4},{29,5},{102,6},{31,7},{104,8},... | collective-permute-start | bytes 1376264 | tf_op jit(solution)/shard_map/ppermute | solution.py:65

commit v5 on v4

--- a/solution.py
+++ b/solution.py
@@ -70,18 +70,18 @@
     return col % 2, x, col // 2 % 4, (x + col // 8) % 4
 
 
-def live_kernel(lengths, momentum, o0, o1, o2, o3, rows, sems):
+def live_kernel(which, lengths, momentum, *refs):
     home = places()[3]
-    outs = (o0, o1, o2, o3)
-    experts = [lax.rem(home + d, 4) for d in OFFSETS]
+    outs, (rows, sems) = refs[:-2], refs[-2:]
+    experts = [lax.rem(home + OFFSETS[i], 4) for i in which]
     loads = [
         pltpu.make_async_copy(momentum.at[experts[d]], rows.at[d], sems.at[d])
-        for d in range(4)
+        for d in range(len(which))
     ]
     for load in loads:
         load.start()
     lane = lax.broadcasted_iota(jnp.int32, (1, 4), 1)
-    for d in (1, 2, 3, 0):
+    for d in range(len(which)):
         loads[d].wait()
         slot = lax.broadcasted_iota(jnp.int32, (CAP, 128), 0)
         keep = slot < jnp.sum(jnp.where(lane == experts[d], lengths[...], 0))
@@ -91,20 +91,20 @@
             outs[d][:, at:at + 128] = value * keep
 
 
-def live(lengths, momentum):
+def live(which, lengths, momentum):
     return pl.pallas_call(
-        live_kernel,
-        out_shape=[jax.ShapeDtypeStruct((CAP, R), jnp.bfloat16)] * 4,
+        functools.partial(live_kernel, which),
+        out_shape=[jax.ShapeDtypeStruct((CAP, R), jnp.bfloat16)] * len(which),
         in_specs=[
             pl.BlockSpec(memory_space=pltpu.VMEM),
             pl.BlockSpec(memory_space=pltpu.HBM),
         ],
-        out_specs=[pl.BlockSpec(memory_space=pltpu.VMEM)] * 4,
+        out_specs=[pl.BlockSpec(memory_space=pltpu.VMEM)] * len(which),
         scratch_shapes=[
-            pltpu.VMEM((4, CAP, R), jnp.bfloat16),
-            pltpu.SemaphoreType.DMA((4,)),
+            pltpu.VMEM((len(which), CAP, R), jnp.bfloat16),
+            pltpu.SemaphoreType.DMA((len(which),)),
         ],
-        compiler_params=pltpu.CompilerParams(vmem_limit_bytes=61 << 20),
+        compiler_params=pltpu.CompilerParams(vmem_limit_bytes=(61 if len(which) == 1 else 16) << 20),
         name="live",
     )(lengths, momentum)
 
@@ -392,7 +392,9 @@
 
 def on_device(momentum, lengths, weight):
     routes = {d: to_expert(OFFSETS[d]) for d in (1, 2, 3)}
-    rows = live(lengths.reshape(1, 4), momentum)
+    (ahead,) = live((1,), lengths.reshape(1, 4), momentum)
+    second, third, own = live((2, 3, 0), lengths.reshape(1, 4), momentum)
+    rows = [own, ahead, second, third]
     rows = [rows[0]] + [shift(rows[d], routes[d]) for d in (1, 2, 3)]
     other_rows = [shift(part, OTHER_CORE) for part in rows]
 

time: 122 us -> 121 us (level)
  waiting for transfers between devices: 42.1 us -> 37.1 us
  starting transfers between devices: 50.9 us -> 52.8 us
    ppermute x34, waiting for transfers between devices: 42.1 us -> 37.1 us  [shift(): return lax.ppermute(value, AXES, steps)]
    ppermute x34, starting transfers between devices: 50.9 us -> 52.8 us  [shift(): return lax.ppermute(value, AXES, steps)]
    pallas_call x1 -> x2, Pallas kernels: 3.78 us -> 4.22 us  [live(): pl.pallas_call(functools.partial(live_kernel, which), out_shape=[jax.Shap...]
  transfers between devices with their start and end apart: 34 -> 34, of which waited for: 13 -> 16; matrix products, arithmetic and copies ran while one was open for 1% -> 1% of each run, Pallas kernels for 6% -> 9%
where the time goes in v5:
time: 121 us; the launch traced here: 120 us
  starting transfers between devices  52.8 us (44%)
  waiting for transfers between devices  37.1 us (31%)
  Pallas kernels  26.7 us (22%)
  local copies, waits for them, and re-layouts  2.16 us (2%)
    ppermute x34, starting transfers between devices, shift(): return lax.ppermute(value, AXES, steps)  52.8 us
    ppermute x34, waiting for transfers between devices, shift(): return lax.ppermute(value, AXES, steps)  37.1 us
    pallas_call x1, Pallas kernels, update(): pl.pallas_call(update_kernel, out_shape=[jax.ShapeDtypeStruct((CAP, R), j...  10.2 us
    pallas_call x3, Pallas kernels, gram(): pl.pallas_call(functools.partial(gram_kernel, count, before is None, last...  7.07 us
    pallas_call x4, Pallas kernels, apply(): pl.pallas_call(functools.partial(apply_kernel, d), out_shape=[jax.ShapeDt...  5.21 us
    pallas_call x2, Pallas kernels, live(): pl.pallas_call(functools.partial(live_kernel, which), out_shape=[jax.Shap...  4.22 us
  transfers between devices with their start and end apart: 34, of which 16 were waited for; matrix products, arithmetic and copies ran while one was open for 1% of the time, Pallas kernels for 9%

profile of v5, /device:TPU:0, one launch (start us, length us, event | category | flops | bytes accessed | tf_op | source)
XLA Modules:
  0.0 120.5 jit_solution(4311823275092158919)
XLA Ops:
  0.6 1.5 %copy-done.1 = bf16[4,112,2048]{2,1,0:T(8,128)(2,1)S(1)} copy-done((bf16[4,112,2048]{2,1,0:T(8,128)(2,1)S(1)}, bf16[4,112,2048]{2,1,0:T(8,128)(2,1)}, u32[]{:S(2)}) %copy-start.1) | copy-done | bytes 1835032
  2.1 0.7 copy-done.2
  2.8 1.5 %live.2 = (bf16[112,2048]{1,0:T(8,128)(2,1)S(1)}, bf16[112,2048]{1,0:T(8,128)(2,1)S(1)}, bf16[112,2048]{1,0:T(8,128)(2,1)S(1)}) custom-call(s32[1,4]{1,0:T(1,128)S(1)} %bitcast.2, bf16[4,112,2048]{2,1,0:T(8,128)(2,1)S(1)} %copy-done.1), custom_call_target="tpu_custom_call" | custom-call | tf_op jit(solution)/shard_map/live/pallas_call | solution.py:95
  4.3 1.6 %collective-permute-start.1 = (bf16[112,2048]{1,0:T(8,128)(2,1)S(1)}, bf16[112,2048]{1,0:T(8,128)(2,1)S(1)}, u32[]{:S(2)}, u32[]{:S(2)}) collective-permute-start(bf16[112,2048]{1,0:T(8,128)(2,1)S(1)} %get-tuple-element.24), channel_id=1, source_target_pairs={{0,32},{1,9},{2,34},{3,11},{4,36},{5,13},{6,38},{7,15},{8,40},{9,1... | collective-permute-start | bytes 1376264 | tf_op jit(solution)/shard_map/ppermute | solution.py:65
  6.0 1.7 %collective-permute-start.2 = (bf16[112,2048]{1,0:T(8,128)(2,1)S(1)}, bf16[112,2048]{1,0:T(8,128)(2,1)S(1)}, u32[]{:S(2)}, u32[]{:S(2)}) collective-permute-start(bf16[112,2048]{1,0:T(8,128)(2,1)S(1)} %get-tuple-element.25), channel_id=1, source_target_pairs={{0,96},{1,25},{2,98},{3,27},{4,100},{5,29},{6,102},{7,31},{8,104},... | collective-permute-start | bytes 1376264 | tf_op jit(solution)/shard_map/ppermute | solution.py:65
  7.6 2.7 %live.3 = bf16[112,2048]{1,0:T(8,128)(2,1)} custom-call(s32[1,4]{1,0:T(1,128)} %bitcast.1, bf16[4,112,2048]{2,1,0:T(8,128)(2,1)} %momentum.3), custom_call_target="tpu_custom_call" | custom-call | tf_op jit(solution)/shard_map/live/pallas_call | solution.py:95
  10.3 3.4 %collective-permute-start = (bf16[112,2048]{1,0:T(8,128)(2,1)}, bf16[112,2048]{1,0:T(8,128)(2,1)S(1)}, u32[]{:S(2)}, u32[]{:S(2)}) collective-permute-start(bf16[112,2048]{1,0:T(8,128)(2,1)} %live.3), channel_id=1, source_target_pairs={{0,16},{1,65},{2,18},{3,67},{4,20},{5,69},{6,22},{7,71},{8,24},{9,... | collective-permute-start | bytes 1376264 | tf_op jit(solution)/shard_map/ppermute | solution.py:65
  13.7 1.1 gram.3.refs_3_
  14.8 0.6 collective-permute-start.5
  15.5 5.1 %collective-permute-done.refs_0_.refs_1_ = bf16[112,2048]{1,0:T(8,128)(2,1)S(1)} collective-permute-done((bf16[112,2048]{1,0:T(8,128)(2,1)}, bf16[112,2048]{1,0:T(8,128)(2,1)S(1)}, u32[]{:S(2)}, u32[]{:S(2)}) %collective-permute-start) | collective-permute-done | bytes 458784 | tf_op jit(solution)/shard_map/ppermute | solution.py:65
  20.6 2.9 %gram.4.refs_4_ = f32[4608,256]{1,0:T(8,128)S(1)} custom-call(bf16[112,2048]{1,0:T(8,128)(2,1)S(1)} %collective-permute-done.refs_0_.refs_1_, bf16[112,2048]{1,0:T(8,128)(2,1)S(1)} %collective-permute-done.1.refs_1_.refs_2_, bf16[112,2048]{1,0:T(8,128)(2,1)S(1)} %collective-permute-done.2.refs_2_.refs_3_, ...), custom_call_target="tpu_custom_call", output_to_operand_aliasing={{}: (3, {})} | custom-call | flops 31708938240 | bytes 10813440 | tf_op jit(solution)/shard_map/gram/pallas_call | solution.py:193
  23.6 3.1 %gram.5 = (bf16[544,256]{1,0:T(8,128)(2,1)S(1)}, bf16[544,256]{1,0:T(8,128)(2,1)S(1)}, bf16[544,256]{1,0:T(8,128)(2,1)S(1)}, bf16[544,256]{1,0:T(8,128)(2,1)S(1)...) custom-call(bf16[112,2048]{1,0:T(8,128)(2,1)S(1)} %collective-permut, ...), custom_call_target="tpu_custom_call" | custom-call | flops 1056964608 | bytes 11272192 | tf_op jit(solution)/shard_map/gram/pallas_call | solution.py:193
  26.6 4.0 %collective-permute-start.16 = (bf16[544,256]{1,0:T(8,128)(2,1)S(1)}, bf16[544,256]{1,0:T(8,128)(2,1)S(1)}, u32[]{:S(2)}, u32[]{:S(2)}) collective-permute-start(bf16[544,256]{1,0:T(8,128)(2,1)S(1)} %get-tuple-element.31), channel_id=1, source_target_pairs={{0,4},{1,5},{2,6},{3,7},{4,0},{5,1},{6,2},{7,3},{8,12},{9,13},{10,... | collective-permute-start | bytes 835592 | tf_op jit(solution)/shard_map/ppermute | solution.py:65
  30.7 1.0 collective-permute-start.17
  31.7 2.2 %collective-permute-start.18 = (bf16[544,256]{1,0:T(8,128)(2,1)S(1)}, bf16[544,256]{1,0:T(8,128)(2,1)S(1)}, u32[]{:S(2)}, u32[]{:S(2)}) collective-permute-start(bf16[544,256]{1,0:T(8,128)(2,1)S(1)} %get-tuple-element.33), channel_id=1, source_target_pairs={{0,6},{1,7},{2,0},{3,1},{4,2},{5,3},{6,4},{7,5},{8,14},{9,15},{10,... | collective-permute-start | bytes 835592 | tf_op jit(solution)/shard_map/ppermute | solution.py:65
  33.9 4.4 %collective-permute-start.7 = (bf16[544,256]{1,0:T(8,128)(2,1)S(1)}, bf16[544,256]{1,0:T(8,128)(2,1)S(1)}, u32[]{:S(2)}, u32[]{:S(2)}) collective-permute-start(bf16[544,256]{1,0:T(8,128)(2,1)S(1)} %get-tuple-element.27), channel_id=1, source_target_pairs={{0,80},{1,81},{2,82},{3,83},{4,84},{5,85},{6,86},{7,87},{8,88},{9,... | collective-permute-start | bytes 835592 | tf_op jit(solution)/shard_map/ppermute | solution.py:65
  38.4 1.7 %collective-permute-start.8 = (bf16[544,256]{1,0:T(8,128)(2,1)S(1)}, bf16[544,256]{1,0:T(8,128)(2,1)S(1)}, u32[]{:S(2)}, u32[]{:S(2)}) collective-permute-start(bf16[544,256]{1,0:T(8,128)(2,1)S(1)} %get-tuple-element.28), channel_id=1, source_target_pairs={{0,56},{1,57},{2,58},{3,59},{4,60},{5,61},{6,62},{7,63},{8,32},{9,... | collective-permute-start | bytes 835592 | tf_op jit(solution)/shard_map/ppermute | solution.py:65
  40.1 2.4 %collective-permute-start.9 = (bf16[544,256]{1,0:T(8,128)(2,1)S(1)}, bf16[544,256]{1,0:T(8,128)(2,1)S(1)}, u32[]{:S(2)}, u32[]{:S(2)}) collective-permute-start(bf16[544,256]{1,0:T(8,128)(2,1)S(1)} %get-tuple-element.29), channel_id=1, source_target_pairs={{0,104},{1,105},{2,106},{3,107},{4,108},{5,109},{6,110},{7,111},{8... | collective-permute-start | bytes 835592 | tf_op jit(solution)/shard_map/ppermute | solution.py:65
  42.5 1.5 %collective-permute-done.17 = bf16[544,256]{1,0:T(8,128)(2,1)S(1)} collective-permute-done((bf16[544,256]{1,0:T(8,128)(2,1)S(1)}, bf16[544,256]{1,0:T(8,128)(2,1)S(1)}, u32[]{:S(2)}, u32[]{:S(2)}) %collective-permute-start.17) | collective-permute-done | bytes 278560 | tf_op jit(solution)/shard_map/ppermute | solution.py:65
  44.0 0.8 collective-permute-done.18
  44.9 4.5 %collective-permute-start.19 = (bf16[544,256]{1,0:T(8,128)(2,1)S(1)}, bf16[544,256]{1,0:T(8,128)(2,1)S(1)}, u32[]{:S(2)}, u32[]{:S(2)}) collective-permute-start(bf16[544,256]{1,0:T(8,128)(2,1)S(1)} %add_convert_fusion.1), channel_id=1, source_target_pairs={{0,80},{1,81},{2,82},{3,83},{4,84},{5,85},{6,86},{7,87},{8,88},{9,... | collective-permute-start | bytes 835592 | tf_op jit(solution)/shard_map/ppermute | solution.py:65
  49.4 1.2 collective-permute-start.20
  50.6 2.9 %collective-permute-start.21 = (bf16[544,256]{1,0:T(8,128)(2,1)S(1)}, bf16[544,256]{1,0:T(8,128)(2,1)S(1)}, u32[]{:S(2)}, u32[]{:S(2)}) collective-permute-start(bf16[544,256]{1,0:T(8,128)(2,1)S(1)} %add_convert_fusion.1), channel_id=1, source_target_pairs={{0,104},{1,105},{2,106},{3,107},{4,108},{5,109},{6,110},{7,111},{8... | collective-permute-start | bytes 835592 | tf_op jit(solution)/shard_map/ppermute | solution.py:65
  53.7 2.1 %collective-permute-start.10 = (bf16[544,256]{1,0:T(8,128)(2,1)S(1)}, bf16[544,256]{1,0:T(8,128)(2,1)S(1)}, u32[]{:S(2)}, u32[]{:S(2)}) collective-permute-start(bf16[544,256]{1,0:T(8,128)(2,1)S(1)} %add_convert_fusion.3), channel_id=1, source_target_pairs={{0,4},{1,5},{2,6},{3,7},{4,0},{5,1},{6,2},{7,3},{8,12},{9,13},{10,... | collective-permute-start | bytes 835592 | tf_op jit(solution)/shard_map/ppermute | solution.py:65
  55.8 1.5 %collective-permute-start.11 = (bf16[544,256]{1,0:T(8,128)(2,1)S(1)}, bf16[544,256]{1,0:T(8,128)(2,1)S(1)}, u32[]{:S(2)}, u32[]{:S(2)}) collective-permute-start(bf16[544,256]{1,0:T(8,128)(2,1)S(1)} %add_convert_fusion.3), channel_id=1, source_target_pairs={{0,2},{1,3},{2,4},{3,5},{4,6},{5,7},{6,0},{7,1},{8,10},{9,11},{10,... | collective-permute-start | bytes 835592 | tf_op jit(solution)/shard_map/ppermute | solution.py:65
  57.3 6.5 %collective-permute-done.19 = bf16[544,256]{1,0:T(8,128)(2,1)S(1)} collective-permute-done((bf16[544,256]{1,0:T(8,128)(2,1)S(1)}, bf16[544,256]{1,0:T(8,128)(2,1)S(1)}, u32[]{:S(2)}, u32[]{:S(2)}) %collective-permute-start.19) | collective-permute-done | bytes 278560 | tf_op jit(solution)/shard_map/ppermute | solution.py:65
  63.8 1.0 collective-permute-done.20
  64.8 2.0 %collective-permute-done.21 = bf16[544,256]{1,0:T(8,128)(2,1)S(1)} collective-permute-done((bf16[544,256]{1,0:T(8,128)(2,1)S(1)}, bf16[544,256]{1,0:T(8,128)(2,1)S(1)}, u32[]{:S(2)}, u32[]{:S(2)}) %collective-permute-start.21) | collective-permute-done | bytes 278560 | tf_op jit(solution)/shard_map/ppermute | solution.py:65
  67.2 1.6 %collective-permute-done.11 = bf16[544,256]{1,0:T(8,128)(2,1)S(1)} collective-permute-done((bf16[544,256]{1,0:T(8,128)(2,1)S(1)}, bf16[544,256]{1,0:T(8,128)(2,1)S(1)}, u32[]{:S(2)}, u32[]{:S(2)}) %collective-permute-start.11) | collective-permute-done | bytes 278560 | tf_op jit(solution)/shard_map/ppermute | solution.py:65
  68.8 3.6 %collective-permute-done.12 = bf16[544,256]{1,0:T(8,128)(2,1)S(1)} collective-permute-done((bf16[544,256]{1,0:T(8,128)(2,1)S(1)}, bf16[544,256]{1,0:T(8,128)(2,1)S(1)}, u32[]{:S(2)}, u32[]{:S(2)}) %collective-permute-start.12) | collective-permute-done | bytes 278560 | tf_op jit(solution)/shard_map/ppermute | solution.py:65
  72.6 4.4 %collective-permute-start.14 = (bf16[544,256]{1,0:T(8,128)(2,1)S(1)}, bf16[544,256]{1,0:T(8,128)(2,1)S(1)}, u32[]{:S(2)}, u32[]{:S(2)}) collective-permute-start(bf16[544,256]{1,0:T(8,128)(2,1)S(1)} %add_convert_fusion.2.refs_4_), channel_id=1, source_target_pairs={{0,80},{1,81},{2,82},{3,83},{4,84},{5,85},{6,86},{7,87},{8,88},{9,... | collective-permute-start | bytes 835592 | tf_op jit(solution)/shard_map/ppermute | solution.py:65
  77.0 3.9 %collective-permute-start.24 = (bf16[544,256]{1,0:T(8,128)(2,1)S(1)}, bf16[544,256]{1,0:T(8,128)(2,1)S(1)}, u32[]{:S(2)}, u32[]{:S(2)}) collective-permute-start(bf16[544,256]{1,0:T(8,128)(2,1)S(1)} %add_convert_fusion.refs_8_), channel_id=1, source_target_pairs={{0,6},{1,7},{2,0},{3,1},{4,2},{5,3},{6,4},{7,5},{8,14},{9,15},{10,... | collective-permute-start | bytes 835592 | tf_op jit(solution)/shard_map/ppermute | solution.py:65
  80.9 4.1 %collective-permute-start.13 = (bf16[544,256]{1,0:T(8,128)(2,1)S(1)}, bf16[544,256]{1,0:T(8,128)(2,1)S(1)}, u32[]{:S(2)}, u32[]{:S(2)}) collective-permute-start(bf16[544,256]{1,0:T(8,128)(2,1)S(1)} %add_convert_fusion.2.refs_4_), channel_id=1, source_target_pairs={{0,56},{1,57},{2,58},{3,59},{4,60},{5,61},{6,62},{7,63},{8,32},{9,... | collective-permute-start | bytes 835592 | tf_op jit(solution)/shard_map/ppermute | solution.py:65
  85.1 0.7 collective-permute-done.14.refs_6_
  85.9 0.5 collective-permute-start.29
  86.4 2.3 %collective-permute-done.22.refs_9_ = bf16[544,256]{1,0:T(8,128)(2,1)S(1)} collective-permute-done((bf16[544,256]{1,0:T(8,128)(2,1)S(1)}, bf16[544,256]{1,0:T(8,128)(2,1)S(1)}, u32[]{:S(2)}, u32[]{:S(2)}) %collective-permute-start.22) | collective-permute-done | bytes 278560 | tf_op jit(solution)/shard_map/ppermute | solution.py:65
  88.7 0.9 collective-permute-done.15.refs_7_
  89.7 0.4 collective-permute-start.26
  90.2 1.0 collective-permute-done.30.refs_17_
  91.2 0.4 collective-permute-done.26.refs_13_
  92.0 10.2 %update.1 = (bf16[112,2048]{1,0:T(8,128)(2,1)S(1)}, bf16[112,2048]{1,0:T(8,128)(2,1)S(1)}, bf16[112,2048]{1,0:T(8,128)(2,1)S(1)}, bf16[112,2048]{1,0:T(8,128)(2,1)S(1)}) custom-call(bf16[112,2048]{1,0:T(8,128)(2,1)S(1)} %get-tuple-element.23.refs_0_, bf16[112,2048]{1,0:T(8,128)(2,1)S(1)} %collective-permute-done.refs_0_.refs_1_, ...), custom_call_target="tpu_custom_call" | custom-call | tf_op jit(solution)/shard_map/update/pallas_call | solution.py:317
  102.3 1.3 %collective-permute-start.32 = (bf16[112,2048]{1,0:T(8,128)(2,1)S(1)}, bf16[112,2048]{1,0:T(8,128)(2,1)S(1)}, u32[]{:S(2)}, u32[]{:S(2)}) collective-permute-start(bf16[112,2048]{1,0:T(8,128)(2,1)S(1)} %get-tuple-element.35), channel_id=1, source_target_pairs={{32,0},{9,1},{34,2},{11,3},{36,4},{13,5},{38,6},{15,7},{40,8},{17,... | collective-permute-start | bytes 1376264 | tf_op jit(solution)/shard_map/ppermute | solution.py:65
  103.6 2.1 %collective-permute-start.31 = (bf16[112,2048]{1,0:T(8,128)(2,1)S(1)}, bf16[112,2048]{1,0:T(8,128)(2,1)S(1)}, u32[]{:S(2)}, u32[]{:S(2)}) collective-permute-start(bf16[112,2048]{1,0:T(8,128)(2,1)S(1)} %get-tuple-element.34), channel_id=1, source_target_pairs={{96,0},{25,1},{98,2},{27,3},{100,4},{29,5},{102,6},{31,7},{104,8},... | collective-permute-start | bytes 1376264 | tf_op jit(solution)/shard_map/ppermute | solution.py:65
  105.8 1.3 %apply.4 = (bf16[4,112,2048]{2,1,0:T(8,128)(2,1)}, f32[4,112,2048]{2,1,0:T(8,128)}) custom-call(bf16[112,2048]{1,0:T(8,128)(2,1)S(1)} %get-tuple-element.37.value, f32[4,112,2048]{2,1,0:T(8,128)S(1)} %copy-done), custom_call_target="tpu_custom_call" | custom-call | flops 688128 | bytes 2752512 | tf_op jit(solution)/shard_map/apply/pallas_call | solution.py:364
  107.1 9.3 %collective-permute-done.33.value = bf16[112,2048]{1,0:T(8,128)(2,1)S(1)} collective-permute-done((bf16[112,2048]{1,0:T(8,128)(2,1)S(1)}, bf16[112,2048]{1,0:T(8,128)(2,1)S(1)}, u32[]{:S(2)}, u32[]{:S(2)}) %collective-permute-start.33) | collective-permute-done | bytes 458784 | tf_op jit(solution)/shard_map/ppermute | solution.py:65
  116.4 1.3 %apply.5 = (bf16[4,112,2048]{2,1,0:T(8,128)(2,1)}, f32[4,112,2048]{2,1,0:T(8,128)}) custom-call(bf16[112,2048]{1,0:T(8,128)(2,1)S(1)} %collective-permute-done.33.value, f32[4,112,2048]{2,1,0:T(8,128)S(1)} %copy-done, bf16[4,112,2048]{2,1,0:T(8,128)(2,1)} %get-tuple-element.38.refs_0_, ...), custom_call_target="tpu_custom_call", output_to_operand_aliasing={{0}: (2, {}), {1}: (3, {})} | custom-call | flops 688128 | bytes 2752512 | tf_op jit(solution)/shard_map/apply/pallas_call | solution.py:364
  117.7 1.3 %apply.6 = (bf16[4,112,2048]{2,1,0:T(8,128)(2,1)}, f32[4,112,2048]{2,1,0:T(8,128)}) custom-call(bf16[112,2048]{1,0:T(8,128)(2,1)S(1)} %collective-permute-done.32.value, f32[4,112,2048]{2,1,0:T(8,128)S(1)} %copy-done, bf16[4,112,2048]{2,1,0:T(8,128)(2,1)} %get-tuple-element.40.refs_0_, ...), custom_call_target="tpu_custom_call", output_to_operand_aliasing={{0}: (2, {}), {1}: (3, {})} | custom-call | flops 688128 | bytes 2752512 | tf_op jit(solution)/shard_map/apply/pallas_call | solution.py:364
  119.0 1.3 %apply.7 = (bf16[4,112,2048]{2,1,0:T(8,128)(2,1)}, f32[4,112,2048]{2,1,0:T(8,128)}) custom-call(bf16[112,2048]{1,0:T(8,128)(2,1)S(1)} %collective-permute-done.31.value, f32[4,112,2048]{2,1,0:T(8,128)S(1)} %copy-done, bf16[4,112,2048]{2,1,0:T(8,128)(2,1)} %get-tuple-element.42.refs_0_, ...), custom_call_target="tpu_custom_call", output_to_operand_aliasing={{0}: (2, {}), {1}: (3, {})} | custom-call | flops 688128 | bytes 2752512 | tf_op jit(solution)/shard_map/apply/pallas_call | solution.py:364
  (42 shorter events, 1.9 us)
Async XLA Ops:
  0.6 1.5 %copy-start.1 = (bf16[4,112,2048]{2,1,0:T(8,128)(2,1)S(1)}, bf16[4,112,2048]{2,1,0:T(8,128)(2,1)}, u32[]{:S(2)}) copy-start(bf16[4,112,2048]{2,1,0:T(8,128)(2,1)} %momentum.3) | copy-start | bytes 5505028
  2.1 0.7 copy-start.2
  4.3 10.5 %collective-permute-start.1 = (bf16[112,2048]{1,0:T(8,128)(2,1)S(1)}, bf16[112,2048]{1,0:T(8,128)(2,1)S(1)}, u32[]{:S(2)}, u32[]{:S(2)}) collective-permute-start(bf16[112,2048]{1,0:T(8,128)(2,1)S(1)} %get-tuple-element.24), channel_id=1, source_target_pairs={{0,32},{1,9},{2,34},{3,11},{4,36},{5,13},{6,38},{7,15},{8,40},{9,1... | collective-permute-start | bytes 1376264 | tf_op jit(solution)/shard_map/ppermute | solution.py:65
  6.0 9.4 %collective-permute-start.2 = (bf16[112,2048]{1,0:T(8,128)(2,1)S(1)}, bf16[112,2048]{1,0:T(8,128)(2,1)S(1)}, u32[]{:S(2)}, u32[]{:S(2)}) collective-permute-start(bf16[112,2048]{1,0:T(8,128)(2,1)S(1)} %get-tuple-element.25), channel_id=1, source_target_pairs={{0,96},{1,25},{2,98},{3,27},{4,100},{5,29},{6,102},{7,31},{8,104},... | collective-permute-start | bytes 1376264 | tf_op jit(solution)/shard_map/ppermute | solution.py:65
  10.3 10.3 %collective-permute-start = (bf16[112,2048]{1,0:T(8,128)(2,1)}, bf16[112,2048]{1,0:T(8,128)(2,1)S(1)}, u32[]{:S(2)}, u32[]{:S(2)}) collective-permute-start(bf16[112,2048]{1,0:T(8,128)(2,1)} %live.3), channel_id=1, source_target_pairs={{0,16},{1,65},{2,18},{3,67},{4,20},{5,69},{6,22},{7,71},{8,24},{9,... | collective-permute-start | bytes 1376264 | tf_op jit(solution)/shard_map/ppermute | solution.py:65
  13.7 9.8 %collective-permute-start.3 = (bf16[112,2048]{1,0:T(8,128)(2,1)S(1)}, bf16[112,2048]{1,0:T(8,128)(2,1)S(1)}, u32[]{:S(2)}, u32[]{:S(2)}) collective-permute-start(bf16[112,2048]{1,0:T(8,128)(2,1)S(1)} %get-tuple-element.23.refs_0_), channel_id=1, source_target_pairs={{0,1},{1,0},{2,3},{3,2},{4,5},{5,4},{6,7},{7,6},{8,9},{9,8},{10,11... | collective-permute-start | bytes 1376264 | tf_op jit(solution)/shard_map/ppermute | solution.py:65
  14.8 8.7 %collective-permute-start.5 = (bf16[112,2048]{1,0:T(8,128)(2,1)S(1)}, bf16[112,2048]{1,0:T(8,128)(2,1)S(1)}, u32[]{:S(2)}, u32[]{:S(2)}) collective-permute-start(bf16[112,2048]{1,0:T(8,128)(2,1)S(1)} %collective-permute-done.1.refs_1_.refs_2_), channel_id=1, source_target_pairs={{0,1},{1,0},{2,3},{3,2},{4,5},{5,4},{6,7},{7,6},{8,9},{9,8},{10,11... | collective-permute-start | bytes 1376264 | tf_op jit(solution)/shard_map/ppermute | solution.py:65
  15.4 8.1 %collective-permute-start.6 = (bf16[112,2048]{1,0:T(8,128)(2,1)S(1)}, bf16[112,2048]{1,0:T(8,128)(2,1)S(1)}, u32[]{:S(2)}, u32[]{:S(2)}) collective-permute-start(bf16[112,2048]{1,0:T(8,128)(2,1)S(1)} %collective-permute-done.2.refs_2_.refs_3_), channel_id=1, source_target_pairs={{0,1},{1,0},{2,3},{3,2},{4,5},{5,4},{6,7},{7,6},{8,9},{9,8},{10,11... | collective-permute-start | bytes 1376264 | tf_op jit(solution)/shard_map/ppermute | solution.py:65
  20.6 3.0 %collective-permute-start.4 = (bf16[112,2048]{1,0:T(8,128)(2,1)S(1)}, bf16[112,2048]{1,0:T(8,128)(2,1)S(1)}, u32[]{:S(2)}, u32[]{:S(2)}) collective-permute-start(bf16[112,2048]{1,0:T(8,128)(2,1)S(1)} %collective-permute-done.refs_0_.refs_1_), channel_id=1, source_target_pairs={{0,1},{1,0},{2,3},{3,2},{4,5},{5,4},{6,7},{7,6},{8,9},{9,8},{10,11... | collective-permute-start | bytes 1376264 | tf_op jit(solution)/shard_map/ppermute | solution.py:65
  26.6 13.4 %collective-permute-start.16 = (bf16[544,256]{1,0:T(8,128)(2,1)S(1)}, bf16[544,256]{1,0:T(8,128)(2,1)S(1)}, u32[]{:S(2)}, u32[]{:S(2)}) collective-permute-start(bf16[544,256]{1,0:T(8,128)(2,1)S(1)} %get-tuple-element.31), channel_id=1, source_target_pairs={{0,4},{1,5},{2,6},{3,7},{4,0},{5,1},{6,2},{7,3},{8,12},{9,13},{10,... | collective-permute-start | bytes 835592 | tf_op jit(solution)/shard_map/ppermute | solution.py:65
  30.7 13.3 %collective-permute-start.17 = (bf16[544,256]{1,0:T(8,128)(2,1)S(1)}, bf16[544,256]{1,0:T(8,128)(2,1)S(1)}, u32[]{:S(2)}, u32[]{:S(2)}) collective-permute-start(bf16[544,256]{1,0:T(8,128)(2,1)S(1)} %get-tuple-element.32), channel_id=1, source_target_pairs={{0,2},{1,3},{2,4},{3,5},{4,6},{5,7},{6,0},{7,1},{8,10},{9,11},{10,... | collective-permute-start | bytes 835592 | tf_op jit(solution)/shard_map/ppermute | solution.py:65
  31.7 13.1 %collective-permute-start.18 = (bf16[544,256]{1,0:T(8,128)(2,1)S(1)}, bf16[544,256]{1,0:T(8,128)(2,1)S(1)}, u32[]{:S(2)}, u32[]{:S(2)}) collective-permute-start(bf16[544,256]{1,0:T(8,128)(2,1)S(1)} %get-tuple-element.33), channel_id=1, source_target_pairs={{0,6},{1,7},{2,0},{3,1},{4,2},{5,3},{6,4},{7,5},{8,14},{9,15},{10,... | collective-permute-start | bytes 835592 | tf_op jit(solution)/shard_map/ppermute | solution.py:65
  33.9 16.7 %collective-permute-start.7 = (bf16[544,256]{1,0:T(8,128)(2,1)S(1)}, bf16[544,256]{1,0:T(8,128)(2,1)S(1)}, u32[]{:S(2)}, u32[]{:S(2)}) collective-permute-start(bf16[544,256]{1,0:T(8,128)(2,1)S(1)} %get-tuple-element.27), channel_id=1, source_target_pairs={{0,80},{1,81},{2,82},{3,83},{4,84},{5,85},{6,86},{7,87},{8,88},{9,... | collective-permute-start | bytes 835592 | tf_op jit(solution)/shard_map/ppermute | solution.py:65
  38.4 15.2 %collective-permute-start.8 = (bf16[544,256]{1,0:T(8,128)(2,1)S(1)}, bf16[544,256]{1,0:T(8,128)(2,1)S(1)}, u32[]{:S(2)}, u32[]{:S(2)}) collective-permute-start(bf16[544,256]{1,0:T(8,128)(2,1)S(1)} %get-tuple-element.28), channel_id=1, source_target_pairs={{0,56},{1,57},{2,58},{3,59},{4,60},{5,61},{6,62},{7,63},{8,32},{9,... | collective-permute-start | bytes 835592 | tf_op jit(solution)/shard_map/ppermute | solution.py:65
  40.1 13.5 %collective-permute-start.9 = (bf16[544,256]{1,0:T(8,128)(2,1)S(1)}, bf16[544,256]{1,0:T(8,128)(2,1)S(1)}, u32[]{:S(2)}, u32[]{:S(2)}) collective-permute-start(bf16[544,256]{1,0:T(8,128)(2,1)S(1)} %get-tuple-element.29), channel_id=1, source_target_pairs={{0,104},{1,105},{2,106},{3,107},{4,108},{5,109},{6,110},{7,111},{8... | collective-permute-start | bytes 835592 | tf_op jit(solution)/shard_map/ppermute | solution.py:65
  44.9 18.9 %collective-permute-start.19 = (bf16[544,256]{1,0:T(8,128)(2,1)S(1)}, bf16[544,256]{1,0:T(8,128)(2,1)S(1)}, u32[]{:S(2)}, u32[]{:S(2)}) collective-permute-start(bf16[544,256]{1,0:T(8,128)(2,1)S(1)} %add_convert_fusion.1), channel_id=1, source_target_pairs={{0,80},{1,81},{2,82},{3,83},{4,84},{5,85},{6,86},{7,87},{8,88},{9,... | collective-permute-start | bytes 835592 | tf_op jit(solution)/shard_map/ppermute | solution.py:65
  49.4 15.3 %collective-permute-start.20 = (bf16[544,256]{1,0:T(8,128)(2,1)S(1)}, bf16[544,256]{1,0:T(8,128)(2,1)S(1)}, u32[]{:S(2)}, u32[]{:S(2)}) collective-permute-start(bf16[544,256]{1,0:T(8,128)(2,1)S(1)} %add_convert_fusion.1), channel_id=1, source_target_pairs={{0,56},{1,57},{2,58},{3,59},{4,60},{5,61},{6,62},{7,63},{8,32},{9,... | collective-permute-start | bytes 835592 | tf_op jit(solution)/shard_map/ppermute | solution.py:65
  50.6 16.1 %collective-permute-start.21 = (bf16[544,256]{1,0:T(8,128)(2,1)S(1)}, bf16[544,256]{1,0:T(8,128)(2,1)S(1)}, u32[]{:S(2)}, u32[]{:S(2)}) collective-permute-start(bf16[544,256]{1,0:T(8,128)(2,1)S(1)} %add_convert_fusion.1), channel_id=1, source_target_pairs={{0,104},{1,105},{2,106},{3,107},{4,108},{5,109},{6,110},{7,111},{8... | collective-permute-start | bytes 835592 | tf_op jit(solution)/shard_map/ppermute | solution.py:65
  53.7 13.5 %collective-permute-start.10 = (bf16[544,256]{1,0:T(8,128)(2,1)S(1)}, bf16[544,256]{1,0:T(8,128)(2,1)S(1)}, u32[]{:S(2)}, u32[]{:S(2)}) collective-permute-start(bf16[544,256]{1,0:T(8,128)(2,1)S(1)} %add_convert_fusion.3), channel_id=1, source_target_pairs={{0,4},{1,5},{2,6},{3,7},{4,0},{5,1},{6,2},{7,3},{8,12},{9,13},{10,... | collective-permute-start | bytes 835592 | tf_op jit(solution)/shard_map/ppermute | solution.py:65
  55.8 13.0 %collective-permute-start.11 = (bf16[544,256]{1,0:T(8,128)(2,1)S(1)}, bf16[544,256]{1,0:T(8,128)(2,1)S(1)}, u32[]{:S(2)}, u32[]{:S(2)}) collective-permute-start(bf16[544,256]{1,0:T(8,128)(2,1)S(1)} %add_convert_fusion.3), channel_id=1, source_target_pairs={{0,2},{1,3},{2,4},{3,5},{4,6},{5,7},{6,0},{7,1},{8,10},{9,11},{10,... | collective-permute-start | bytes 835592 | tf_op jit(solution)/shard_map/ppermute | solution.py:65
  63.8 8.7 %collective-permute-start.12 = (bf16[544,256]{1,0:T(8,128)(2,1)S(1)}, bf16[544,256]{1,0:T(8,128)(2,1)S(1)}, u32[]{:S(2)}, u32[]{:S(2)}) collective-permute-start(bf16[544,256]{1,0:T(8,128)(2,1)S(1)} %add_convert_fusion.3), channel_id=1, source_target_pairs={{0,6},{1,7},{2,0},{3,1},{4,2},{5,3},{6,4},{7,5},{8,14},{9,15},{10,... | collective-permute-start | bytes 835592 | tf_op jit(solution)/shard_map/ppermute | solution.py:65
  66.9 14.1 %collective-permute-start.23 = (bf16[544,256]{1,0:T(8,128)(2,1)S(1)}, bf16[544,256]{1,0:T(8,128)(2,1)S(1)}, u32[]{:S(2)}, u32[]{:S(2)}) collective-permute-start(bf16[544,256]{1,0:T(8,128)(2,1)S(1)} %add_convert_fusion.refs_8_), channel_id=1, source_target_pairs={{0,4},{1,5},{2,6},{3,7},{4,0},{5,1},{6,2},{7,3},{8,12},{9,13},{10,... | collective-permute-start | bytes 835592 | tf_op jit(solution)/shard_map/ppermute | solution.py:65
  72.6 13.2 %collective-permute-start.14 = (bf16[544,256]{1,0:T(8,128)(2,1)S(1)}, bf16[544,256]{1,0:T(8,128)(2,1)S(1)}, u32[]{:S(2)}, u32[]{:S(2)}) collective-permute-start(bf16[544,256]{1,0:T(8,128)(2,1)S(1)} %add_convert_fusion.2.refs_4_), channel_id=1, source_target_pairs={{0,80},{1,81},{2,82},{3,83},{4,84},{5,85},{6,86},{7,87},{8,88},{9,... | collective-permute-start | bytes 835592 | tf_op jit(solution)/shard_map/ppermute | solution.py:65
  77.0 8.8 %collective-permute-start.24 = (bf16[544,256]{1,0:T(8,128)(2,1)S(1)}, bf16[544,256]{1,0:T(8,128)(2,1)S(1)}, u32[]{:S(2)}, u32[]{:S(2)}) collective-permute-start(bf16[544,256]{1,0:T(8,128)(2,1)S(1)} %add_convert_fusion.refs_8_), channel_id=1, source_target_pairs={{0,6},{1,7},{2,0},{3,1},{4,2},{5,3},{6,4},{7,5},{8,14},{9,15},{10,... | collective-permute-start | bytes 835592 | tf_op jit(solution)/shard_map/ppermute | solution.py:65
  80.9 7.8 %collective-permute-start.22 = (bf16[544,256]{1,0:T(8,128)(2,1)S(1)}, bf16[544,256]{1,0:T(8,128)(2,1)S(1)}, u32[]{:S(2)}, u32[]{:S(2)}) collective-permute-start(bf16[544,256]{1,0:T(8,128)(2,1)S(1)} %add_convert_fusion.refs_8_), channel_id=1, source_target_pairs={{0,2},{1,3},{2,4},{3,5},{4,6},{5,7},{6,0},{7,1},{8,10},{9,11},{10,... | collective-permute-start | bytes 835592 | tf_op jit(solution)/shard_map/ppermute | solution.py:65
  80.9 8.7 %collective-permute-start.15 = (bf16[544,256]{1,0:T(8,128)(2,1)S(1)}, bf16[544,256]{1,0:T(8,128)(2,1)S(1)}, u32[]{:S(2)}, u32[]{:S(2)}) collective-permute-start(bf16[544,256]{1,0:T(8,128)(2,1)S(1)} %add_convert_fusion.2.refs_4_), channel_id=1, source_target_pairs={{0,104},{1,105},{2,106},{3,107},{4,108},{5,109},{6,110},{7,111},{8... | collective-permute-start | bytes 835592 | tf_op jit(solution)/shard_map/ppermute | solution.py:65
  80.9 8.7 %collective-permute-start.13 = (bf16[544,256]{1,0:T(8,128)(2,1)S(1)}, bf16[544,256]{1,0:T(8,128)(2,1)S(1)}, u32[]{:S(2)}, u32[]{:S(2)}) collective-permute-start(bf16[544,256]{1,0:T(8,128)(2,1)S(1)} %add_convert_fusion.2.refs_4_), channel_id=1, source_target_pairs={{0,56},{1,57},{2,58},{3,59},{4,60},{5,61},{6,62},{7,63},{8,32},{9,... | collective-permute-start | bytes 835592 | tf_op jit(solution)/shard_map/ppermute | solution.py:65
  85.8 6.1 %collective-permute-start.28 = (bf16[1088,256]{1,0:T(8,128)(2,1)S(1)}, bf16[1088,256]{1,0:T(8,128)(2,1)S(1)}, u32[]{:S(2)}, u32[]{:S(2)}) collective-permute-start(bf16[1088,256]{1,0:T(8,128)(2,1)S(1)} %pad_maximum_fusion.1), channel_id=1, source_target_pairs={{0,1},{1,0},{2,3},{3,2},{4,5},{5,4},{6,7},{7,6},{8,9},{9,8},{10,11... | collective-permute-start | bytes 1671176 | tf_op jit(solution)/shard_map/ppermute | solution.py:65
  85.9 4.3 %collective-permute-start.29 = (bf16[544,256]{1,0:T(8,128)(2,1)S(1)}, bf16[544,256]{1,0:T(8,128)(2,1)S(1)}, u32[]{:S(2)}, u32[]{:S(2)}) collective-permute-start(bf16[544,256]{1,0:T(8,128)(2,1)S(1)} %collective-permute-done.24.refs_11_), channel_id=1, source_target_pairs={{0,1},{1,0},{2,3},{3,2},{4,5},{5,4},{6,7},{7,6},{8,9},{9,8},{10,11... | collective-permute-start | bytes 835592 | tf_op jit(solution)/shard_map/ppermute | solution.py:65
  86.4 19.4 %copy-start = (f32[4,112,2048]{2,1,0:T(8,128)S(1)}, f32[4,112,2048]{2,1,0:T(8,128)}, u32[]{:S(2)}) copy-start(f32[4,112,2048]{2,1,0:T(8,128)} %weight.7) | copy-start | bytes 11010052
  88.7 3.3 %collective-permute-start.25 = (bf16[1088,256]{1,0:T(8,128)(2,1)S(1)}, bf16[1088,256]{1,0:T(8,128)(2,1)S(1)}, u32[]{:S(2)}, u32[]{:S(2)}) collective-permute-start(bf16[1088,256]{1,0:T(8,128)(2,1)S(1)} %pad_maximum_fusion), channel_id=1, source_target_pairs={{0,1},{1,0},{2,3},{3,2},{4,5},{5,4},{6,7},{7,6},{8,9},{9,8},{10,11... | collective-permute-start | bytes 1671176 | tf_op jit(solution)/shard_map/ppermute | solution.py:65
  89.6 1.6 %collective-permute-start.30 = (bf16[544,256]{1,0:T(8,128)(2,1)S(1)}, bf16[544,256]{1,0:T(8,128)(2,1)S(1)}, u32[]{:S(2)}, u32[]{:S(2)}) collective-permute-start(bf16[544,256]{1,0:T(8,128)(2,1)S(1)} %collective-permute-done.22.refs_9_), channel_id=1, source_target_pairs={{0,1},{1,0},{2,3},{3,2},{4,5},{5,4},{6,7},{7,6},{8,9},{9,8},{10,11... | collective-permute-start | bytes 835592 | tf_op jit(solution)/shard_map/ppermute | solution.py:65
  89.7 1.9 %collective-permute-start.26 = (bf16[544,256]{1,0:T(8,128)(2,1)S(1)}, bf16[544,256]{1,0:T(8,128)(2,1)S(1)}, u32[]{:S(2)}, u32[]{:S(2)}) collective-permute-start(bf16[544,256]{1,0:T(8,128)(2,1)S(1)} %collective-permute-done.15.refs_7_), channel_id=1, source_target_pairs={{0,1},{1,0},{2,3},{3,2},{4,5},{5,4},{6,7},{7,6},{8,9},{9,8},{10,11... | collective-permute-start | bytes 835592 | tf_op jit(solution)/shard_map/ppermute | solution.py:65
  90.1 1.8 %collective-permute-start.27 = (bf16[544,256]{1,0:T(8,128)(2,1)S(1)}, bf16[544,256]{1,0:T(8,128)(2,1)S(1)}, u32[]{:S(2)}, u32[]{:S(2)}) collective-permute-start(bf16[544,256]{1,0:T(8,128)(2,1)S(1)} %collective-permute-done.13.refs_5_), channel_id=1, source_target_pairs={{0,1},{1,0},{2,3},{3,2},{4,5},{5,4},{6,7},{7,6},{8,9},{9,8},{10,11... | collective-permute-start | bytes 835592 | tf_op jit(solution)/shard_map/ppermute | solution.py:65
  102.2 14.2 %collective-permute-start.33 = (bf16[112,2048]{1,0:T(8,128)(2,1)S(1)}, bf16[112,2048]{1,0:T(8,128)(2,1)S(1)}, u32[]{:S(2)}, u32[]{:S(2)}) collective-permute-start(bf16[112,2048]{1,0:T(8,128)(2,1)S(1)} %get-tuple-element.36), channel_id=1, source_target_pairs={{16,0},{65,1},{18,2},{67,3},{20,4},{69,5},{22,6},{71,7},{24,8},{73... | collective-permute-start | bytes 1376264 | tf_op jit(solution)/shard_map/ppermute | solution.py:65
  102.3 15.4 %collective-permute-start.32 = (bf16[112,2048]{1,0:T(8,128)(2,1)S(1)}, bf16[112,2048]{1,0:T(8,128)(2,1)S(1)}, u32[]{:S(2)}, u32[]{:S(2)}) collective-permute-start(bf16[112,2048]{1,0:T(8,128)(2,1)S(1)} %get-tuple-element.35), channel_id=1, source_target_pairs={{32,0},{9,1},{34,2},{11,3},{36,4},{13,5},{38,6},{15,7},{40,8},{17,... | collective-permute-start | bytes 1376264 | tf_op jit(solution)/shard_map/ppermute | solution.py:65
  103.6 15.4 %collective-permute-start.31 = (bf16[112,2048]{1,0:T(8,128)(2,1)S(1)}, bf16[112,2048]{1,0:T(8,128)(2,1)S(1)}, u32[]{:S(2)}, u32[]{:S(2)}) collective-permute-start(bf16[112,2048]{1,0:T(8,128)(2,1)S(1)} %get-tuple-element.34), channel_id=1, source_target_pairs={{96,0},{25,1},{98,2},{27,3},{100,4},{29,5},{102,6},{31,7},{104,8},... | collective-permute-start | bytes 1376264 | tf_op jit(solution)/shard_map/ppermute | solution.py:65
